TPU v7x, 512 devices: a whole 4x4x16 slice. The times are simulated.
512 devices in a mesh: rows: 64 (over y, z), cols: 8 (over x, core).
Axes of the slice: x: 4, y: 4, z: 16, core: 2. Of those that a mesh axis runs over, the one named last changes fastest.
Arguments:
- descriptors: bfloat16 [16384, 1024], P(('rows', 'cols')), may hold values from -6 to 6
- sparse_points: bfloat16 [8192, 1024], P('cols'), may hold values from -6 to 6
- point_scale: float32 [8192], P('cols'), may hold values from 0.3 to 3
- env_owner: int32 [16384, 1], P('rows'), may hold values from 0 to 63; in each aligned block of 128 rows (0 to 127, 128 to 255, ...) at most 3 rows name the same one
- env_structure: int32 [16384], P('rows'), may hold values from 0 to 63
- row_weight: float32 [4096], P('rows'), may hold values from 0.01 to 0.1
- ridge_factor: float32 [1], replicated, may hold values from 0.05 to 0.5
Outputs:
- r_rows: float32 [128, 8192], P(None, 'cols')
- reduced: float32 [4096, 8192], P('rows', 'cols')
Inputs may be any that keep to these rules, and one draw needn't show every extreme that they name: `env_owner`: in each aligned block of 128 environments, no owner is named by more than 3 of them.
All inputs are finite; a program needn't handle non-finite values.
Results may differ from a plain program's by a relative error of at most 0.0045.
Values may be sent and summed in bfloat16 or wider, within the bound.
No kernel may reach another device: no remote copies, remote signals or barrier semaphores. Data moves between devices by JAX's collectives and lax.ppermute only.
A program may use at most 64 MiB of HBM per device.

v0:
```python
import math

import jax
import jax.numpy as jnp
from jax import lax
from jax.sharding import PartitionSpec as P

PW = 64
PANELS = 2


def copy_for_each(array, axis):
    copies = jnp.broadcast_to(array, (lax.axis_size(axis), *array.shape))
    return lax.all_to_all(copies, axis, split_axis=0, concat_axis=0, tiled=True)


def joined_along(pieces, dim):
    pieces = jnp.moveaxis(pieces, 0, dim)
    dims = pieces.shape
    return pieces.reshape(*dims[:dim], dims[dim] * dims[dim + 1], *dims[dim + 2 :])


def gathered_copies(array, axis, dim):
    pieces = copy_for_each(array, axis)
    return joined_along(pieces, dim)


def picked(array, axis, root):
    return lax.dynamic_index_in_dim(lax.all_gather(array, axis), root, 0, keepdims=False)


def split_up(array, dim, length):
    before, after = (array.shape[:dim], array.shape[dim + 1 :])
    return jnp.moveaxis(array.reshape(*before, length, -1, *after), dim, 0)


def summed_on_arrival(array, axis, dim):
    pieces = split_up(array, dim, lax.axis_size(axis))
    arrived = lax.all_to_all(pieces, axis, split_axis=0, concat_axis=0, tiled=True)
    return arrived.sum(axis=0)


def filled_up(lines, length):
    spare = -len(lines) % length
    return jnp.pad(lines, [(0, spare)] + [(0, 0)] * (lines.ndim - 1))


def nested_sum(array, axes):
    own = summed_on_arrival(filled_up(array, lax.axis_size(axes)), axes, 0)
    whole = gathered_copies(own, axes, 0)
    return whole[: len(array)].reshape(array.shape)


def in_one(arrays, axis):
    ravelled, at, finished = (jnp.concatenate([a.reshape(-1) for a in arrays]), 0, [])
    total = nested_sum(ravelled, axis)
    for a in arrays:
        finished.append(total[at : at + a.size].reshape(a.shape))
        at += a.size
    return tuple(finished)


def kernel_rows(env_rows, sparse_points, point_scale):
    dot_scale = env_rows.shape[1] ** (-0.5)
    products = (
        lax.dot_general(
            env_rows, sparse_points, (((1,), (1,)), ((), ())), preferred_element_type=jnp.float32
        )
        * dot_scale
    )
    squared = products * products
    return (point_scale[None, :] * squared * squared).astype(jnp.bfloat16)


def pack_slots(kernel, owner_ids, struct_ids, capacity, owner_count):
    row_count = kernel.shape[0]
    labels = lax.broadcasted_iota(jnp.int32, (row_count, owner_count), 1)
    matches = (owner_ids[:, None] == labels).astype(jnp.int32)
    before = jnp.cumsum(matches, axis=0) - matches
    within = jnp.sum(before * matches, axis=1)
    slot_idx = owner_ids * capacity + within
    slot_total = owner_count * capacity
    packed = jnp.zeros((slot_total, kernel.shape[1]), kernel.dtype).at[slot_idx].set(kernel)
    slot_labels = jnp.full((slot_total,), -1, jnp.int32).at[slot_idx].set(struct_ids)
    return (packed, slot_labels)


def fold_structures(received, labels_in, eq_count):
    targets = lax.broadcasted_iota(jnp.int32, (eq_count, labels_in.shape[0]), 0)
    selector = (labels_in[None, :] == targets).astype(jnp.bfloat16)
    return jnp.dot(selector, received, preferred_element_type=jnp.float32)


def inner_cols(left, right):
    return lax.dot_general(
        left,
        right,
        (((0,), (0,)), ((), ())),
        precision=lax.Precision.HIGHEST,
        preferred_element_type=jnp.float32,
    )


def factor(gram_mat, ridge_factor):
    shift = ridge_factor[0] * jnp.trace(gram_mat) / PW + 1e-06
    chol_lower = jnp.linalg.cholesky(gram_mat + shift * jnp.eye(PW, dtype=jnp.float32))
    inverse = jax.scipy.linalg.solve_triangular(
        chol_lower, jnp.eye(PW, dtype=jnp.float32), lower=True
    )
    return (chol_lower, inverse)


def body(
    descriptors, sparse_points, point_scale, env_owner, env_structure, row_weight, ridge_factor
):
    owner_count = lax.axis_size("rows")
    eq_count = row_weight.shape[0]
    owner_ids = env_owner[:, 0]
    env_count = owner_ids.shape[0]
    half_count = env_count // 2
    capacity = max(2, (3 * half_count + 2 * owner_count - 1) // (2 * owner_count))
    kernel_all = kernel_rows(gathered_copies(descriptors, "cols", 0), sparse_points, point_scale)
    packed, slot_labels = pack_slots(
        kernel_all, owner_ids, env_structure, 2 * capacity, owner_count
    )
    received, labels_in = (
        lax.all_to_all(packed, "rows", split_axis=0, concat_axis=0, tiled=True),
        lax.all_to_all(slot_labels, "rows", split_axis=0, concat_axis=0, tiled=True),
    )
    sums = fold_structures(received, labels_in, eq_count)
    matrix = sums * row_weight[:, None]
    col_count = matrix.shape[1]
    col_ids = lax.axis_index("cols") * col_count + lax.broadcasted_iota(
        jnp.int32, (1, col_count), 1
    )
    norm_scale = 1.0 / math.sqrt(owner_count * eq_count)
    r_blocks = []
    for panel_idx in range(PANELS):
        first_col = panel_idx * PW
        local_cols = lax.slice_in_dim(matrix, first_col, first_col + PW, axis=1)
        panel_cols = picked(local_cols, "cols", 0)
        gram_mat, cross_terms = in_one(
            (inner_cols(panel_cols, panel_cols), inner_cols(panel_cols, matrix)), "rows"
        )
        chol_lower, inverse = factor(gram_mat, ridge_factor)
        q_cols = jnp.dot(
            panel_cols,
            inverse.T,
            precision=lax.Precision.HIGHEST,
            preferred_element_type=jnp.float32,
        )
        coupled = jnp.dot(
            inverse,
            cross_terms,
            precision=lax.Precision.HIGHEST,
            preferred_element_type=jnp.float32,
        )
        later_mask = col_ids >= first_col + PW
        inside = (col_ids >= first_col) & (col_ids < first_col + PW)
        coupled = jnp.where(later_mask, coupled, 0.0)
        update = jnp.dot(
            q_cols, coupled, precision=lax.Precision.HIGHEST, preferred_element_type=jnp.float32
        )
        q_wide = jnp.pad(q_cols, ((0, 0), (first_col, col_count - first_col - PW)))
        matrix = jnp.where(inside, q_wide, matrix - update)
        r_wide = jnp.pad(chol_lower.T, ((0, 0), (first_col, col_count - first_col - PW)))
        r_blocks.append(jnp.where(inside, r_wide, coupled) * norm_scale)
    return (jnp.concatenate(r_blocks, axis=0), matrix)


def solution(mesh):
    return jax.shard_map(
        body,
        mesh=mesh,
        in_specs=(
            P(("rows", "cols"), None),
            P("cols", None),
            P("cols"),
            P("rows", None),
            P("rows"),
            P("rows"),
            P(),
        ),
        out_specs=(P(None, "cols"), P("rows", "cols")),
        check_vma=False,
    )
```

profile of v0, /device:TPU:8, one launch (start us, length us, event | category | flops | bytes accessed | tf_op | source)
XLA Modules:
  0.0 305.2 jit_solution(422997033180291629)
XLA Ops:
  2.5 4.3 %all-to-all-start.1 = ((bf16[8,32,1024]{2,1,0:T(8,128)(2,1)}), bf16[8,32,1024]{2,1,0:T(8,128)(2,1)S(1)}, u32[]{:S(2)}, u32[]{:S(2)}) async-start(bf16[8,32,1024]{2,1,0:T(8,128)(2,1)} %broadcast_in_dim.66), calls=%async_computation.1 | async-start | bytes 1048576 | tf_op jit(solution)/shard_map/all_to_all | solution.py:14
  12.1 5.0 %all-to-all-done.1 = bf16[8,32,1024]{2,1,0:T(8,128)(2,1)S(1)} async-done(((bf16[8,32,1024]{2,1,0:T(8,128)(2,1)}), bf16[8,32,1024]{2,1,0:T(8,128)(2,1)S(1)}, u32[]{:S(2)}, u32[]{:S(2)}) %all-to-all-start.1) | async-done | bytes 524320 | tf_op jit(solution)/shard_map/all_to_all | solution.py:14
  17.1 18.7 %all-to-all-start = ((s32[64,6,1]{1,2,0:T(1,128)}), s32[64,6,1]{1,2,0:T(1,128)S(1)}, u32[]{:S(2)}, u32[]{:S(2)}) async-start(s32[64,6,1]{1,2,0:T(1,128)} %bitcast.5), calls=%async_computation | async-start | bytes 65536 | tf_op jit(solution)/shard_map/all_to_all | solution.py:128
  35.9 2.3 fusion.1
  38.2 2.4 scatter_custom_fusion.1
  41.8 7.5 %all-to-all-done = s32[64,6,1]{1,2,0:T(1,128)S(1)} async-done(((s32[64,6,1]{1,2,0:T(1,128)}), s32[64,6,1]{1,2,0:T(1,128)S(1)}, u32[]{:S(2)}, u32[]{:S(2)}) %all-to-all-start) | async-done | bytes 1568 | tf_op jit(solution)/shard_map/all_to_all | solution.py:128
  49.3 7.8 %all-to-all-start.2 = ((bf16[64,6,1024]{2,1,0:T(8,128)(2,1)}), bf16[64,6,1024]{2,1,0:T(8,128)(2,1)S(1)}, u32[]{:S(2)}, u32[]{:S(2)}) async-start(bf16[64,6,1024]{2,1,0:T(8,128)(2,1)} %all_to_all.40), calls=%async_computation.2 | async-start | bytes 2097152 | tf_op jit(solution)/shard_map/all_to_all | solution.py:127
  58.5 51.4 %all-to-all-done.2 = bf16[64,6,1024]{2,1,0:T(8,128)(2,1)S(1)} async-done(((bf16[64,6,1024]{2,1,0:T(8,128)(2,1)}), bf16[64,6,1024]{2,1,0:T(8,128)(2,1)S(1)}, u32[]{:S(2)}, u32[]{:S(2)}) %all-to-all-start.2) | async-done | bytes 786464 | tf_op jit(solution)/shard_map/all_to_all | solution.py:127
  112.7 12.8 %all-gather = f32[512,64]{1,0:T(8,128)S(1)} all-gather(f32[64,64]{1,0:T(8,128)S(1)} %copy.71), channel_id=2, replica_groups=mesh['rows'=64,'cols'=8] {'cols'}, dimensions={0}, use_global_device_ids=true | all-gather | bytes 147456 | tf_op jit(solution)/shard_map/all_gather | solution.py:29
  127.0 29.7 %all_to_all.56 = f32[64,1,1088]{2,1,0:T(1,128)S(1)} all-to-all(f32[64,1,1088]{2,1,0:T(1,128)S(1)} %all_to_all.43), channel_id=1, replica_groups=mesh['rows'=64,'cols'=8] {'rows'}, dimensions={0} | all-to-all | bytes 557056 | tf_op jit(solution)/shard_map/all_to_all | solution.py:39
  157.7 6.5 %all-to-all-start.4 = ((f32[64,1,1088]{2,1,0:T(1,128)}), f32[64,1,1088]{2,1,0:T(1,128)S(1)}, u32[]{:S(2)}, u32[]{:S(2)}) async-start(f32[64,1,1088]{2,1,0:T(1,128)} %broadcast_in_dim.67), calls=%async_computation.4 | async-start | bytes 589824 | tf_op jit(solution)/shard_map/all_to_all | solution.py:14
  164.9 20.9 %all-to-all-done.4 = f32[64,1,1088]{2,1,0:T(1,128)S(1)} async-done(((f32[64,1,1088]{2,1,0:T(1,128)}), f32[64,1,1088]{2,1,0:T(1,128)S(1)}, u32[]{:S(2)}, u32[]{:S(2)}) %all-to-all-start.4) | async-done | bytes 278560 | tf_op jit(solution)/shard_map/all_to_all | solution.py:14
  190.0 5.8 %cholesky.44 = f32[64,64]{1,0:T(8,128)S(1)} custom-call(f32[64,64]{1,0:T(8,128)S(1)} %fusion.20), custom_call_target="Cholesky" | custom-call | tf_op jit(solution)/shard_map/jit(cholesky)/cholesky | solution.py:106
  197.2 4.9 %custom-call.6 = f32[1,64,64]{1,2,0:T(8,128)S(1)} custom-call(f32[1,64,64]{2,1,0:T(8,128)S(1)} %get-tuple-element.15), custom_call_target="InvertDiagBlocksLowerTriangular" | custom-call | tf_op jit(solution)/shard_map/jit(_solve_triangular)/triangular_solve | solution.py:107
  202.6 2.3 select_multiply_fusion.1
  205.5 12.8 %all-gather.1 = f32[512,64]{1,0:T(8,128)S(1)} all-gather(f32[64,64]{1,0:T(8,128)S(1)} %copy.78), channel_id=3, replica_groups=mesh['rows'=64,'cols'=8] {'cols'}, dimensions={0}, use_global_device_ids=true | all-gather | bytes 147456 | tf_op jit(solution)/shard_map/all_gather | solution.py:29
  219.9 29.1 %all_to_all.57 = f32[64,1,1088]{2,1,0:T(1,128)S(1)} all-to-all(f32[64,1,1088]{2,1,0:T(1,128)S(1)} %all_to_all.46), channel_id=1, replica_groups=mesh['rows'=64,'cols'=8] {'rows'}, dimensions={0} | all-to-all | bytes 557056 | tf_op jit(solution)/shard_map/all_to_all | solution.py:39
  250.1 6.5 %all-to-all-start.6 = ((f32[64,1,1088]{2,1,0:T(1,128)}), f32[64,1,1088]{2,1,0:T(1,128)S(1)}, u32[]{:S(2)}, u32[]{:S(2)}) async-start(f32[64,1,1088]{2,1,0:T(1,128)} %broadcast_in_dim.72), calls=%async_computation.6 | async-start | bytes 589824 | tf_op jit(solution)/shard_map/all_to_all | solution.py:14
  256.6 21.6 %all-to-all-done.6 = f32[64,1,1088]{2,1,0:T(1,128)S(1)} async-done(((f32[64,1,1088]{2,1,0:T(1,128)}), f32[64,1,1088]{2,1,0:T(1,128)S(1)}, u32[]{:S(2)}, u32[]{:S(2)}) %all-to-all-start.6) | async-done | bytes 278560 | tf_op jit(solution)/shard_map/all_to_all | solution.py:14
  282.5 5.8 %cholesky.55 = f32[64,64]{1,0:T(8,128)S(1)} custom-call(f32[64,64]{1,0:T(8,128)S(1)} %fusion.18), custom_call_target="Cholesky" | custom-call | tf_op jit(solution)/shard_map/jit(cholesky)/cholesky | solution.py:106
  289.8 4.9 %custom-call.7 = f32[1,64,64]{1,2,0:T(8,128)S(1)} custom-call(f32[1,64,64]{2,1,0:T(8,128)S(1)} %get-tuple-element.17), custom_call_target="InvertDiagBlocksLowerTriangular" | custom-call | tf_op jit(solution)/shard_map/jit(_solve_triangular)/triangular_solve | solution.py:107
  296.6 2.3 select_multiply_fusion
  298.9 2.1 fusion.2
  301.0 1.9 copy.86
  (81 shorter events, 32.7 us)
Async XLA Ops:
  0.6 35.2 %copy-start = (bf16[1024,1024]{1,0:T(8,128)(2,1)S(1)}, bf16[1024,1024]{1,0:T(8,128)(2,1)}, u32[]{:S(2)}) copy-start(bf16[1024,1024]{1,0:T(8,128)(2,1)} %param.11) | copy-start | bytes 6291460
  2.5 14.6 %all-to-all-start.1 = ((bf16[8,32,1024]{2,1,0:T(8,128)(2,1)}), bf16[8,32,1024]{2,1,0:T(8,128)(2,1)S(1)}, u32[]{:S(2)}, u32[]{:S(2)}) async-start(bf16[8,32,1024]{2,1,0:T(8,128)(2,1)} %broadcast_in_dim.66), calls=%async_computation.1 | async-start | bytes 1048576 | tf_op jit(solution)/shard_map/all_to_all | solution.py:14
  17.1 32.2 %all-to-all-start = ((s32[64,6,1]{1,2,0:T(1,128)}), s32[64,6,1]{1,2,0:T(1,128)S(1)}, u32[]{:S(2)}, u32[]{:S(2)}) async-start(s32[64,6,1]{1,2,0:T(1,128)} %bitcast.5), calls=%async_computation | async-start | bytes 65536 | tf_op jit(solution)/shard_map/all_to_all | solution.py:128
  41.8 69.2 %copy-start.3 = (f32[64]{0:T(128)S(1)}, f32[64]{0:T(128)}, u32[]{:S(2)}) copy-start(f32[64]{0:T(128)} %param.15) | copy-start | bytes 772
  49.3 60.5 %all-to-all-start.2 = ((bf16[64,6,1024]{2,1,0:T(8,128)(2,1)}), bf16[64,6,1024]{2,1,0:T(8,128)(2,1)S(1)}, u32[]{:S(2)}, u32[]{:S(2)}) async-start(bf16[64,6,1024]{2,1,0:T(8,128)(2,1)} %all_to_all.40), calls=%async_computation.2 | async-start | bytes 2097152 | tf_op jit(solution)/shard_map/all_to_all | solution.py:127
  157.7 28.1 %all-to-all-start.4 = ((f32[64,1,1088]{2,1,0:T(1,128)}), f32[64,1,1088]{2,1,0:T(1,128)S(1)}, u32[]{:S(2)}, u32[]{:S(2)}) async-start(f32[64,1,1088]{2,1,0:T(1,128)} %broadcast_in_dim.67), calls=%async_computation.4 | async-start | bytes 589824 | tf_op jit(solution)/shard_map/all_to_all | solution.py:14
  218.4 1.1 copy-start.2
  250.1 28.1 %all-to-all-start.6 = ((f32[64,1,1088]{2,1,0:T(1,128)}), f32[64,1,1088]{2,1,0:T(1,128)S(1)}, u32[]{:S(2)}, u32[]{:S(2)}) async-start(f32[64,1,1088]{2,1,0:T(1,128)} %broadcast_in_dim.72), calls=%async_computation.6 | async-start | bytes 589824 | tf_op jit(solution)/shard_map/all_to_all | solution.py:14
  282.5 20.5 %copy-start.1 = (f32[64,1024]{0,1:T(8,128)S(1)}, f32[64,1024]{0,1:T(8,128)}, u32[]{:S(2)}) copy-start(f32[64,1024]{0,1:T(8,128)} %get-tuple-element.20) | copy-start | bytes 786436
where the time goes:
time: 306 us; the launch traced here: 305 us
  waiting for transfers between devices  106 us (35%)
  blocking collectives  84.5 us (28%)
  starting transfers between devices  43.9 us (14%)
  other arithmetic  32.3 us (11%)
  local copies, waits for them, and re-layouts  20.5 us (7%)
  matrix products  14.6 us (5%)
    all_to_all x2, blocking collectives, summed_on_arrival(): lax.all_to_all(pieces, axis, split_axis=0, concat_axis=0, tiled=True)  58.8 us
    all_to_all x1, waiting for transfers between devices, body(): lax.all_to_all(packed, 'rows', split_axis=0, concat_axis=0, tiled=True)  51.4 us
    all_to_all x3, waiting for transfers between devices, copy_for_each(): return lax.all_to_all(copies, axis, split_axis=0, concat_axis=0, tiled=True)  47.6 us
    all_gather x2, blocking collectives, picked(): lax.all_gather(array, axis)  25.7 us
    all_to_all x1, starting transfers between devices, body(): lax.all_to_all(slot_labels, 'rows', split_axis=0, concat_axis=0, tiled=True)  18.7 us
    all_to_all x3, starting transfers between devices, copy_for_each(): return lax.all_to_all(copies, axis, split_axis=0, concat_axis=0, tiled=True)  17.4 us
    another operation x6, other arithmetic, factor(): jnp.linalg.cholesky(gram_mat + shift * jnp.eye(PW, dtype=jnp.float32))  13.1 us
    another operation x2, other arithmetic, factor(): jax.scipy.linalg.solve_triangular(chol_lower, jnp.eye(PW, dtype=jnp.float...  9.79 us
  transfers between devices with their start and end apart: 5, of which 5 were waited for; matrix products, arithmetic and copies ran while one was open for 3% of the time, Pallas kernels for 0%

commit v1 on v0

v1 whole, which is shorter than its diff:
```python
import functools
import math

import jax
import jax.numpy as jnp
from jax import lax
from jax.experimental import pallas as pl
from jax.experimental.pallas import tpu as pltpu
from jax.sharding import PartitionSpec as P

PW = 64
PANELS = 2
WIDE = PW * PANELS
CAP = 3
HALF = 128
LANES = 128
GROUP = 8
SLOTS = 2 * CAP
Y, Z = 4, 16
F32, BF16 = jnp.float32, jnp.bfloat16
HIGHEST = lax.Precision.HIGHEST
VMEM_LIMIT = 48 * 2**20


def dot(a, b, dims=((1,), (0,)), precision=None):
    return lax.dot_general(
        a, b, (dims, ((), ())), precision=precision, preferred_element_type=F32
    )


def iota(shape, dim):
    return lax.broadcasted_iota(jnp.int32, shape, dim)


def one_hot(condition):
    return condition.astype(F32).astype(BF16)


def called(kernel, out_shape, *args):
    return pl.pallas_call(
        kernel,
        out_shape=out_shape,
        compiler_params=pltpu.CompilerParams(vmem_limit_bytes=VMEM_LIMIT),
    )(*args)


def to_each(array, axis, groups=None):
    count = lax.axis_size(axis) if groups is None else len(groups[0])
    copies = jnp.broadcast_to(array, (count, *array.shape))
    return lax.all_to_all(
        copies, axis, split_axis=0, concat_axis=0, tiled=True, axis_index_groups=groups
    )


def pack_kernel(env_ref, owner_ref, structure_ref, out_ref, owners):
    owner = owner_ref[...]
    envs = owner.shape[1]
    matches = iota((owners, envs), 0) == owner
    earlier = (iota((envs, envs), 0) < iota((envs, envs), 1)) & (
        iota((envs, envs), 0) // HALF == iota((envs, envs), 1) // HALF
    )
    before = dot(one_hot(matches), one_hot(earlier))
    within = jnp.sum(jnp.where(matches, before, 0.0), axis=0, keepdims=True).astype(jnp.int32)
    place = (iota((1, envs), 1) // HALF) * CAP + within
    slot = owner * GROUP + place
    chosen = one_hot(iota((owners * GROUP, envs), 0) == slot)
    data = dot(chosen, env_ref[...].reshape(envs, LANES))
    named = jnp.where(matches, structure_ref[...], 0).astype(F32).astype(BF16)
    at = one_hot(iota((LANES, envs), 0) == place)
    labels = dot(named, at, ((1,), (1,)))
    spread = one_hot(iota((owners * GROUP, owners), 0) == iota((owners * GROUP, owners), 1) * GROUP + SLOTS)
    out_ref[...] = (data + dot(spread, labels.astype(BF16))).astype(BF16)


def unpack_kernel(got_ref, out_ref, label_ref):
    rows = got_ref.shape[0]
    sources = rows // GROUP
    slots = sources * SLOTS
    got = got_ref[...]
    slot, row = iota((slots, rows), 0), iota((slots, rows), 1)
    source, place = slot // SLOTS, slot % SLOTS
    out_ref[...] = dot(one_hot(row == source * GROUP + place), got).astype(BF16)
    named = dot(one_hot(row == source * GROUP + SLOTS), got)
    own = iota((slots, LANES), 1) == iota((slots, LANES), 0) % SLOTS
    label_ref[...] = jnp.sum(jnp.where(own, named, 0.0), axis=1, keepdims=True)


def equations_kernel(
    got_ref, label_ref, points_ref, scale_ref, extra_ref, weight_ref, matrix_ref, sums_ref, env_ref
):
    chunks, rows, _ = got_ref.shape
    slots = rows - WIDE
    eqs = weight_ref.shape[0]
    cols = points_ref.shape[0]
    for chunk in range(chunks):
        env_ref[:, chunk * LANES : (chunk + 1) * LANES] = got_ref[chunk]
    dot_scale = env_ref.shape[1] ** (-0.5)
    chosen = one_hot(label_ref[...].astype(jnp.int32) == iota((slots, eqs), 1))
    weight = weight_ref[...]

    def block(points, scale):
        z = dot(env_ref[0:slots, :], points, ((1,), (1,))) * dot_scale
        squared = z * z
        kernel = (scale * squared * squared).astype(BF16)
        return dot(chosen, kernel, ((0,), (0,))) * weight

    extra = extra_ref[...].astype(F32)
    panel = block(env_ref[slots:rows, :], extra[0:1] + extra[1:2] + extra[2:3])
    matrix_ref[:, cols : cols + WIDE] = panel
    gram = dot(panel, panel, ((0,), (0,)), HIGHEST)
    high = gram.astype(BF16)
    low = (gram - high.astype(F32)).astype(BF16)
    count = sums_ref.shape[0]
    row, col = iota((count * 8, 4 * count), 0), iota((count * 8, 4 * count), 1)
    spread = one_hot((row // 8 == col % count) & (row % 8 == col // count))
    gram_rows = dot(spread, jnp.concatenate([high, low], axis=0))
    sums_ref[:, 16:24, :] = gram_rows.astype(BF16).reshape(count, 8, LANES)
    step = 256
    for first in range(0, cols, step):
        part = block(points_ref[first : first + step, :], scale_ref[:, first : first + step])
        matrix_ref[:, first : first + step] = part
        cross = dot(panel, part, ((0,), (0,)), HIGHEST).astype(BF16)
        for at in range(0, step, LANES):
            k = (first + at) // LANES
            sums_ref[8 * k : 8 * k + 8, 0:16, :] = cross[:, at : at + LANES].reshape(8, 16, LANES)


def added_kernel(got_ref, out_ref):
    total = jnp.sum(got_ref[...].astype(F32), axis=0)
    out_ref[0:16, :] = total[0:16]
    out_ref[16:18, :] = total[16:18] + total[18:20]
    out_ref[18:24, :] = jnp.zeros((6, LANES), F32)


def eliminated(gram, shift):
    own = iota((PW, PW), 0) == iota((PW, PW), 1)
    eye = own.astype(F32)
    work = jnp.concatenate([gram + shift * eye, eye], axis=1)
    rows = iota((PW, 1), 0)
    for k in range(PW - 1):
        pivot_row = work[k : k + 1, :]
        ratio = work[:, k : k + 1] / work[k : k + 1, k : k + 1]
        work = work - jnp.where(rows > k, ratio, 0.0) * pivot_row
    pivots = jnp.sum(jnp.where(own, work[:, :PW], 0.0), axis=1, keepdims=True)
    work = work * lax.rsqrt(pivots)
    upper = jnp.where(iota((PW, PW), 0) <= iota((PW, PW), 1), work[:, :PW], 0.0)
    return upper, work[:, PW:]


def factor_kernel(total_ref, matrix_ref, ridge_ref, first_ref, r_ref, reduced_ref, norm_scale):
    ridge = ridge_ref[0]
    first = first_ref[0] == 0
    eqs, cols = reduced_ref.shape
    gram = jnp.concatenate([total_ref[:, 16, :], total_ref[:, 17, :]], axis=0)
    own = iota((PW, PW), 0) == iota((PW, PW), 1)

    def shift_of(a):
        return ridge * jnp.sum(jnp.where(own, a, 0.0)) / PW + 1e-06

    g00, g01, g11 = gram[:PW, :PW], gram[:PW, PW:], gram[PW:, PW:]
    shift0 = shift_of(g00)
    upper0, inverse0 = eliminated(g00, shift0)
    c01 = dot(inverse0, g01, precision=HIGHEST)
    w01 = dot(inverse0, c01, ((0,), (0,)), HIGHEST)
    gram1 = (
        g11
        - dot(c01, c01, ((0,), (0,)), HIGHEST)
        - shift0 * dot(w01, w01, ((0,), (0,)), HIGHEST)
    )
    upper1, inverse1 = eliminated(gram1, shift_of(gram1))
    panel = matrix_ref[:, cols : cols + WIDE]
    q0 = dot(panel[:, :PW], inverse0, ((1,), (1,)), HIGHEST)
    q1 = dot(panel[:, PW:] - dot(q0, c01, precision=HIGHEST), inverse1, ((1,), (1,)), HIGHEST)
    zero = jnp.zeros((PW, PW), F32)
    for k in range(cols // LANES):
        at = slice(k * LANES, (k + 1) * LANES)
        cross = total_ref[8 * k : 8 * k + 8, 0:16, :].reshape(WIDE, LANES)
        c0 = dot(inverse0, cross[:PW], precision=HIGHEST)
        w0 = dot(inverse0, c0, ((0,), (0,)), HIGHEST)
        rest = (
            cross[PW:]
            - dot(c01, c0, ((0,), (0,)), HIGHEST)
            - shift0 * dot(w01, w0, ((0,), (0,)), HIGHEST)
        )
        c1 = dot(inverse1, rest, precision=HIGHEST)
        left = matrix_ref[:, at] - dot(q0, c0, precision=HIGHEST) - dot(q1, c1, precision=HIGHEST)
        if k == 0:
            c0 = jnp.where(first, jnp.concatenate([upper0, c01], axis=1), c0)
            c1 = jnp.where(first, jnp.concatenate([zero, upper1], axis=1), c1)
            left = jnp.where(first, jnp.concatenate([q0, q1], axis=1), left)
        r_ref[0:PW, at] = c0 * norm_scale
        r_ref[PW:WIDE, at] = c1 * norm_scale
        reduced_ref[:, at] = left


def body(
    descriptors, sparse_points, point_scale, env_owner, env_structure, row_weight, ridge_factor
):
    owners, peers = lax.axis_size("rows"), lax.axis_size("cols")
    eqs, cols = row_weight.shape[0], point_scale.shape[0]
    mine = descriptors.shape[0]
    envs = mine * peers
    z_groups = [[y * Z + z for z in range(Z)] for y in range(Y)]
    y_groups = [[y * Z + z for y in range(Y)] for z in range(Z)]

    scale = point_scale[:WIDE]
    high = lax.reduce_precision(scale, 8, 7)
    middle = lax.reduce_precision(scale - high, 8, 7)
    low = scale - high - middle
    parts = jnp.zeros((16, WIDE), F32).at[0].set(high).at[1].set(middle).at[2].set(low)
    sent = jnp.concatenate([descriptors, sparse_points[:WIDE]], axis=0)
    sent = sent.reshape(mine + WIDE, peers, LANES).transpose(1, 0, 2)
    sent = jnp.concatenate(
        [sent, jnp.broadcast_to(parts.astype(BF16), (peers, 16, WIDE))], axis=1
    )
    got = lax.all_to_all(sent, "cols", split_axis=0, concat_axis=0, tiled=True)
    panel_part = got[0, mine : mine + WIDE]
    extra = got[0, mine + WIDE :]

    packed = called(
        functools.partial(pack_kernel, owners=owners),
        jax.ShapeDtypeStruct((owners * GROUP, LANES), BF16),
        got[:, :mine],
        env_owner.reshape(1, envs),
        env_structure.reshape(1, envs),
    )
    arrived = lax.all_to_all(packed, "rows", split_axis=0, concat_axis=0, tiled=True)
    slots = owners * SLOTS
    slot_rows, labels = called(
        unpack_kernel,
        (
            jax.ShapeDtypeStruct((slots, LANES), BF16),
            jax.ShapeDtypeStruct((slots, 1), F32),
        ),
        arrived,
    )
    gathered = to_each(jnp.concatenate([slot_rows, panel_part], axis=0), "cols")

    matrix, sums = pl.pallas_call(
        equations_kernel,
        out_shape=(
            jax.ShapeDtypeStruct((eqs, cols + WIDE), F32),
            jax.ShapeDtypeStruct((owners, 24, LANES), BF16),
        ),
        scratch_shapes=[pltpu.VMEM((slots + WIDE, peers * LANES), BF16)],
        compiler_params=pltpu.CompilerParams(vmem_limit_bytes=VMEM_LIMIT),
    )(
        gathered,
        labels,
        sparse_points,
        point_scale.reshape(1, cols),
        extra,
        row_weight.reshape(eqs, 1),
    )
    partial = lax.all_to_all(sums, "rows", split_axis=0, concat_axis=0, tiled=True)
    added = called(added_kernel, jax.ShapeDtypeStruct((24, LANES), F32), partial)
    total = to_each(to_each(added, "rows", z_groups), "rows", y_groups)
    total = total.reshape(owners, 24, LANES)

    vmem, smem = pl.BlockSpec(memory_space=pltpu.VMEM), pl.BlockSpec(memory_space=pltpu.SMEM)
    return pl.pallas_call(
        functools.partial(factor_kernel, norm_scale=1.0 / math.sqrt(owners * eqs)),
        out_shape=(
            jax.ShapeDtypeStruct((WIDE, cols), F32),
            jax.ShapeDtypeStruct((eqs, cols), F32),
        ),
        in_specs=[vmem, vmem, smem, smem],
        out_specs=(vmem, vmem),
        compiler_params=pltpu.CompilerParams(vmem_limit_bytes=VMEM_LIMIT),
    )(total, matrix, ridge_factor, lax.axis_index("cols").reshape(1))


def solution(mesh):
    return jax.shard_map(
        body,
        mesh=mesh,
        in_specs=(
            P(("rows", "cols"), None),
            P("cols", None),
            P("cols"),
            P("rows", None),
            P("rows"),
            P("rows"),
            P(),
        ),
        out_specs=(P(None, "cols"), P("rows", "cols")),
        check_vma=False,
    )
```

time: 306 us -> 162 us (0.53)
  the two profiles are of different devices: /device:TPU:8 before, /device:TPU:32 now
where the time goes in v1:
time: 162 us; the launch traced here: 161 us
  blocking collectives  64.8 us (40%)
  waiting for transfers between devices  40.3 us (25%)
  starting transfers between devices  25.6 us (16%)
  Pallas kernels  22.6 us (14%)
  local copies, waits for them, and re-layouts  4.89 us (3%)
  other arithmetic  1.64 us (1%)
    all_to_all x1, blocking collectives, body(): lax.all_to_all(sums, 'rows', split_axis=0, concat_axis=0, tiled=True)  31.4 us
    all_to_all x2, waiting for transfers between devices, to_each(): lax.all_to_all(copies, axis, split_axis=0, concat_axis=0, tiled=True, axi...  24.7 us
    all_to_all x1, blocking collectives, to_each(): lax.all_to_all(copies, axis, split_axis=0, concat_axis=0, tiled=True, axi...  20.7 us
    all_to_all x1, starting transfers between devices, body(): lax.all_to_all(packed, 'rows', split_axis=0, concat_axis=0, tiled=True)  18.4 us
    pallas_call x1, Pallas kernels, body(): pl.pallas_call(functools.partial(factor_kernel, norm_scale=1.0 / math.sqr...  17.1 us
    all_to_all x1, waiting for transfers between devices, body(): lax.all_to_all(packed, 'rows', split_axis=0, concat_axis=0, tiled=True)  15.7 us
    all_to_all x1, blocking collectives, body(): got = lax.all_to_all(sent, 'cols', split_axis=0, concat_axis=0, tiled=True)  12.7 us
    all_to_all x2, starting transfers between devices, to_each(): lax.all_to_all(copies, axis, split_axis=0, concat_axis=0, tiled=True, axi...  7.23 us
  transfers between devices with their start and end apart: 3, of which 3 were waited for; matrix products, arithmetic and copies ran while one was open for 0% of the time, Pallas kernels for 0%

profile of v1, /device:TPU:32, one launch (start us, length us, event | category | flops | bytes accessed | tf_op | source)
XLA Modules:
  0.0 161.3 jit_solution(13597660847976577324)
XLA Ops:
  0.6 0.7 fusion
  1.4 1.0 slice.59
  2.3 0.9 bitcast_bitcast_fusion
  3.3 12.7 %all_to_all.36 = bf16[8,176,128]{2,1,0:T(8,128)(2,1)S(1)} all-to-all(bf16[8,176,128]{2,1,0:T(8,128)(2,1)S(1)} %pad_maximum_fusion), channel_id=1, replica_groups=mesh['rows'=64,'cols'=8] {'cols'}, dimensions={0} | all-to-all | bytes 720896 | tf_op jit(solution)/shard_map/all_to_all | solution.py:216
  16.1 0.0 copy-start.7
  16.1 0.0 copy-start.3
  16.1 1.2 shard_map.86
  17.3 18.4 %all-to-all-start.1 = ((bf16[64,8,128]{2,1,0:T(8,128)(2,1)}), bf16[64,8,128]{2,1,0:T(8,128)(2,1)S(1)}, u32[]{:S(2)}, u32[]{:S(2)}) async-start(bf16[64,8,128]{2,1,0:T(8,128)(2,1)} %bitcast.6), calls=%async_computation.1 | async-start | bytes 262144 | tf_op jit(solution)/shard_map/all_to_all | solution.py:227
  35.7 15.7 %all-to-all-done.1 = bf16[64,8,128]{2,1,0:T(8,128)(2,1)S(1)} async-done(((bf16[64,8,128]{2,1,0:T(8,128)(2,1)}), bf16[64,8,128]{2,1,0:T(8,128)(2,1)S(1)}, u32[]{:S(2)}, u32[]{:S(2)}) %all-to-all-start.1) | async-done | bytes 131104 | tf_op jit(solution)/shard_map/all_to_all | solution.py:227
  51.4 0.5 shard_map.87
  51.9 1.1 broadcast_in_dim.14
  53.0 3.6 %all-to-all-start.2 = ((bf16[8,512,128]{2,1,0:T(8,128)(2,1)}), bf16[8,512,128]{2,1,0:T(8,128)(2,1)S(1)}, u32[]{:S(2)}, u32[]{:S(2)}) async-start(bf16[8,512,128]{2,1,0:T(8,128)(2,1)} %broadcast_in_dim.14), calls=%async_computation.2 | async-start | bytes 2097152 | tf_op jit(solution)/shard_map/all_to_all | solution.py:50
  56.6 0.1 copy.11.weight_ref
  56.7 0.7 slice_bitcast_fusion.1.extra_ref
  57.4 15.1 %all-to-all-done.2.got_ref = bf16[8,512,128]{2,1,0:T(8,128)(2,1)S(1)} async-done(((bf16[8,512,128]{2,1,0:T(8,128)(2,1)}), bf16[8,512,128]{2,1,0:T(8,128)(2,1)S(1)}, u32[]{:S(2)}, u32[]{:S(2)}) %all-to-all-start.2) | async-done | bytes 1048608 | tf_op jit(solution)/shard_map/all_to_all | solution.py:50
  72.5 0.9 copy-done.2
  73.4 3.8 %shard_map.88 = (f32[64,1152]{1,0:T(8,128)S(1)}, bf16[64,24,128]{2,1,0:T(8,128)(2,1)S(1)}) custom-call(bf16[8,512,128]{2,1,0:T(8,128)(2,1)S(1)} %all-to-all-done.2.got_ref, f32[384,1]{1,0:T(8,128)S(1)} %copy-done.2, bf16[1024,1024]{1,0:T(8,128)(2,1)S(1)} %copy-done, f32[1,1024]{1,0:T(1,128)S(1)} %bitcast.27, ...), custom_call_target="tpu_custom_call" | custom-call | tf_op jit(solution)/shard_map/pallas_call | solution.py:239
  77.2 31.4 %all_to_all.37.got_ref = bf16[64,24,128]{2,1,0:T(8,128)(2,1)S(1)} all-to-all(bf16[64,24,128]{2,1,0:T(8,128)(2,1)S(1)} %get-tuple-element.44), channel_id=1, replica_groups=mesh['rows'=64,'cols'=8] {'rows'}, dimensions={0} | all-to-all | bytes 786432 | tf_op jit(solution)/shard_map/all_to_all | solution.py:255
  108.6 0.1 shard_map.89
  108.7 20.7 %all_to_all.38 = f32[16,24,128]{2,1,0:T(8,128)S(1)} all-to-all(f32[16,24,128]{2,1,0:T(8,128)S(1)} %broadcast_in_dim.15), channel_id=1, replica_groups={{0,8,16,24,32,40,48,56,64,72,80,88,96,104,112,120},{128,136,144,152,160..., dimensions={0} | all-to-all | bytes 393216 | tf_op jit(solution)/shard_map/all_to_all | solution.py:50
  129.4 1.0 broadcast_in_dim.16
  130.4 3.7 %all-to-all-start.5 = ((f32[4,16,24,128]{3,2,1,0:T(8,128)}), f32[4,16,24,128]{3,2,1,0:T(8,128)S(1)}, u32[]{:S(2)}, u32[]{:S(2)}) async-start(f32[4,16,24,128]{3,2,1,0:T(8,128)} %broadcast_in_dim.16), calls=%async_computation.5 | async-start | bytes 1572864 | tf_op jit(solution)/shard_map/all_to_all | solution.py:50
  134.7 9.6 %all-to-all-done.5 = f32[4,16,24,128]{3,2,1,0:T(8,128)S(1)} async-done(((f32[4,16,24,128]{3,2,1,0:T(8,128)}), f32[4,16,24,128]{3,2,1,0:T(8,128)S(1)}, u32[]{:S(2)}, u32[]{:S(2)}) %all-to-all-start.5) | async-done | bytes 786464 | tf_op jit(solution)/shard_map/all_to_all | solution.py:50
  144.3 17.1 %shard_map.90 = (f32[128,1024]{1,0:T(8,128)}, f32[64,1024]{1,0:T(8,128)}) custom-call(f32[64,24,128]{2,1,0:T(8,128)S(1)} %bitcast.25, f32[64,1152]{1,0:T(8,128)S(1)} %get-tuple-element.45.matrix_ref, f32[1]{0:T(128)S(6)} %copy.16.ridge_ref, s32[1]{0:T(128)} %bitcast.13.first_ref), custom_call_target="tpu_custom_call" | custom-call | tf_op jit(solution)/shard_map/pallas_call | solution.py:261
  (22 shorter events, 0.2 us)
Async XLA Ops:
  0.6 15.4 %copy-start.5 = (s32[256]{0:T(256)S(1)}, s32[256]{0:T(256)}, u32[]{:S(2)}) copy-start(s32[256]{0:T(256)} %param.17) | copy-start | bytes 3076
  0.6 15.4 %copy-start.4 = (s32[256,1]{0,1:T(1,128)S(1)}, s32[256,1]{0,1:T(1,128)}, u32[]{:S(2)}) copy-start(s32[256,1]{0,1:T(1,128)} %param.16) | copy-start | bytes 3076
  16.0 37.0 %copy-start.6 = (bf16[8,176,128]{2,1,0:T(8,128)(2,1)}, bf16[8,176,128]{2,1,0:T(8,128)(2,1)S(1)}, u32[]{:S(2)}) copy-start(bf16[8,176,128]{2,1,0:T(8,128)(2,1)S(1)} %all_to_all.36) | copy-start | bytes 1081348
  16.1 40.5 %copy-start.7 = (f32[64]{0:T(128)S(1)}, f32[64]{0:T(128)}, u32[]{:S(2)}) copy-start(f32[64]{0:T(128)} %param.18) | copy-start | bytes 772
  16.1 56.4 %copy-start = (bf16[1024,1024]{1,0:T(8,128)(2,1)S(1)}, bf16[1024,1024]{1,0:T(8,128)(2,1)}, u32[]{:S(2)}) copy-start(bf16[1024,1024]{1,0:T(8,128)(2,1)} %points_ref.1) | copy-start | bytes 6291460
  16.1 56.4 %copy-start.3 = (f32[1024]{0:T(1024)S(1)}, f32[1024]{0:T(1024)}, u32[]{:S(2)}) copy-start(f32[1024]{0:T(1024)} %param.15) | copy-start | bytes 12292
  17.3 34.1 %all-to-all-start.1 = ((bf16[64,8,128]{2,1,0:T(8,128)(2,1)}), bf16[64,8,128]{2,1,0:T(8,128)(2,1)S(1)}, u32[]{:S(2)}, u32[]{:S(2)}) async-start(bf16[64,8,128]{2,1,0:T(8,128)(2,1)} %bitcast.6), calls=%async_computation.1 | async-start | bytes 262144 | tf_op jit(solution)/shard_map/all_to_all | solution.py:227
  51.9 1.1 copy-start.1
  53.0 19.4 %all-to-all-start.2 = ((bf16[8,512,128]{2,1,0:T(8,128)(2,1)}), bf16[8,512,128]{2,1,0:T(8,128)(2,1)S(1)}, u32[]{:S(2)}, u32[]{:S(2)}) async-start(bf16[8,512,128]{2,1,0:T(8,128)(2,1)} %broadcast_in_dim.14), calls=%async_computation.2 | async-start | bytes 2097152 | tf_op jit(solution)/shard_map/all_to_all | solution.py:50
  72.5 0.9 copy-start.2
  130.4 13.9 %all-to-all-start.5 = ((f32[4,16,24,128]{3,2,1,0:T(8,128)}), f32[4,16,24,128]{3,2,1,0:T(8,128)S(1)}, u32[]{:S(2)}, u32[]{:S(2)}) async-start(f32[4,16,24,128]{3,2,1,0:T(8,128)} %broadcast_in_dim.16), calls=%async_computation.5 | async-start | bytes 1572864 | tf_op jit(solution)/shard_map/all_to_all | solution.py:50

commit v2 on v1

v2 whole, which is shorter than its diff:
```python
import functools
import math

import jax
import jax.numpy as jnp
from jax import lax
from jax.experimental import pallas as pl
from jax.experimental.pallas import tpu as pltpu
from jax.sharding import PartitionSpec as P

PW = 64
PANELS = 2
WIDE = PW * PANELS
CAP = 3
HALF = 128
LANES = 128
GROUP = 8
SLOTS = 2 * CAP
STEP = 4
Y, Z = 4, 16
F32, BF16 = jnp.float32, jnp.bfloat16
HIGHEST = lax.Precision.HIGHEST
VMEM_LIMIT = 48 * 2**20


def dot(a, b, dims=((1,), (0,)), precision=None):
    return lax.dot_general(
        a, b, (dims, ((), ())), precision=precision, preferred_element_type=F32
    )


def iota(shape, dim):
    return lax.broadcasted_iota(jnp.int32, shape, dim)


def one_hot(condition):
    return condition.astype(F32).astype(BF16)


def called(kernel, out_shape, *args):
    return pl.pallas_call(
        kernel,
        out_shape=out_shape,
        compiler_params=pltpu.CompilerParams(vmem_limit_bytes=VMEM_LIMIT),
    )(*args)


def to_each(array, axis, groups=None):
    count = lax.axis_size(axis) if groups is None else len(groups[0])
    copies = jnp.broadcast_to(array, (count, *array.shape))
    return lax.all_to_all(
        copies, axis, split_axis=0, concat_axis=0, tiled=True, axis_index_groups=groups
    )


def pack_kernel(env_ref, owner_ref, structure_ref, out_ref, owners):
    owner = owner_ref[...]
    envs = owner.shape[1]
    matches = iota((owners, envs), 0) == owner
    earlier = (iota((envs, envs), 0) < iota((envs, envs), 1)) & (
        iota((envs, envs), 0) // HALF == iota((envs, envs), 1) // HALF
    )
    before = dot(one_hot(matches), one_hot(earlier))
    within = jnp.sum(jnp.where(matches, before, 0.0), axis=0, keepdims=True).astype(jnp.int32)
    place = (iota((1, envs), 1) // HALF) * CAP + within
    slot = owner * GROUP + place
    chosen = one_hot(iota((owners * GROUP, envs), 0) == slot)
    data = dot(chosen, env_ref[...].reshape(envs, LANES))
    named = jnp.where(matches, structure_ref[...], 0).astype(F32).astype(BF16)
    at = one_hot(iota((LANES, envs), 0) == place)
    labels = dot(named, at, ((1,), (1,)))
    spread = one_hot(iota((owners * GROUP, owners), 0) == iota((owners * GROUP, owners), 1) * GROUP + SLOTS)
    out_ref[...] = (data + dot(spread, labels.astype(BF16))).astype(BF16)


def unpack_kernel(got_ref, out_ref, label_ref):
    rows = got_ref.shape[0]
    sources = rows // GROUP
    slots = sources * SLOTS
    got = got_ref[...]
    slot, row = iota((slots, rows), 0), iota((slots, rows), 1)
    source, place = slot // SLOTS, slot % SLOTS
    data = dot(one_hot(row == source * GROUP + place), got).astype(BF16)
    for copy in range(out_ref.shape[0]):
        out_ref[copy] = data
    named = dot(one_hot(row == source * GROUP + SLOTS), got)
    own = iota((slots, LANES), 1) == iota((slots, LANES), 0) % SLOTS
    label_ref[...] = jnp.sum(jnp.where(own, named, 0.0), axis=1, keepdims=True)


def equations_kernel(
    core_ref,
    own_ref,
    other_ref,
    label_ref,
    points_ref,
    scale_ref,
    panel_ref,
    weight_ref,
    matrix_ref,
    sums_ref,
    env_ref,
):
    chips, slots, _ = own_ref.shape
    eqs = weight_ref.shape[0]
    cols = points_ref.shape[0]
    core = core_ref[0]
    for chip in range(chips):
        at = pl.multiple_of((2 * chip + core) * LANES, LANES)
        env_ref[:, pl.ds(at, LANES)] = own_ref[chip]
        at = pl.multiple_of((2 * chip + 1 - core) * LANES, LANES)
        env_ref[:, pl.ds(at, LANES)] = other_ref[chip]
    dot_scale = env_ref.shape[1] ** (-0.5)
    chosen = one_hot(label_ref[...].astype(jnp.int32) == iota((slots, eqs), 1))
    weight = weight_ref[...]

    def block(points, scale):
        z = dot(env_ref[...], points, ((1,), (1,))) * dot_scale
        squared = z * z
        kernel = (scale * squared * squared).astype(BF16)
        return dot(chosen, kernel, ((0,), (0,))) * weight

    parts = panel_ref[WIDE:, 0:WIDE].astype(F32)
    panel = block(panel_ref[0:WIDE, :], parts[0:1] + parts[1:2] + parts[2:3])
    matrix_ref[:, cols : cols + WIDE] = panel
    gram = dot(panel, panel, ((0,), (0,)), HIGHEST)
    high = gram.astype(BF16)
    low = (gram - high.astype(F32)).astype(BF16)
    members, length, _ = sums_ref.shape
    own_rows = length - 2 * WIDE
    for member in range(members):
        sums_ref[member, own_rows : own_rows + WIDE] = high
        sums_ref[member, own_rows + WIDE : length] = low
    step = 256
    for first in range(0, cols, step):
        part = block(points_ref[first : first + step, :], scale_ref[:, first : first + step])
        matrix_ref[:, first : first + step] = part
        cross = dot(panel, part, ((0,), (0,)), HIGHEST).astype(BF16)
        for at in range(0, step, LANES):
            member, start = divmod((first + at) // LANES * WIDE, own_rows)
            sums_ref[member, start : start + WIDE] = cross[:, at : at + LANES]


def near_kernel(got_ref, out_ref):
    total = jnp.sum(got_ref[...].astype(F32), axis=0)
    count, length, _ = out_ref.shape
    own_rows = total.shape[0] - 2 * WIDE
    own = own_rows // count
    gram = total[own_rows : own_rows + WIDE] + total[own_rows + WIDE :]
    out_ref[:, 0:own] = total[:own_rows].reshape(count, own, LANES)
    out_ref[:, own:length] = gram.reshape(count, length - own, LANES)


def far_kernel(got_ref, out_ref):
    total = jnp.sum(got_ref[...], axis=0)
    for copy in range(out_ref.shape[0]):
        out_ref[copy] = total


def eliminated(gram, shift):
    own = iota((PW, PW), 0) == iota((PW, PW), 1)
    eye = own.astype(F32)
    work = jnp.concatenate([gram + shift * eye, eye], axis=1)
    rows = iota((PW, 1), 0)
    for k in range(0, PW, STEP):
        cols = [jnp.broadcast_to(work[:, k + j : k + j + 1], (PW, WIDE)) for j in range(STEP)]
        pivot = [work[k + i : k + i + 1, :] for i in range(STEP)]
        inner = [[cols[j][k + i : k + i + 1, :] for j in range(STEP)] for i in range(STEP)]
        for a in range(STEP):
            inverse = 1.0 / inner[a][a]
            for i in range(a + 1, STEP):
                ratio = inner[i][a] * inverse
                pivot[i] = pivot[i] - ratio * pivot[a]
                for j in range(a + 1, STEP):
                    inner[i][j] = inner[i][j] - ratio * inner[a][j]
            cols[a] = cols[a] * inverse
            for j in range(a + 1, STEP):
                cols[j] = cols[j] - cols[a] * inner[a][j]
        below = work
        for a in range(STEP):
            below = below - cols[a] * pivot[a]
        work = jnp.where(rows >= k + STEP, below, work)
        for a in range(STEP):
            work = jnp.where(rows == k + a, pivot[a], work)
    pivots = jnp.sum(jnp.where(own, work[:, :PW], 0.0), axis=1, keepdims=True)
    work = work * lax.rsqrt(pivots)
    upper = jnp.where(iota((PW, PW), 0) <= iota((PW, PW), 1), work[:, :PW], 0.0)
    return upper, work[:, PW:]


def factor_kernel(gram_ref, ridge_ref, terms_ref, turn_ref, upper_ref):
    ridge = ridge_ref[0]
    count, length, _ = gram_ref.shape
    gram = gram_ref[:, length - WIDE // count : length].reshape(WIDE, WIDE)
    own = iota((PW, PW), 0) == iota((PW, PW), 1)

    def shift_of(a):
        return ridge * jnp.sum(jnp.where(own, a, 0.0)) / PW + 1e-06

    g00, g01, g11 = gram[:PW, :PW], gram[:PW, PW:], gram[PW:, PW:]
    shift0 = shift_of(g00)
    upper0, inverse0 = eliminated(g00, shift0)
    c01 = dot(inverse0, g01, precision=HIGHEST)
    w01 = dot(inverse0, c01, ((0,), (0,)), HIGHEST)
    gram1 = (
        g11
        - dot(c01, c01, ((0,), (0,)), HIGHEST)
        - shift0 * dot(w01, w01, ((0,), (0,)), HIGHEST)
    )
    upper1, inverse1 = eliminated(gram1, shift_of(gram1))
    mixed = c01 + shift0 * dot(inverse0, w01, precision=HIGHEST)
    both = jnp.concatenate([mixed, c01], axis=1)
    taken = dot(both, inverse0, ((0,), (0,)), HIGHEST)
    zero = jnp.zeros((PW, PW), F32)
    terms_ref[0:PW, :] = jnp.concatenate([inverse0, zero], axis=1)
    terms_ref[PW:WIDE, :] = jnp.concatenate(
        [-dot(inverse1, taken[:PW], precision=HIGHEST), inverse1], axis=1
    )
    turn_ref[0:PW, :] = jnp.concatenate([inverse0, zero], axis=1)
    turn_ref[PW:WIDE, :] = jnp.concatenate(
        [-dot(inverse1, taken[PW:], precision=HIGHEST), inverse1], axis=1
    )
    upper_ref[0:PW, :] = jnp.concatenate([upper0, c01], axis=1)
    upper_ref[PW:WIDE, :] = jnp.concatenate([zero, upper1], axis=1)


def final_kernel(
    first_ref, total_ref, terms_ref, turn_ref, upper_ref, matrix_ref, r_ref, reduced_ref, norm_scale
):
    first = first_ref[0] == 0
    cols = reduced_ref.shape[1]
    terms = terms_ref[...]
    q = dot(matrix_ref[:, cols : cols + WIDE], turn_ref[...], ((1,), (1,)), HIGHEST)
    step = 256
    for k in range(cols // step):
        at = slice(k * step, (k + 1) * step)
        cross = jnp.concatenate(
            [
                total_ref[8 * j : 8 * j + 8].reshape(WIDE, LANES)
                for j in range(k * step // LANES, (k + 1) * step // LANES)
            ],
            axis=1,
        )
        coupled = dot(terms, cross, precision=HIGHEST)
        r_ref[:, at] = coupled * norm_scale
        reduced_ref[:, at] = matrix_ref[:, at] - dot(q, coupled, precision=HIGHEST)

    @pl.when(first)
    def _():
        r_ref[:, 0:WIDE] = upper_ref[...] * norm_scale
        reduced_ref[:, 0:WIDE] = q


def body(
    descriptors, sparse_points, point_scale, env_owner, env_structure, row_weight, ridge_factor
):
    owners, peers = lax.axis_size("rows"), lax.axis_size("cols")
    eqs, cols = row_weight.shape[0], point_scale.shape[0]
    mine = descriptors.shape[0]
    envs = mine * peers
    z_groups = [[y * Z + z for z in range(Z)] for y in range(Y)]
    y_groups = [[y * Z + z for y in range(Y)] for z in range(Z)]

    scale = point_scale[:WIDE]
    high = lax.reduce_precision(scale, 8, 7)
    middle = lax.reduce_precision(scale - high, 8, 7)
    low = scale - high - middle
    parts = jnp.pad(jnp.stack([high, middle, low]), ((0, 13), (0, peers * LANES - WIDE)))
    panel = jnp.concatenate([sparse_points[:WIDE], parts.astype(BF16)], axis=0)

    sent = descriptors.reshape(mine, peers, LANES).transpose(1, 0, 2)
    got = lax.all_to_all(sent, "cols", split_axis=0, concat_axis=0, tiled=True)

    packed = called(
        functools.partial(pack_kernel, owners=owners),
        jax.ShapeDtypeStruct((owners * GROUP, LANES), BF16),
        got,
        env_owner.reshape(1, envs),
        env_structure.reshape(1, envs),
    )
    col = lax.axis_index("cols")
    near = jnp.where(col == 0, panel, lax.ppermute(panel, "cols", [(0, 1)]))
    for chip in range(1, peers // 2):
        reached = lax.ppermute(near, "cols", [(0, 2 * chip), (1, 2 * chip + 1)])
        panel = near + reached if chip == 1 else panel + reached
    arrived = lax.all_to_all(packed, "rows", split_axis=0, concat_axis=0, tiled=True)
    arrived, panel = lax.optimization_barrier((arrived, panel))
    slots = owners * SLOTS
    slot_rows, labels = called(
        unpack_kernel,
        (
            jax.ShapeDtypeStruct((peers // 2, slots, LANES), BF16),
            jax.ShapeDtypeStruct((slots, 1), F32),
        ),
        arrived,
    )
    own = lax.all_to_all(
        slot_rows,
        "cols",
        split_axis=0,
        concat_axis=0,
        tiled=True,
        axis_index_groups=[list(range(0, peers, 2)), list(range(1, peers, 2))],
    )
    other = lax.ppermute(own, "cols", [(c, c ^ 1) for c in range(peers)])

    vmem, smem = pl.BlockSpec(memory_space=pltpu.VMEM), pl.BlockSpec(memory_space=pltpu.SMEM)
    params = pltpu.CompilerParams(vmem_limit_bytes=VMEM_LIMIT)
    own_rows = cols // LANES * WIDE // Y
    matrix, sums = pl.pallas_call(
        equations_kernel,
        out_shape=(
            jax.ShapeDtypeStruct((eqs, cols + WIDE), F32),
            jax.ShapeDtypeStruct((Y, own_rows + 2 * WIDE, LANES), BF16),
        ),
        in_specs=[smem] + [vmem] * 7,
        out_specs=(vmem, vmem),
        scratch_shapes=[pltpu.VMEM((slots, peers * LANES), BF16)],
        compiler_params=params,
    )(
        (col % 2).reshape(1),
        own,
        other,
        labels,
        sparse_points,
        point_scale.reshape(1, cols),
        panel,
        row_weight.reshape(eqs, 1),
    )
    def exchanged(array, groups):
        return lax.all_to_all(
            array, "rows", split_axis=0, concat_axis=0, tiled=True, axis_index_groups=groups
        )

    own = own_rows // Z
    length = own + WIDE // Z
    message = jax.ShapeDtypeStruct((Z, length, LANES), F32)
    summed = called(near_kernel, message, exchanged(sums, y_groups))
    summed = called(far_kernel, message, exchanged(summed, z_groups))
    column = exchanged(summed, z_groups)
    total = to_each(column[:, :own], "rows", y_groups)
    total = total.reshape(owners, own, LANES)

    square = jax.ShapeDtypeStruct((WIDE, WIDE), F32)
    terms, turn, upper = pl.pallas_call(
        factor_kernel,
        out_shape=(square, square, square),
        in_specs=[vmem, smem],
        out_specs=(vmem, vmem, vmem),
        compiler_params=params,
        cost_estimate=pl.CostEstimate(flops=8_000_000_000, bytes_accessed=262144, transcendentals=0),
    )(column, ridge_factor)
    return pl.pallas_call(
        functools.partial(final_kernel, norm_scale=1.0 / math.sqrt(owners * eqs)),
        out_shape=(
            jax.ShapeDtypeStruct((WIDE, cols), F32),
            jax.ShapeDtypeStruct((eqs, cols), F32),
        ),
        in_specs=[smem] + [vmem] * 5,
        out_specs=(vmem, vmem),
        compiler_params=params,
    )(col.reshape(1), total, terms, turn, upper, matrix)


def solution(mesh):
    return jax.shard_map(
        body,
        mesh=mesh,
        in_specs=(
            P(("rows", "cols"), None),
            P("cols", None),
            P("cols"),
            P("rows", None),
            P("rows"),
            P("rows"),
            P(),
        ),
        out_specs=(P(None, "cols"), P("rows", "cols")),
        check_vma=False,
    )
```

time: 162 us -> 142 us (0.88)
  blocking collectives: 64.8 us -> 42.8 us
  starting transfers between devices: 25.6 us -> 41.8 us
  Pallas kernels: 22.6 us -> 15 us
  waiting for transfers between devices: 40.3 us -> 32.8 us
    all_to_all x2 -> x1, waiting for transfers between devices: 24.7 us -> 2.3 us  [to_each(): lax.all_to_all(copies, axis, split_axis=0, concat_axis=0, tiled=True, axi...]
    all_to_all x3, blocking collectives: 64.8 us -> 42.8 us  [the longest x2 33.1 us: exchanged(): lax.all_to_all(array, 'rows', split_axis=0, concat_axis=0, tiled=True, ax...]
    all_to_all x0 -> x2, waiting for transfers between devices: none -> 14.8 us  [the longest x1 14.8 us: exchanged(): lax.all_to_all(array, 'rows', split_axis=0, concat_axis=0, tiled=True, ax...]
    ppermute x0 -> x5, starting transfers between devices: none -> 11.8 us  [the longest x3 8.04 us: body(): reached = lax.ppermute(near, 'cols', [(0, 2 * chip), (1, 2 * chip + 1)])]
    pallas_call x1 -> x2, Pallas kernels: 17.1 us -> 8.23 us  [the longest x1 5.75 us: body(): pl.pallas_call(factor_kernel, out_shape=(square, square, square), in_spec...]
    all_to_all x0 -> x2, starting transfers between devices: none -> 8.06 us  [the longest x1 4.71 us: exchanged(): lax.all_to_all(array, 'rows', split_axis=0, concat_axis=0, tiled=True, ax...]
    all_to_all x2 -> x1, starting transfers between devices: 7.23 us -> 3.47 us  [to_each(): lax.all_to_all(copies, axis, split_axis=0, concat_axis=0, tiled=True, axi...]
  transfers between devices with their start and end apart: 3 -> 9, of which waited for: 3 -> 4; matrix products, arithmetic and copies ran while one was open for 0% -> 2% of each run, Pallas kernels for 0% -> 5%
where the time goes in v2:
time: 142 us; the launch traced here: 141 us
  blocking collectives  42.8 us (30%)
  starting transfers between devices  41.8 us (29%)
  waiting for transfers between devices  32.8 us (23%)
  Pallas kernels  15 us (11%)
  local copies, waits for them, and re-layouts  5.56 us (4%)
  other arithmetic  1.89 us (1%)
  between operations  1.51 us (1%)
    all_to_all x2, blocking collectives, exchanged(): lax.all_to_all(array, 'rows', split_axis=0, concat_axis=0, tiled=True, ax...  33.1 us
    all_to_all x1, starting transfers between devices, body(): lax.all_to_all(packed, 'rows', split_axis=0, concat_axis=0, tiled=True)  18.4 us
    all_to_all x1, waiting for transfers between devices, exchanged(): lax.all_to_all(array, 'rows', split_axis=0, concat_axis=0, tiled=True, ax...  14.8 us
    all_to_all x1, waiting for transfers between devices, body(): lax.all_to_all(packed, 'rows', split_axis=0, concat_axis=0, tiled=True)  14.7 us
    all_to_all x1, blocking collectives, body(): lax.all_to_all(slot_rows, 'cols', split_axis=0, concat_axis=0, tiled=True...  9.76 us
    ppermute x3, starting transfers between devices, body(): reached = lax.ppermute(near, 'cols', [(0, 2 * chip), (1, 2 * chip + 1)])  8.04 us
    pallas_call x1, Pallas kernels, body(): pl.pallas_call(factor_kernel, out_shape=(square, square, square), in_spec...  5.75 us
    all_to_all x1, starting transfers between devices, exchanged(): lax.all_to_all(array, 'rows', split_axis=0, concat_axis=0, tiled=True, ax...  4.71 us
  transfers between devices with their start and end apart: 9, of which 4 were waited for; matrix products, arithmetic and copies ran while one was open for 2% of the time, Pallas kernels for 5%

profile of v2, /device:TPU:32, one launch (start us, length us, event | category | flops | bytes accessed | tf_op | source)
XLA Modules:
  0.0 141.2 jit_solution(12606181378888807398)
XLA Ops:
  1.4 1.0 slice.9
  2.4 1.9 %collective-permute-start = (bf16[144,1024]{1,0:T(8,128)(2,1)S(1)}, bf16[144,1024]{1,0:T(8,128)(2,1)S(1)}, u32[]{:S(2)}, u32[]{:S(2)}) collective-permute-start(bf16[144,1024]{1,0:T(8,128)(2,1)S(1)} %pad_maximum_fusion), channel_id=1, source_target_pairs={{0,1},{8,9},{16,17},{24,25},{32,33},{40,41},{48,49},{56,57},{64,65... | collective-permute-start | bytes 884744 | tf_op jit(solution)/shard_map/ppermute | solution.py:282
  5.0 3.4 %all-to-all-start = ((bf16[8,32,128]{2,1,0:T(8,128)(2,1)}), bf16[8,32,128]{2,1,0:T(8,128)(2,1)S(1)}, u32[]{:S(2)}, u32[]{:S(2)}) async-start(bf16[8,32,128]{2,1,0:T(8,128)(2,1)} %bitcast_bitcast_fusion), calls=%async_computation | async-start | bytes 131072 | tf_op jit(solution)/shard_map/all_to_all | solution.py:272
  8.5 3.8 %collective-permute-start.1 = (bf16[144,1024]{1,0:T(8,128)(2,1)S(1)}, bf16[144,1024]{1,0:T(8,128)(2,1)S(1)}, u32[]{:S(2)}, u32[]{:S(2)}) collective-permute-start(bf16[144,1024]{1,0:T(8,128)(2,1)S(1)} %broadcast_select_fusion), channel_id=1, source_target_pairs={{0,2},{1,3},{8,10},{9,11},{16,18},{17,19},{24,26},{25,27},{32,34},... | collective-permute-start | bytes 884744 | tf_op jit(solution)/shard_map/ppermute | solution.py:284
  12.3 2.2 %collective-permute-start.2 = (bf16[144,1024]{1,0:T(8,128)(2,1)S(1)}, bf16[144,1024]{1,0:T(8,128)(2,1)S(1)}, u32[]{:S(2)}, u32[]{:S(2)}) collective-permute-start(bf16[144,1024]{1,0:T(8,128)(2,1)S(1)} %broadcast_select_fusion), channel_id=1, source_target_pairs={{0,4},{1,5},{8,12},{9,13},{16,20},{17,21},{24,28},{25,29},{32,36},... | collective-permute-start | bytes 884744 | tf_op jit(solution)/shard_map/ppermute | solution.py:284
  14.5 2.0 %collective-permute-start.3 = (bf16[144,1024]{1,0:T(8,128)(2,1)S(1)}, bf16[144,1024]{1,0:T(8,128)(2,1)}, u32[]{:S(2)}, u32[]{:S(2)}) collective-permute-start(bf16[144,1024]{1,0:T(8,128)(2,1)S(1)} %broadcast_select_fusion), channel_id=1, source_target_pairs={{0,6},{1,7},{8,14},{9,15},{16,22},{17,23},{24,30},{25,31},{32,38},... | collective-permute-start | bytes 884744 | tf_op jit(solution)/shard_map/ppermute | solution.py:284
  16.5 1.2 shard_map.86
  17.7 18.4 %all-to-all-start.1 = ((bf16[64,8,128]{2,1,0:T(8,128)(2,1)}), bf16[64,8,128]{2,1,0:T(8,128)(2,1)S(1)}, u32[]{:S(2)}, u32[]{:S(2)}) async-start(bf16[64,8,128]{2,1,0:T(8,128)(2,1)} %bitcast.5), calls=%async_computation.1 | async-start | bytes 262144 | tf_op jit(solution)/shard_map/all_to_all | solution.py:286
  36.2 1.1 add_add_fusion.panel_ref
  37.2 14.7 %all-to-all-done.1 = bf16[64,8,128]{2,1,0:T(8,128)(2,1)S(1)} async-done(((bf16[64,8,128]{2,1,0:T(8,128)(2,1)}), bf16[64,8,128]{2,1,0:T(8,128)(2,1)S(1)}, u32[]{:S(2)}, u32[]{:S(2)}) %all-to-all-start.1) | async-done | bytes 131104 | tf_op jit(solution)/shard_map/all_to_all | solution.py:286
  53.1 9.8 %all_to_all.42.own_ref = bf16[4,384,128]{2,1,0:T(8,128)(2,1)S(1)} all-to-all(bf16[4,384,128]{2,1,0:T(8,128)(2,1)S(1)} %get-tuple-element.12), channel_id=1, replica_groups={{0,2,4,6},{1,3,5,7},{8,10,12,14},{9,11,13,15},{16,18,20,22},{17,19,21,2..., dimensions={0} | all-to-all | bytes 786432 | tf_op jit(solution)/shard_map/all_to_all | solution.py:297
  62.8 1.9 %collective-permute-start.4 = (bf16[4,384,128]{2,1,0:T(8,128)(2,1)S(1)}, bf16[4,384,128]{2,1,0:T(8,128)(2,1)S(1)}, u32[]{:S(2)}, u32[]{:S(2)}) collective-permute-start(bf16[4,384,128]{2,1,0:T(8,128)(2,1)S(1)} %all_to_all.42.own_ref), channel_id=1, source_target_pairs={{0,1},{1,0},{2,3},{3,2},{4,5},{5,4},{6,7},{7,6},{8,9},{9,8},{10,11... | collective-permute-start | bytes 1179656 | tf_op jit(solution)/shard_map/ppermute | solution.py:305
  65.5 1.0 collective-permute-done.4.other_ref
  66.4 0.9 copy-done.3
  68.1 4.3 %shard_map.88 = (f32[64,1152]{1,0:T(8,128)S(1)}, bf16[4,512,128]{2,1,0:T(8,128)(2,1)S(1)}) custom-call(s32[1]{0:T(128)} %bitcast.1.core_ref, bf16[4,384,128]{2,1,0:T(8,128)(2,1)S(1)} %all_to_all.42.own_ref, bf16[4,384,128]{2,1,0:T(8,128)(2,1)S(1)} %collective-permute-done.4.other_ref, f32[384,1]{1,0:T(8,128)S(1)} %copy-done.3, ...), custom_call_target="tpu_custom_call" | custom-call | tf_op jit(solution)/shard_map/pallas_call | solution.py:310
  72.4 13.1 %all_to_all.43.got_ref = bf16[4,512,128]{2,1,0:T(8,128)(2,1)S(1)} all-to-all(bf16[4,512,128]{2,1,0:T(8,128)(2,1)S(1)} %get-tuple-element.15), channel_id=1, replica_groups={{0,128,256,384},{8,136,264,392},{16,144,272,400},{24,152,280,408},{32,1..., dimensions={0} | all-to-all | bytes 1048576 | tf_op jit(solution)/shard_map/all_to_all | solution.py:331
  85.6 20.0 %all_to_all.44.got_ref = f32[16,24,128]{2,1,0:T(8,128)S(1)} all-to-all(f32[16,24,128]{2,1,0:T(8,128)S(1)} %shard_map.89), channel_id=1, replica_groups={{0,8,16,24,32,40,48,56,64,72,80,88,96,104,112,120},{128,136,144,152,160..., dimensions={0} | all-to-all | bytes 393216 | tf_op jit(solution)/shard_map/all_to_all | solution.py:331
  106.2 4.7 %all-to-all-start.5 = ((f32[16,24,128]{2,1,0:T(8,128)}), f32[16,24,128]{2,1,0:T(8,128)S(1)}, u32[]{:S(2)}, u32[]{:S(2)}) async-start(f32[16,24,128]{2,1,0:T(8,128)} %shard_map.90), calls=%async_computation.5 | async-start | bytes 393216 | tf_op jit(solution)/shard_map/all_to_all | solution.py:331
  111.6 14.8 %all-to-all-done.5.gram_ref = f32[16,24,128]{2,1,0:T(8,128)S(1)} async-done(((f32[16,24,128]{2,1,0:T(8,128)}), f32[16,24,128]{2,1,0:T(8,128)S(1)}, u32[]{:S(2)}, u32[]{:S(2)}) %all-to-all-start.5) | async-done | bytes 196640 | tf_op jit(solution)/shard_map/all_to_all | solution.py:331
  126.4 0.8 broadcast_in_dim.3
  127.2 3.5 %all-to-all-start.6 = ((f32[4,16,16,128]{3,2,1,0:T(8,128)}), f32[4,16,16,128]{3,2,1,0:T(8,128)S(1)}, u32[]{:S(2)}, u32[]{:S(2)}) async-start(f32[4,16,16,128]{3,2,1,0:T(8,128)} %broadcast_in_dim.3), calls=%async_computation.6 | async-start | bytes 1048576 | tf_op jit(solution)/shard_map/all_to_all | solution.py:51
  130.7 5.7 %shard_map.91 = (f32[128,128]{1,0:T(8,128)S(1)}, f32[128,128]{1,0:T(8,128)S(1)}, f32[128,128]{1,0:T(8,128)S(1)}) custom-call(f32[16,24,128]{2,1,0:T(8,128)S(1)} %all-to-all-done.5.gram_ref, f32[1]{0:T(128)S(6)} %copy.14.ridge_ref), custom_call_target="tpu_custom_call" | custom-call | flops 8000000000 | bytes 262144 | tf_op jit(solution)/shard_map/pallas_call | solution.py:345
  136.5 2.3 %all-to-all-done.6 = f32[4,16,16,128]{3,2,1,0:T(8,128)S(1)} async-done(((f32[4,16,16,128]{3,2,1,0:T(8,128)}), f32[4,16,16,128]{3,2,1,0:T(8,128)S(1)}, u32[]{:S(2)}, u32[]{:S(2)}) %all-to-all-start.6) | async-done | bytes 524320 | tf_op jit(solution)/shard_map/all_to_all | solution.py:51
  138.8 2.5 %shard_map.92 = (f32[128,1024]{1,0:T(8,128)}, f32[64,1024]{1,0:T(8,128)}) custom-call(s32[1]{0:T(128)} %bitcast.first_ref, f32[64,16,128]{2,1,0:T(8,128)S(1)} %bitcast.22, f32[128,128]{1,0:T(8,128)S(1)} %get-tuple-element.16.terms_ref, f32[128,128]{1,0:T(8,128)S(1)} %get-tuple-element.17.turn_ref, f32[128,128]{1,0:T(8,128)S(1)} %get-tuple-element.18.upper_ref, ...), custom_call_target="tpu_custom_call" | custom-call | tf_op jit(solution)/shard_map/pallas_call | solution.py:353
  (32 shorter events, 4.9 us)
Async XLA Ops:
  0.6 3.7 %copy-start = (bf16[32,1024]{1,0:T(8,128)(2,1)S(1)}, bf16[32,1024]{1,0:T(8,128)(2,1)}, u32[]{:S(2)}) copy-start(bf16[32,1024]{1,0:T(8,128)(2,1)} %param.7) | copy-start | bytes 196612
  0.6 15.9 %copy-start.6 = (s32[256,1]{0,1:T(1,128)S(1)}, s32[256,1]{0,1:T(1,128)}, u32[]{:S(2)}) copy-start(s32[256,1]{0,1:T(1,128)} %param.10) | copy-start | bytes 3076
  0.7 15.9 %copy-start.7 = (s32[256]{0:T(256)S(1)}, s32[256]{0:T(256)}, u32[]{:S(2)}) copy-start(s32[256]{0:T(256)} %param.11) | copy-start | bytes 3076
  2.4 62.3 %copy-start.8 = (f32[64]{0:T(128)S(1)}, f32[64]{0:T(128)}, u32[]{:S(2)}) copy-start(f32[64]{0:T(128)} %param.12) | copy-start | bytes 772
  2.4 64.0 %copy-start.1 = (bf16[1024,1024]{1,0:T(8,128)(2,1)S(1)}, bf16[1024,1024]{1,0:T(8,128)(2,1)}, u32[]{:S(2)}) copy-start(bf16[1024,1024]{1,0:T(8,128)(2,1)} %points_ref.1) | copy-start | bytes 6291460
  2.4 64.0 %copy-start.5 = (f32[1024]{0:T(1024)S(1)}, f32[1024]{0:T(1024)}, u32[]{:S(2)}) copy-start(f32[1024]{0:T(1024)} %param.9) | copy-start | bytes 12292
  2.4 5.9 %collective-permute-start = (bf16[144,1024]{1,0:T(8,128)(2,1)S(1)}, bf16[144,1024]{1,0:T(8,128)(2,1)S(1)}, u32[]{:S(2)}, u32[]{:S(2)}) collective-permute-start(bf16[144,1024]{1,0:T(8,128)(2,1)S(1)} %pad_maximum_fusion), channel_id=1, source_target_pairs={{0,1},{8,9},{16,17},{24,25},{32,33},{40,41},{48,49},{56,57},{64,65... | collective-permute-start | bytes 884744 | tf_op jit(solution)/shard_map/ppermute | solution.py:282
  5.0 11.5 %all-to-all-start = ((bf16[8,32,128]{2,1,0:T(8,128)(2,1)}), bf16[8,32,128]{2,1,0:T(8,128)(2,1)S(1)}, u32[]{:S(2)}, u32[]{:S(2)}) async-start(bf16[8,32,128]{2,1,0:T(8,128)(2,1)} %bitcast_bitcast_fusion), calls=%async_computation | async-start | bytes 131072 | tf_op jit(solution)/shard_map/all_to_all | solution.py:272
  8.5 27.7 %collective-permute-start.1 = (bf16[144,1024]{1,0:T(8,128)(2,1)S(1)}, bf16[144,1024]{1,0:T(8,128)(2,1)S(1)}, u32[]{:S(2)}, u32[]{:S(2)}) collective-permute-start(bf16[144,1024]{1,0:T(8,128)(2,1)S(1)} %broadcast_select_fusion), channel_id=1, source_target_pairs={{0,2},{1,3},{8,10},{9,11},{16,18},{17,19},{24,26},{25,27},{32,34},... | collective-permute-start | bytes 884744 | tf_op jit(solution)/shard_map/ppermute | solution.py:284
  12.3 23.9 %collective-permute-start.2 = (bf16[144,1024]{1,0:T(8,128)(2,1)S(1)}, bf16[144,1024]{1,0:T(8,128)(2,1)S(1)}, u32[]{:S(2)}, u32[]{:S(2)}) collective-permute-start(bf16[144,1024]{1,0:T(8,128)(2,1)S(1)} %broadcast_select_fusion), channel_id=1, source_target_pairs={{0,4},{1,5},{8,12},{9,13},{16,20},{17,21},{24,28},{25,29},{32,36},... | collective-permute-start | bytes 884744 | tf_op jit(solution)/shard_map/ppermute | solution.py:284
  14.5 21.7 %collective-permute-start.3 = (bf16[144,1024]{1,0:T(8,128)(2,1)S(1)}, bf16[144,1024]{1,0:T(8,128)(2,1)}, u32[]{:S(2)}, u32[]{:S(2)}) collective-permute-start(bf16[144,1024]{1,0:T(8,128)(2,1)S(1)} %broadcast_select_fusion), channel_id=1, source_target_pairs={{0,6},{1,7},{8,14},{9,15},{16,22},{17,23},{24,30},{25,31},{32,38},... | collective-permute-start | bytes 884744 | tf_op jit(solution)/shard_map/ppermute | solution.py:284
  17.7 34.2 %all-to-all-start.1 = ((bf16[64,8,128]{2,1,0:T(8,128)(2,1)}), bf16[64,8,128]{2,1,0:T(8,128)(2,1)S(1)}, u32[]{:S(2)}, u32[]{:S(2)}) async-start(bf16[64,8,128]{2,1,0:T(8,128)(2,1)} %bitcast.5), calls=%async_computation.1 | async-start | bytes 262144 | tf_op jit(solution)/shard_map/all_to_all | solution.py:286
  52.4 0.7 copy-start.2
  62.8 3.6 %collective-permute-start.4 = (bf16[4,384,128]{2,1,0:T(8,128)(2,1)S(1)}, bf16[4,384,128]{2,1,0:T(8,128)(2,1)S(1)}, u32[]{:S(2)}, u32[]{:S(2)}) collective-permute-start(bf16[4,384,128]{2,1,0:T(8,128)(2,1)S(1)} %all_to_all.42.own_ref), channel_id=1, source_target_pairs={{0,1},{1,0},{2,3},{3,2},{4,5},{5,4},{6,7},{7,6},{8,9},{9,8},{10,11... | collective-permute-start | bytes 1179656 | tf_op jit(solution)/shard_map/ppermute | solution.py:305
  66.4 0.9 copy-start.3
  67.4 0.8 copy-start.4
  106.2 20.1 %all-to-all-start.5 = ((f32[16,24,128]{2,1,0:T(8,128)}), f32[16,24,128]{2,1,0:T(8,128)S(1)}, u32[]{:S(2)}, u32[]{:S(2)}) async-start(f32[16,24,128]{2,1,0:T(8,128)} %shard_map.90), calls=%async_computation.5 | async-start | bytes 393216 | tf_op jit(solution)/shard_map/all_to_all | solution.py:331
  127.2 11.5 %all-to-all-start.6 = ((f32[4,16,16,128]{3,2,1,0:T(8,128)}), f32[4,16,16,128]{3,2,1,0:T(8,128)S(1)}, u32[]{:S(2)}, u32[]{:S(2)}) async-start(f32[4,16,16,128]{3,2,1,0:T(8,128)} %broadcast_in_dim.3), calls=%async_computation.6 | async-start | bytes 1048576 | tf_op jit(solution)/shard_map/all_to_all | solution.py:51

commit v3 on v2

--- a/solution.py
+++ b/solution.py
@@ -20,7 +20,7 @@
 Y, Z = 4, 16
 F32, BF16 = jnp.float32, jnp.bfloat16
 HIGHEST = lax.Precision.HIGHEST
-VMEM_LIMIT = 48 * 2**20
+VMEM_LIMIT = 20 * 2**20
 
 
 def dot(a, b, dims=((1,), (0,)), precision=None):
@@ -83,9 +83,8 @@
     data = dot(one_hot(row == source * GROUP + place), got).astype(BF16)
     for copy in range(out_ref.shape[0]):
         out_ref[copy] = data
-    named = dot(one_hot(row == source * GROUP + SLOTS), got)
-    own = iota((slots, LANES), 1) == iota((slots, LANES), 0) % SLOTS
-    label_ref[...] = jnp.sum(jnp.where(own, named, 0.0), axis=1, keepdims=True)
+    source, row = iota((sources, rows), 0), iota((sources, rows), 1)
+    label_ref[...] = dot(one_hot(row == source * GROUP + SLOTS), got).astype(BF16)
 
 
 def equations_kernel(
@@ -102,7 +101,7 @@
     env_ref,
 ):
     chips, slots, _ = own_ref.shape
-    eqs = weight_ref.shape[0]
+    eqs = weight_ref.shape[1]
     cols = points_ref.shape[0]
     core = core_ref[0]
     for chip in range(chips):
@@ -111,8 +110,14 @@
         at = pl.multiple_of((2 * chip + 1 - core) * LANES, LANES)
         env_ref[:, pl.ds(at, LANES)] = other_ref[chip]
     dot_scale = env_ref.shape[1] ** (-0.5)
-    chosen = one_hot(label_ref[...].astype(jnp.int32) == iota((slots, eqs), 1))
-    weight = weight_ref[...]
+    sources = label_ref.shape[0]
+    source = one_hot(iota((slots, sources), 0) // SLOTS == iota((slots, sources), 1))
+    named = dot(source, label_ref[...])
+    mine = iota((slots, LANES), 1) == iota((slots, LANES), 0) % SLOTS
+    label = jnp.sum(jnp.where(mine, named, 0.0), axis=1, keepdims=True)
+    chosen = one_hot(label.astype(jnp.int32) == iota((slots, eqs), 1))
+    diagonal = jnp.where(iota((eqs, eqs), 0) == iota((eqs, eqs), 1), weight_ref[...], 0.0)
+    weight = jnp.sum(diagonal, axis=1, keepdims=True)
 
     def block(points, scale):
         z = dot(env_ref[...], points, ((1,), (1,))) * dot_scale
@@ -278,22 +283,23 @@
         env_owner.reshape(1, envs),
         env_structure.reshape(1, envs),
     )
+    packed, panel = lax.optimization_barrier((packed, panel))
     col = lax.axis_index("cols")
     near = jnp.where(col == 0, panel, lax.ppermute(panel, "cols", [(0, 1)]))
     for chip in range(1, peers // 2):
         reached = lax.ppermute(near, "cols", [(0, 2 * chip), (1, 2 * chip + 1)])
         panel = near + reached if chip == 1 else panel + reached
     arrived = lax.all_to_all(packed, "rows", split_axis=0, concat_axis=0, tiled=True)
-    arrived, panel = lax.optimization_barrier((arrived, panel))
     slots = owners * SLOTS
     slot_rows, labels = called(
         unpack_kernel,
         (
             jax.ShapeDtypeStruct((peers // 2, slots, LANES), BF16),
-            jax.ShapeDtypeStruct((slots, 1), F32),
+            jax.ShapeDtypeStruct((owners, LANES), BF16),
         ),
         arrived,
     )
+    slot_rows, panel = lax.optimization_barrier((slot_rows, panel))
     own = lax.all_to_all(
         slot_rows,
         "cols",
@@ -325,7 +331,7 @@
         sparse_points,
         point_scale.reshape(1, cols),
         panel,
-        row_weight.reshape(eqs, 1),
+        row_weight.reshape(1, eqs),
     )
     def exchanged(array, groups):
         return lax.all_to_all(

time: 142 us -> 149 us (1.049)
  blocking collectives: 42.8 us -> 51.4 us
  starting transfers between devices: 41.8 us -> 39.3 us
    all_to_all x2, blocking collectives: 33.1 us -> 41.3 us  [exchanged(): lax.all_to_all(array, 'rows', split_axis=0, concat_axis=0, tiled=True, ax...]
    all_to_all x1, waiting for transfers between devices: 14.7 us -> 10.5 us  [body(): lax.all_to_all(packed, 'rows', split_axis=0, concat_axis=0, tiled=True)]
    all_to_all x1, waiting for transfers between devices: 0.01 us -> 3.9 us  [body(): got = lax.all_to_all(sent, 'cols', split_axis=0, concat_axis=0, tiled=True)]
    ppermute x3, starting transfers between devices: 8.04 us -> 4.84 us  [body(): reached = lax.ppermute(near, 'cols', [(0, 2 * chip), (1, 2 * chip + 1)])]
    unnamed x18 -> x12, local copies, waits for them, and re-layouts: 2.4 us -> 3.54 us
  transfers between devices with their start and end apart: 9 -> 9, of which waited for: 4 -> 5; matrix products, arithmetic and copies ran while one was open for 2% -> 1% of each run, Pallas kernels for 5% -> 4%
where the time goes in v3:
time: 149 us; the launch traced here: 148 us
  blocking collectives  51.4 us (34%)
  starting transfers between devices  39.3 us (26%)
  waiting for transfers between devices  33.2 us (22%)
  Pallas kernels  14.8 us (10%)
  local copies, waits for them, and re-layouts  5.99 us (4%)
  other arithmetic  1.78 us (1%)
    all_to_all x2, blocking collectives, exchanged(): lax.all_to_all(array, 'rows', split_axis=0, concat_axis=0, tiled=True, ax...  41.3 us
    all_to_all x1, starting transfers between devices, body(): lax.all_to_all(packed, 'rows', split_axis=0, concat_axis=0, tiled=True)  18.4 us
    all_to_all x1, waiting for transfers between devices, exchanged(): lax.all_to_all(array, 'rows', split_axis=0, concat_axis=0, tiled=True, ax...  14.8 us
    all_to_all x1, waiting for transfers between devices, body(): lax.all_to_all(packed, 'rows', split_axis=0, concat_axis=0, tiled=True)  10.5 us
    all_to_all x1, blocking collectives, body(): lax.all_to_all(slot_rows, 'cols', split_axis=0, concat_axis=0, tiled=True...  10.2 us
    pallas_call x1, Pallas kernels, body(): pl.pallas_call(factor_kernel, out_shape=(square, square, square), in_spec...  5.75 us
    ppermute x3, starting transfers between devices, body(): reached = lax.ppermute(near, 'cols', [(0, 2 * chip), (1, 2 * chip + 1)])  4.84 us
    all_to_all x1, starting transfers between devices, exchanged(): lax.all_to_all(array, 'rows', split_axis=0, concat_axis=0, tiled=True, ax...  4.71 us
  transfers between devices with their start and end apart: 9, of which 5 were waited for; matrix products, arithmetic and copies ran while one was open for 1% of the time, Pallas kernels for 4%

profile of v3, /device:TPU:32, one launch (start us, length us, event | category | flops | bytes accessed | tf_op | source)
XLA Modules:
  0.0 147.9 jit_solution(6039370548260687406)
XLA Ops:
  2.1 4.3 %all-to-all-start = ((bf16[8,32,128]{2,1,0:T(8,128)(2,1)}), bf16[8,32,128]{2,1,0:T(8,128)(2,1)S(1)}, u32[]{:S(2)}, u32[]{:S(2)}) async-start(bf16[8,32,128]{2,1,0:T(8,128)(2,1)} %bitcast_bitcast_fusion), calls=%async_computation | async-start | bytes 131072 | tf_op jit(solution)/shard_map/all_to_all | solution.py:277
  7.1 1.0 slice.9
  8.1 3.9 %all-to-all-done.env_ref = bf16[8,32,128]{2,1,0:T(8,128)(2,1)S(1)} async-done(((bf16[8,32,128]{2,1,0:T(8,128)(2,1)}), bf16[8,32,128]{2,1,0:T(8,128)(2,1)S(1)}, u32[]{:S(2)}, u32[]{:S(2)}) %all-to-all-start) | async-done | bytes 65568 | tf_op jit(solution)/shard_map/all_to_all | solution.py:277
  13.4 1.2 shard_map.86
  14.6 1.6 %collective-permute-start = (bf16[144,1024]{1,0:T(8,128)(2,1)S(1)}, bf16[144,1024]{1,0:T(8,128)(2,1)S(1)}, u32[]{:S(2)}, u32[]{:S(2)}) collective-permute-start(bf16[144,1024]{1,0:T(8,128)(2,1)S(1)} %pad_maximum_fusion), channel_id=1, source_target_pairs={{0,1},{8,9},{16,17},{24,25},{32,33},{40,41},{48,49},{56,57},{64,65... | collective-permute-start | bytes 884744 | tf_op jit(solution)/shard_map/ppermute | solution.py:288
  16.3 18.4 %all-to-all-start.1 = ((bf16[64,8,128]{2,1,0:T(8,128)(2,1)}), bf16[64,8,128]{2,1,0:T(8,128)(2,1)S(1)}, u32[]{:S(2)}, u32[]{:S(2)}) async-start(bf16[64,8,128]{2,1,0:T(8,128)(2,1)} %bitcast.8), calls=%async_computation.1 | async-start | bytes 262144 | tf_op jit(solution)/shard_map/all_to_all | solution.py:292
  34.7 1.5 %collective-permute-start.1 = (bf16[144,1024]{1,0:T(8,128)(2,1)S(1)}, bf16[144,1024]{1,0:T(8,128)(2,1)S(1)}, u32[]{:S(2)}, u32[]{:S(2)}) collective-permute-start(bf16[144,1024]{1,0:T(8,128)(2,1)S(1)} %broadcast_select_fusion), channel_id=1, source_target_pairs={{0,2},{1,3},{8,10},{9,11},{16,18},{17,19},{24,26},{25,27},{32,34},... | collective-permute-start | bytes 884744 | tf_op jit(solution)/shard_map/ppermute | solution.py:290
  36.3 1.3 collective-permute-start.2
  37.6 2.0 %collective-permute-start.3 = (bf16[144,1024]{1,0:T(8,128)(2,1)S(1)}, bf16[144,1024]{1,0:T(8,128)(2,1)}, u32[]{:S(2)}, u32[]{:S(2)}) collective-permute-start(bf16[144,1024]{1,0:T(8,128)(2,1)S(1)} %broadcast_select_fusion), channel_id=1, source_target_pairs={{0,6},{1,7},{8,14},{9,15},{16,22},{17,23},{24,30},{25,31},{32,38},... | collective-permute-start | bytes 884744 | tf_op jit(solution)/shard_map/ppermute | solution.py:290
  39.6 10.5 %all-to-all-done.1 = bf16[64,8,128]{2,1,0:T(8,128)(2,1)S(1)} async-done(((bf16[64,8,128]{2,1,0:T(8,128)(2,1)}), bf16[64,8,128]{2,1,0:T(8,128)(2,1)S(1)}, u32[]{:S(2)}, u32[]{:S(2)}) %all-to-all-start.1) | async-done | bytes 131104 | tf_op jit(solution)/shard_map/all_to_all | solution.py:292
  50.4 1.0 add_add_fusion.panel_ref
  51.5 10.2 %all_to_all.41.own_ref = bf16[4,384,128]{2,1,0:T(8,128)(2,1)S(1)} all-to-all(bf16[4,384,128]{2,1,0:T(8,128)(2,1)S(1)} %get-tuple-element.16), channel_id=1, replica_groups={{0,2,4,6},{1,3,5,7},{8,10,12,14},{9,11,13,15},{16,18,20,22},{17,19,21,2..., dimensions={0} | all-to-all | bytes 786432 | tf_op jit(solution)/shard_map/all_to_all | solution.py:303
  61.6 1.9 %collective-permute-start.4 = (bf16[4,384,128]{2,1,0:T(8,128)(2,1)S(1)}, bf16[4,384,128]{2,1,0:T(8,128)(2,1)S(1)}, u32[]{:S(2)}, u32[]{:S(2)}) collective-permute-start(bf16[4,384,128]{2,1,0:T(8,128)(2,1)S(1)} %all_to_all.41.own_ref), channel_id=1, source_target_pairs={{0,1},{1,0},{2,3},{3,2},{4,5},{5,4},{6,7},{7,6},{8,9},{9,8},{10,11... | collective-permute-start | bytes 1179656 | tf_op jit(solution)/shard_map/ppermute | solution.py:311
  63.5 1.7 %collective-permute-done.4.other_ref = bf16[4,384,128]{2,1,0:T(8,128)(2,1)S(1)} collective-permute-done((bf16[4,384,128]{2,1,0:T(8,128)(2,1)S(1)}, bf16[4,384,128]{2,1,0:T(8,128)(2,1)S(1)}, u32[]{:S(2)}, u32[]{:S(2)}) %collective-permute-start.4) | collective-permute-done | bytes 393248 | tf_op jit(solution)/shard_map/ppermute | solution.py:311
  66.6 4.3 %shard_map.88 = (f32[64,1152]{1,0:T(8,128)S(1)}, bf16[4,512,128]{2,1,0:T(8,128)(2,1)S(1)}) custom-call(s32[1]{0:T(128)} %bitcast.1.core_ref, bf16[4,384,128]{2,1,0:T(8,128)(2,1)S(1)} %all_to_all.41.own_ref, bf16[4,384,128]{2,1,0:T(8,128)(2,1)S(1)} %collective-permute-done.4.other_ref, bf16[64,128]{1,0:T(8,128)(2,1)S(1)} %get-tuple-element.17.label_ref, ...), custom_call_target="tpu_custom_call" | custom-call | tf_op jit(solution)/shard_map/pallas_call | solution.py:316
  70.8 13.9 %all_to_all.42.got_ref = bf16[4,512,128]{2,1,0:T(8,128)(2,1)S(1)} all-to-all(bf16[4,512,128]{2,1,0:T(8,128)(2,1)S(1)} %get-tuple-element.19), channel_id=1, replica_groups={{0,128,256,384},{8,136,264,392},{16,144,272,400},{24,152,280,408},{32,1..., dimensions={0} | all-to-all | bytes 1048576 | tf_op jit(solution)/shard_map/all_to_all | solution.py:337
  84.8 27.4 %all_to_all.43.got_ref = f32[16,24,128]{2,1,0:T(8,128)S(1)} all-to-all(f32[16,24,128]{2,1,0:T(8,128)S(1)} %shard_map.89), channel_id=1, replica_groups={{0,8,16,24,32,40,48,56,64,72,80,88,96,104,112,120},{128,136,144,152,160..., dimensions={0} | all-to-all | bytes 393216 | tf_op jit(solution)/shard_map/all_to_all | solution.py:337
  112.9 4.7 %all-to-all-start.5 = ((f32[16,24,128]{2,1,0:T(8,128)}), f32[16,24,128]{2,1,0:T(8,128)S(1)}, u32[]{:S(2)}, u32[]{:S(2)}) async-start(f32[16,24,128]{2,1,0:T(8,128)} %shard_map.90), calls=%async_computation.5 | async-start | bytes 393216 | tf_op jit(solution)/shard_map/all_to_all | solution.py:337
  118.3 14.8 %all-to-all-done.5.gram_ref = f32[16,24,128]{2,1,0:T(8,128)S(1)} async-done(((f32[16,24,128]{2,1,0:T(8,128)}), f32[16,24,128]{2,1,0:T(8,128)S(1)}, u32[]{:S(2)}, u32[]{:S(2)}) %all-to-all-start.5) | async-done | bytes 196640 | tf_op jit(solution)/shard_map/all_to_all | solution.py:337
  133.1 0.8 broadcast_in_dim.3
  133.9 3.5 %all-to-all-start.6 = ((f32[4,16,16,128]{3,2,1,0:T(8,128)}), f32[4,16,16,128]{3,2,1,0:T(8,128)S(1)}, u32[]{:S(2)}, u32[]{:S(2)}) async-start(f32[4,16,16,128]{3,2,1,0:T(8,128)} %broadcast_in_dim.3), calls=%async_computation.6 | async-start | bytes 1048576 | tf_op jit(solution)/shard_map/all_to_all | solution.py:51
  137.4 5.7 %shard_map.91 = (f32[128,128]{1,0:T(8,128)S(1)}, f32[128,128]{1,0:T(8,128)S(1)}, f32[128,128]{1,0:T(8,128)S(1)}) custom-call(f32[16,24,128]{2,1,0:T(8,128)S(1)} %all-to-all-done.5.gram_ref, f32[1]{0:T(128)S(6)} %copy.12.ridge_ref), custom_call_target="tpu_custom_call" | custom-call | flops 8000000000 | bytes 262144 | tf_op jit(solution)/shard_map/pallas_call | solution.py:351
  143.1 2.3 %all-to-all-done.6 = f32[4,16,16,128]{3,2,1,0:T(8,128)S(1)} async-done(((f32[4,16,16,128]{3,2,1,0:T(8,128)}), f32[4,16,16,128]{3,2,1,0:T(8,128)S(1)}, u32[]{:S(2)}, u32[]{:S(2)}) %all-to-all-start.6) | async-done | bytes 524320 | tf_op jit(solution)/shard_map/all_to_all | solution.py:51
  145.4 2.5 %shard_map.92 = (f32[128,1024]{1,0:T(8,128)}, f32[64,1024]{1,0:T(8,128)}) custom-call(s32[1]{0:T(128)} %bitcast.first_ref, f32[64,16,128]{2,1,0:T(8,128)S(1)} %bitcast.22, f32[128,128]{1,0:T(8,128)S(1)} %get-tuple-element.20.terms_ref, f32[128,128]{1,0:T(8,128)S(1)} %get-tuple-element.21.turn_ref, f32[128,128]{1,0:T(8,128)S(1)} %get-tuple-element.22.upper_ref, ...), custom_call_target="tpu_custom_call" | custom-call | tf_op jit(solution)/shard_map/pallas_call | solution.py:359
  (25 shorter events, 6.0 us)
Async XLA Ops:
  0.6 0.8 copy-start
  2.1 9.9 %all-to-all-start = ((bf16[8,32,128]{2,1,0:T(8,128)(2,1)}), bf16[8,32,128]{2,1,0:T(8,128)(2,1)S(1)}, u32[]{:S(2)}, u32[]{:S(2)}) async-start(bf16[8,32,128]{2,1,0:T(8,128)(2,1)} %bitcast_bitcast_fusion), calls=%async_computation | async-start | bytes 131072 | tf_op jit(solution)/shard_map/all_to_all | solution.py:277
  8.1 57.1 %copy-start.1 = (bf16[1024,1024]{1,0:T(8,128)(2,1)S(1)}, bf16[1024,1024]{1,0:T(8,128)(2,1)}, u32[]{:S(2)}) copy-start(bf16[1024,1024]{1,0:T(8,128)(2,1)} %points_ref.1) | copy-start | bytes 6291460
  12.0 0.7 copy-start.3
  12.7 0.7 copy-start.4
  14.6 20.1 %collective-permute-start = (bf16[144,1024]{1,0:T(8,128)(2,1)S(1)}, bf16[144,1024]{1,0:T(8,128)(2,1)S(1)}, u32[]{:S(2)}, u32[]{:S(2)}) collective-permute-start(bf16[144,1024]{1,0:T(8,128)(2,1)S(1)} %pad_maximum_fusion), channel_id=1, source_target_pairs={{0,1},{8,9},{16,17},{24,25},{32,33},{40,41},{48,49},{56,57},{64,65... | collective-permute-start | bytes 884744 | tf_op jit(solution)/shard_map/ppermute | solution.py:288
  16.3 33.8 %all-to-all-start.1 = ((bf16[64,8,128]{2,1,0:T(8,128)(2,1)}), bf16[64,8,128]{2,1,0:T(8,128)(2,1)S(1)}, u32[]{:S(2)}, u32[]{:S(2)}) async-start(bf16[64,8,128]{2,1,0:T(8,128)(2,1)} %bitcast.8), calls=%async_computation.1 | async-start | bytes 262144 | tf_op jit(solution)/shard_map/all_to_all | solution.py:292
  34.7 15.7 %collective-permute-start.1 = (bf16[144,1024]{1,0:T(8,128)(2,1)S(1)}, bf16[144,1024]{1,0:T(8,128)(2,1)S(1)}, u32[]{:S(2)}, u32[]{:S(2)}) collective-permute-start(bf16[144,1024]{1,0:T(8,128)(2,1)S(1)} %broadcast_select_fusion), channel_id=1, source_target_pairs={{0,2},{1,3},{8,10},{9,11},{16,18},{17,19},{24,26},{25,27},{32,34},... | collective-permute-start | bytes 884744 | tf_op jit(solution)/shard_map/ppermute | solution.py:290
  36.3 14.2 %collective-permute-start.2 = (bf16[144,1024]{1,0:T(8,128)(2,1)S(1)}, bf16[144,1024]{1,0:T(8,128)(2,1)S(1)}, u32[]{:S(2)}, u32[]{:S(2)}) collective-permute-start(bf16[144,1024]{1,0:T(8,128)(2,1)S(1)} %broadcast_select_fusion), channel_id=1, source_target_pairs={{0,4},{1,5},{8,12},{9,13},{16,20},{17,21},{24,28},{25,29},{32,36},... | collective-permute-start | bytes 884744 | tf_op jit(solution)/shard_map/ppermute | solution.py:290
  37.6 12.8 %collective-permute-start.3 = (bf16[144,1024]{1,0:T(8,128)(2,1)S(1)}, bf16[144,1024]{1,0:T(8,128)(2,1)}, u32[]{:S(2)}, u32[]{:S(2)}) collective-permute-start(bf16[144,1024]{1,0:T(8,128)(2,1)S(1)} %broadcast_select_fusion), channel_id=1, source_target_pairs={{0,6},{1,7},{8,14},{9,15},{16,22},{17,23},{24,30},{25,31},{32,38},... | collective-permute-start | bytes 884744 | tf_op jit(solution)/shard_map/ppermute | solution.py:290
  61.6 3.6 %collective-permute-start.4 = (bf16[4,384,128]{2,1,0:T(8,128)(2,1)S(1)}, bf16[4,384,128]{2,1,0:T(8,128)(2,1)S(1)}, u32[]{:S(2)}, u32[]{:S(2)}) collective-permute-start(bf16[4,384,128]{2,1,0:T(8,128)(2,1)S(1)} %all_to_all.41.own_ref), channel_id=1, source_target_pairs={{0,1},{1,0},{2,3},{3,2},{4,5},{5,4},{6,7},{7,6},{8,9},{9,8},{10,11... | collective-permute-start | bytes 1179656 | tf_op jit(solution)/shard_map/ppermute | solution.py:311
  65.2 0.7 copy-start.2
  65.9 0.7 copy-start.5
  112.9 20.1 %all-to-all-start.5 = ((f32[16,24,128]{2,1,0:T(8,128)}), f32[16,24,128]{2,1,0:T(8,128)S(1)}, u32[]{:S(2)}, u32[]{:S(2)}) async-start(f32[16,24,128]{2,1,0:T(8,128)} %shard_map.90), calls=%async_computation.5 | async-start | bytes 393216 | tf_op jit(solution)/shard_map/all_to_all | solution.py:337
  133.9 11.5 %all-to-all-start.6 = ((f32[4,16,16,128]{3,2,1,0:T(8,128)}), f32[4,16,16,128]{3,2,1,0:T(8,128)S(1)}, u32[]{:S(2)}, u32[]{:S(2)}) async-start(f32[4,16,16,128]{3,2,1,0:T(8,128)} %broadcast_in_dim.3), calls=%async_computation.6 | async-start | bytes 1048576 | tf_op jit(solution)/shard_map/all_to_all | solution.py:51

commit v4 on v3

--- a/solution.py
+++ b/solution.py
@@ -53,8 +53,8 @@
     )
 
 
-def pack_kernel(env_ref, owner_ref, structure_ref, out_ref, owners):
-    owner = owner_ref[...]
+def pack_kernel(env_ref, equation_ref, out_ref, owners, eqs):
+    owner, structure = equation_ref[...] // eqs, equation_ref[...] % eqs
     envs = owner.shape[1]
     matches = iota((owners, envs), 0) == owner
     earlier = (iota((envs, envs), 0) < iota((envs, envs), 1)) & (
@@ -66,7 +66,7 @@
     slot = owner * GROUP + place
     chosen = one_hot(iota((owners * GROUP, envs), 0) == slot)
     data = dot(chosen, env_ref[...].reshape(envs, LANES))
-    named = jnp.where(matches, structure_ref[...], 0).astype(F32).astype(BF16)
+    named = jnp.where(matches, structure, 0).astype(F32).astype(BF16)
     at = one_hot(iota((LANES, envs), 0) == place)
     labels = dot(named, at, ((1,), (1,)))
     spread = one_hot(iota((owners * GROUP, owners), 0) == iota((owners * GROUP, owners), 1) * GROUP + SLOTS)
@@ -95,14 +95,13 @@
     points_ref,
     scale_ref,
     panel_ref,
-    weight_ref,
     matrix_ref,
     sums_ref,
     env_ref,
 ):
     chips, slots, _ = own_ref.shape
-    eqs = weight_ref.shape[1]
     cols = points_ref.shape[0]
+    eqs = scale_ref.shape[1] - cols
     core = core_ref[0]
     for chip in range(chips):
         at = pl.multiple_of((2 * chip + core) * LANES, LANES)
@@ -116,7 +115,7 @@
     mine = iota((slots, LANES), 1) == iota((slots, LANES), 0) % SLOTS
     label = jnp.sum(jnp.where(mine, named, 0.0), axis=1, keepdims=True)
     chosen = one_hot(label.astype(jnp.int32) == iota((slots, eqs), 1))
-    diagonal = jnp.where(iota((eqs, eqs), 0) == iota((eqs, eqs), 1), weight_ref[...], 0.0)
+    diagonal = jnp.where(iota((eqs, eqs), 0) == iota((eqs, eqs), 1), scale_ref[:, cols:], 0.0)
     weight = jnp.sum(diagonal, axis=1, keepdims=True)
 
     def block(points, scale):
@@ -277,13 +276,11 @@
     got = lax.all_to_all(sent, "cols", split_axis=0, concat_axis=0, tiled=True)
 
     packed = called(
-        functools.partial(pack_kernel, owners=owners),
+        functools.partial(pack_kernel, owners=owners, eqs=eqs),
         jax.ShapeDtypeStruct((owners * GROUP, LANES), BF16),
         got,
-        env_owner.reshape(1, envs),
-        env_structure.reshape(1, envs),
-    )
-    packed, panel = lax.optimization_barrier((packed, panel))
+        (env_owner[:, 0] * eqs + env_structure).reshape(1, envs),
+    )
     col = lax.axis_index("cols")
     near = jnp.where(col == 0, panel, lax.ppermute(panel, "cols", [(0, 1)]))
     for chip in range(1, peers // 2):
@@ -299,7 +296,6 @@
         ),
         arrived,
     )
-    slot_rows, panel = lax.optimization_barrier((slot_rows, panel))
     own = lax.all_to_all(
         slot_rows,
         "cols",
@@ -319,7 +315,7 @@
             jax.ShapeDtypeStruct((eqs, cols + WIDE), F32),
             jax.ShapeDtypeStruct((Y, own_rows + 2 * WIDE, LANES), BF16),
         ),
-        in_specs=[smem] + [vmem] * 7,
+        in_specs=[smem] + [vmem] * 6,
         out_specs=(vmem, vmem),
         scratch_shapes=[pltpu.VMEM((slots, peers * LANES), BF16)],
         compiler_params=params,
@@ -329,9 +325,8 @@
         other,
         labels,
         sparse_points,
-        point_scale.reshape(1, cols),
+        jnp.concatenate([point_scale, row_weight]).reshape(1, cols + eqs),
         panel,
-        row_weight.reshape(1, eqs),
     )
     def exchanged(array, groups):
         return lax.all_to_all(

time: 149 us -> 139 us (0.933)
  the two profiles are of different devices: /device:TPU:32 before, /device:TPU:4 now
where the time goes in v4:
time: 139 us; the launch traced here: 138 us
  starting transfers between devices  45.3 us (33%)
  waiting for transfers between devices  39.6 us (28%)
  blocking collectives  28.7 us (21%)
  Pallas kernels  15.6 us (11%)
  other arithmetic  4.33 us (3%)
  local copies, waits for them, and re-layouts  3.29 us (2%)
  between operations  1.47 us (1%)
    all_to_all x2, blocking collectives, exchanged(): lax.all_to_all(array, 'rows', split_axis=0, concat_axis=0, tiled=True, ax...  28.7 us
    all_to_all x1, waiting for transfers between devices, body(): lax.all_to_all(packed, 'rows', split_axis=0, concat_axis=0, tiled=True)  14.7 us
    all_to_all x1, starting transfers between devices, body(): lax.all_to_all(packed, 'rows', split_axis=0, concat_axis=0, tiled=True)  14.5 us
    all_to_all x1, waiting for transfers between devices, exchanged(): lax.all_to_all(array, 'rows', split_axis=0, concat_axis=0, tiled=True, ax...  13 us
    ppermute x3, waiting for transfers between devices, body(): reached = lax.ppermute(near, 'cols', [(0, 2 * chip), (1, 2 * chip + 1)])  9.24 us
    all_to_all x1, starting transfers between devices, body(): got = lax.all_to_all(sent, 'cols', split_axis=0, concat_axis=0, tiled=True)  9.15 us
    all_to_all x1, starting transfers between devices, body(): lax.all_to_all(slot_rows, 'cols', split_axis=0, concat_axis=0, tiled=True...  6.07 us
    pallas_call x1, Pallas kernels, body(): pl.pallas_call(factor_kernel, out_shape=(square, square, square), in_spec...  5.75 us
  transfers between devices with their start and end apart: 10, of which 6 were waited for; matrix products, arithmetic and copies ran while one was open for 4% of the time, Pallas kernels for 5%

profile of v4, /device:TPU:4, one launch (start us, length us, event | category | flops | bytes accessed | tf_op | source)
XLA Modules:
  0.0 138.2 jit_solution(9401217608264660457)
XLA Ops:
  2.1 9.2 %all-to-all-start = ((bf16[8,32,128]{2,1,0:T(8,128)(2,1)}), bf16[8,32,128]{2,1,0:T(8,128)(2,1)S(1)}, u32[]{:S(2)}, u32[]{:S(2)}) async-start(bf16[8,32,128]{2,1,0:T(8,128)(2,1)} %bitcast_bitcast_fusion), calls=%async_computation | async-start | bytes 131072 | tf_op jit(solution)/shard_map/all_to_all | solution.py:276
  12.6 1.0 slice.9
  14.4 1.2 shard_map.86
  15.6 14.5 %all-to-all-start.1 = ((bf16[64,8,128]{2,1,0:T(8,128)(2,1)}), bf16[64,8,128]{2,1,0:T(8,128)(2,1)S(1)}, u32[]{:S(2)}, u32[]{:S(2)}) async-start(bf16[64,8,128]{2,1,0:T(8,128)(2,1)} %bitcast.5), calls=%async_computation.1 | async-start | bytes 262144 | tf_op jit(solution)/shard_map/all_to_all | solution.py:289
  30.2 1.4 %collective-permute-start.1 = (bf16[144,1024]{1,0:T(8,128)(2,1)S(1)}, bf16[144,1024]{1,0:T(8,128)(2,1)}, u32[]{:S(2)}, u32[]{:S(2)}) collective-permute-start(bf16[144,1024]{1,0:T(8,128)(2,1)S(1)} %pad_maximum_fusion), channel_id=1, source_target_pairs={{0,1},{8,9},{16,17},{24,25},{32,33},{40,41},{48,49},{56,57},{64,65... | collective-permute-start | bytes 884744 | tf_op jit(solution)/shard_map/ppermute | solution.py:285
  31.5 14.7 %all-to-all-done.1 = bf16[64,8,128]{2,1,0:T(8,128)(2,1)S(1)} async-done(((bf16[64,8,128]{2,1,0:T(8,128)(2,1)}), bf16[64,8,128]{2,1,0:T(8,128)(2,1)S(1)}, u32[]{:S(2)}, u32[]{:S(2)}) %all-to-all-start.1) | async-done | bytes 131104 | tf_op jit(solution)/shard_map/all_to_all | solution.py:289
  46.3 1.1 shard_map.87
  47.3 6.1 %all-to-all-start.2 = ((bf16[4,384,128]{2,1,0:T(8,128)(2,1)}), bf16[4,384,128]{2,1,0:T(8,128)(2,1)S(1)}, u32[]{:S(2)}, u32[]{:S(2)}) async-start(bf16[4,384,128]{2,1,0:T(8,128)(2,1)} %get-tuple-element.9), calls=%async_computation.2 | async-start | bytes 786432 | tf_op jit(solution)/shard_map/all_to_all | solution.py:299
  53.4 1.0 broadcast_select_fusion
  54.5 1.4 %collective-permute-start.2 = (bf16[144,1024]{1,0:T(8,128)(2,1)S(1)}, bf16[144,1024]{1,0:T(8,128)(2,1)}, u32[]{:S(2)}, u32[]{:S(2)}) collective-permute-start(bf16[144,1024]{1,0:T(8,128)(2,1)S(1)} %broadcast_select_fusion), channel_id=1, source_target_pairs={{0,2},{1,3},{8,10},{9,11},{16,18},{17,19},{24,26},{25,27},{32,34},... | collective-permute-start | bytes 884744 | tf_op jit(solution)/shard_map/ppermute | solution.py:287
  55.8 1.3 collective-permute-start.3
  57.1 1.4 %collective-permute-start.4 = (bf16[144,1024]{1,0:T(8,128)(2,1)S(1)}, bf16[144,1024]{1,0:T(8,128)(2,1)}, u32[]{:S(2)}, u32[]{:S(2)}) collective-permute-start(bf16[144,1024]{1,0:T(8,128)(2,1)S(1)} %broadcast_select_fusion), channel_id=1, source_target_pairs={{0,6},{1,7},{8,14},{9,15},{16,22},{17,23},{24,30},{25,31},{32,38},... | collective-permute-start | bytes 884744 | tf_op jit(solution)/shard_map/ppermute | solution.py:287
  58.8 1.9 %collective-permute-start = (bf16[4,384,128]{2,1,0:T(8,128)(2,1)S(1)}, bf16[4,384,128]{2,1,0:T(8,128)(2,1)S(1)}, u32[]{:S(2)}, u32[]{:S(2)}) collective-permute-start(bf16[4,384,128]{2,1,0:T(8,128)(2,1)S(1)} %all-to-all-done.2.own_ref), channel_id=1, source_target_pairs={{0,1},{1,0},{2,3},{3,2},{4,5},{5,4},{6,7},{7,6},{8,9},{9,8},{10,11... | collective-permute-start | bytes 1179656 | tf_op jit(solution)/shard_map/ppermute | solution.py:307
  60.8 9.2 %collective-permute-done.3 = bf16[144,1024]{1,0:T(8,128)(2,1)} collective-permute-done((bf16[144,1024]{1,0:T(8,128)(2,1)S(1)}, bf16[144,1024]{1,0:T(8,128)(2,1)}, u32[]{:S(2)}, u32[]{:S(2)}) %collective-permute-start.3) | collective-permute-done | bytes 294944 | tf_op jit(solution)/shard_map/ppermute | solution.py:287
  70.0 1.2 add_add_fusion.panel_ref
  71.2 4.3 %shard_map.88 = (f32[64,1152]{1,0:T(8,128)S(1)}, bf16[4,512,128]{2,1,0:T(8,128)(2,1)S(1)}) custom-call(s32[1]{0:T(128)} %bitcast.1.core_ref, bf16[4,384,128]{2,1,0:T(8,128)(2,1)S(1)} %all-to-all-done.2.own_ref, bf16[4,384,128]{2,1,0:T(8,128)(2,1)S(1)} %collective-permute-done.other_ref, bf16[64,128]{1,0:T(8,128)(2,1)S(1)} %get-tuple-element.10.label_ref, ...), custom_call_target="tpu_custom_call" | custom-call | tf_op jit(solution)/shard_map/pallas_call | solution.py:312
  75.5 11.5 %all_to_all.41.got_ref = bf16[4,512,128]{2,1,0:T(8,128)(2,1)S(1)} all-to-all(bf16[4,512,128]{2,1,0:T(8,128)(2,1)S(1)} %get-tuple-element.11), channel_id=1, replica_groups={{0,128,256,384},{8,136,264,392},{16,144,272,400},{24,152,280,408},{32,1..., dimensions={0} | all-to-all | bytes 1048576 | tf_op jit(solution)/shard_map/all_to_all | solution.py:332
  87.1 17.2 %all_to_all.42.got_ref = f32[16,24,128]{2,1,0:T(8,128)S(1)} all-to-all(f32[16,24,128]{2,1,0:T(8,128)S(1)} %shard_map.89), channel_id=1, replica_groups={{0,8,16,24,32,40,48,56,64,72,80,88,96,104,112,120},{128,136,144,152,160..., dimensions={0} | all-to-all | bytes 393216 | tf_op jit(solution)/shard_map/all_to_all | solution.py:332
  105.0 4.8 %all-to-all-start.5 = ((f32[16,24,128]{2,1,0:T(8,128)}), f32[16,24,128]{2,1,0:T(8,128)S(1)}, u32[]{:S(2)}, u32[]{:S(2)}) async-start(f32[16,24,128]{2,1,0:T(8,128)} %shard_map.90), calls=%async_computation.5 | async-start | bytes 393216 | tf_op jit(solution)/shard_map/all_to_all | solution.py:332
  110.4 13.0 %all-to-all-done.5.gram_ref = f32[16,24,128]{2,1,0:T(8,128)S(1)} async-done(((f32[16,24,128]{2,1,0:T(8,128)}), f32[16,24,128]{2,1,0:T(8,128)S(1)}, u32[]{:S(2)}, u32[]{:S(2)}) %all-to-all-start.5) | async-done | bytes 196640 | tf_op jit(solution)/shard_map/all_to_all | solution.py:332
  124.2 3.5 %all-to-all-start.6 = ((f32[4,16,16,128]{3,2,1,0:T(8,128)}), f32[4,16,16,128]{3,2,1,0:T(8,128)S(1)}, u32[]{:S(2)}, u32[]{:S(2)}) async-start(f32[4,16,16,128]{3,2,1,0:T(8,128)} %broadcast_in_dim.3), calls=%async_computation.6 | async-start | bytes 1048576 | tf_op jit(solution)/shard_map/all_to_all | solution.py:51
  127.7 5.7 %shard_map.91 = (f32[128,128]{1,0:T(8,128)S(1)}, f32[128,128]{1,0:T(8,128)S(1)}, f32[128,128]{1,0:T(8,128)S(1)}) custom-call(f32[16,24,128]{2,1,0:T(8,128)S(1)} %all-to-all-done.5.gram_ref, f32[1]{0:T(128)S(6)} %copy.12.ridge_ref), custom_call_target="tpu_custom_call" | custom-call | flops 8000000000 | bytes 262144 | tf_op jit(solution)/shard_map/pallas_call | solution.py:346
  133.4 2.3 %all-to-all-done.6 = f32[4,16,16,128]{3,2,1,0:T(8,128)S(1)} async-done(((f32[4,16,16,128]{3,2,1,0:T(8,128)}), f32[4,16,16,128]{3,2,1,0:T(8,128)S(1)}, u32[]{:S(2)}, u32[]{:S(2)}) %all-to-all-start.6) | async-done | bytes 524320 | tf_op jit(solution)/shard_map/all_to_all | solution.py:51
  135.7 2.5 %shard_map.92 = (f32[128,1024]{1,0:T(8,128)}, f32[64,1024]{1,0:T(8,128)}) custom-call(s32[1]{0:T(128)} %bitcast.first_ref, f32[64,16,128]{2,1,0:T(8,128)S(1)} %bitcast.20, f32[128,128]{1,0:T(8,128)S(1)} %get-tuple-element.12.terms_ref, f32[128,128]{1,0:T(8,128)S(1)} %get-tuple-element.13.turn_ref, f32[128,128]{1,0:T(8,128)S(1)} %get-tuple-element.14.upper_ref, ...), custom_call_target="tpu_custom_call" | custom-call | tf_op jit(solution)/shard_map/pallas_call | solution.py:354
  (26 shorter events, 5.5 us)
Async XLA Ops:
  0.6 0.8 copy-start
  0.6 60.1 %copy-start.2 = (f32[1024]{0:T(1024)S(1)}, f32[1024]{0:T(1024)}, u32[]{:S(2)}) copy-start(f32[1024]{0:T(1024)} %param.9) | copy-start | bytes 12292
  0.7 60.1 %copy-start.3 = (f32[64]{0:T(128)S(1)}, f32[64]{0:T(128)}, u32[]{:S(2)}) copy-start(f32[64]{0:T(128)} %param.12) | copy-start | bytes 772
  2.1 12.3 %all-to-all-start = ((bf16[8,32,128]{2,1,0:T(8,128)(2,1)}), bf16[8,32,128]{2,1,0:T(8,128)(2,1)S(1)}, u32[]{:S(2)}, u32[]{:S(2)}) async-start(bf16[8,32,128]{2,1,0:T(8,128)(2,1)} %bitcast_bitcast_fusion), calls=%async_computation | async-start | bytes 131072 | tf_op jit(solution)/shard_map/all_to_all | solution.py:276
  15.6 55.6 %copy-start.1 = (bf16[1024,1024]{1,0:T(8,128)(2,1)S(1)}, bf16[1024,1024]{1,0:T(8,128)(2,1)}, u32[]{:S(2)}) copy-start(bf16[1024,1024]{1,0:T(8,128)(2,1)} %points_ref.1) | copy-start | bytes 6291460
  15.6 30.7 %all-to-all-start.1 = ((bf16[64,8,128]{2,1,0:T(8,128)(2,1)}), bf16[64,8,128]{2,1,0:T(8,128)(2,1)S(1)}, u32[]{:S(2)}, u32[]{:S(2)}) async-start(bf16[64,8,128]{2,1,0:T(8,128)(2,1)} %bitcast.5), calls=%async_computation.1 | async-start | bytes 262144 | tf_op jit(solution)/shard_map/all_to_all | solution.py:289
  30.2 23.3 %collective-permute-start.1 = (bf16[144,1024]{1,0:T(8,128)(2,1)S(1)}, bf16[144,1024]{1,0:T(8,128)(2,1)}, u32[]{:S(2)}, u32[]{:S(2)}) collective-permute-start(bf16[144,1024]{1,0:T(8,128)(2,1)S(1)} %pad_maximum_fusion), channel_id=1, source_target_pairs={{0,1},{8,9},{16,17},{24,25},{32,33},{40,41},{48,49},{56,57},{64,65... | collective-permute-start | bytes 884744 | tf_op jit(solution)/shard_map/ppermute | solution.py:285
  47.3 11.5 %all-to-all-start.2 = ((bf16[4,384,128]{2,1,0:T(8,128)(2,1)}), bf16[4,384,128]{2,1,0:T(8,128)(2,1)S(1)}, u32[]{:S(2)}, u32[]{:S(2)}) async-start(bf16[4,384,128]{2,1,0:T(8,128)(2,1)} %get-tuple-element.9), calls=%async_computation.2 | async-start | bytes 786432 | tf_op jit(solution)/shard_map/all_to_all | solution.py:299
  54.5 6.3 %collective-permute-start.2 = (bf16[144,1024]{1,0:T(8,128)(2,1)S(1)}, bf16[144,1024]{1,0:T(8,128)(2,1)}, u32[]{:S(2)}, u32[]{:S(2)}) collective-permute-start(bf16[144,1024]{1,0:T(8,128)(2,1)S(1)} %broadcast_select_fusion), channel_id=1, source_target_pairs={{0,2},{1,3},{8,10},{9,11},{16,18},{17,19},{24,26},{25,27},{32,34},... | collective-permute-start | bytes 884744 | tf_op jit(solution)/shard_map/ppermute | solution.py:287
  55.8 14.2 %collective-permute-start.3 = (bf16[144,1024]{1,0:T(8,128)(2,1)S(1)}, bf16[144,1024]{1,0:T(8,128)(2,1)}, u32[]{:S(2)}, u32[]{:S(2)}) collective-permute-start(bf16[144,1024]{1,0:T(8,128)(2,1)S(1)} %broadcast_select_fusion), channel_id=1, source_target_pairs={{0,4},{1,5},{8,12},{9,13},{16,20},{17,21},{24,28},{25,29},{32,36},... | collective-permute-start | bytes 884744 | tf_op jit(solution)/shard_map/ppermute | solution.py:287
  57.1 12.9 %collective-permute-start.4 = (bf16[144,1024]{1,0:T(8,128)(2,1)S(1)}, bf16[144,1024]{1,0:T(8,128)(2,1)}, u32[]{:S(2)}, u32[]{:S(2)}) collective-permute-start(bf16[144,1024]{1,0:T(8,128)(2,1)S(1)} %broadcast_select_fusion), channel_id=1, source_target_pairs={{0,6},{1,7},{8,14},{9,15},{16,22},{17,23},{24,30},{25,31},{32,38},... | collective-permute-start | bytes 884744 | tf_op jit(solution)/shard_map/ppermute | solution.py:287
  58.8 12.4 %collective-permute-start = (bf16[4,384,128]{2,1,0:T(8,128)(2,1)S(1)}, bf16[4,384,128]{2,1,0:T(8,128)(2,1)S(1)}, u32[]{:S(2)}, u32[]{:S(2)}) collective-permute-start(bf16[4,384,128]{2,1,0:T(8,128)(2,1)S(1)} %all-to-all-done.2.own_ref), channel_id=1, source_target_pairs={{0,1},{1,0},{2,3},{3,2},{4,5},{5,4},{6,7},{7,6},{8,9},{9,8},{10,11... | collective-permute-start | bytes 1179656 | tf_op jit(solution)/shard_map/ppermute | solution.py:307
  105.0 18.4 %all-to-all-start.5 = ((f32[16,24,128]{2,1,0:T(8,128)}), f32[16,24,128]{2,1,0:T(8,128)S(1)}, u32[]{:S(2)}, u32[]{:S(2)}) async-start(f32[16,24,128]{2,1,0:T(8,128)} %shard_map.90), calls=%async_computation.5 | async-start | bytes 393216 | tf_op jit(solution)/shard_map/all_to_all | solution.py:332
  124.2 11.5 %all-to-all-start.6 = ((f32[4,16,16,128]{3,2,1,0:T(8,128)}), f32[4,16,16,128]{3,2,1,0:T(8,128)S(1)}, u32[]{:S(2)}, u32[]{:S(2)}) async-start(f32[4,16,16,128]{3,2,1,0:T(8,128)} %broadcast_in_dim.3), calls=%async_computation.6 | async-start | bytes 1048576 | tf_op jit(solution)/shard_map/all_to_all | solution.py:51

commit v5 on v4

--- a/solution.py
+++ b/solution.py
@@ -53,6 +53,21 @@
     )
 
 
+def first_kernel(env_ref, points_ref, scale_ref, out_ref):
+    mine, wide = env_ref.shape[0], points_ref.shape[0]
+    scale = scale_ref[...]
+    high = scale.astype(BF16).astype(F32)
+    middle = (scale - high).astype(BF16).astype(F32)
+    low = scale - high - middle
+    row = iota((16, wide), 0)
+    parts = jnp.where(row == 0, high, jnp.where(row == 1, middle, jnp.where(row == 2, low, 0.0)))
+    for peer in range(out_ref.shape[0]):
+        at = slice(peer * LANES, (peer + 1) * LANES)
+        out_ref[peer, 0:mine] = env_ref[:, at]
+        out_ref[peer, mine : mine + wide] = points_ref[:, at]
+        out_ref[peer, mine + wide :] = parts.astype(BF16)
+
+
 def pack_kernel(env_ref, equation_ref, out_ref, owners, eqs):
     owner, structure = equation_ref[...] // eqs, equation_ref[...] % eqs
     envs = owner.shape[1]
@@ -65,7 +80,7 @@
     place = (iota((1, envs), 1) // HALF) * CAP + within
     slot = owner * GROUP + place
     chosen = one_hot(iota((owners * GROUP, envs), 0) == slot)
-    data = dot(chosen, env_ref[...].reshape(envs, LANES))
+    data = dot(chosen, env_ref[:, 0 : envs // env_ref.shape[0]].reshape(envs, LANES))
     named = jnp.where(matches, structure, 0).astype(F32).astype(BF16)
     at = one_hot(iota((LANES, envs), 0) == place)
     labels = dot(named, at, ((1,), (1,)))
@@ -73,7 +88,7 @@
     out_ref[...] = (data + dot(spread, labels.astype(BF16))).astype(BF16)
 
 
-def unpack_kernel(got_ref, out_ref, label_ref):
+def unpack_kernel(got_ref, panel_ref, out_ref, label_ref):
     rows = got_ref.shape[0]
     sources = rows // GROUP
     slots = sources * SLOTS
@@ -82,7 +97,8 @@
     source, place = slot // SLOTS, slot % SLOTS
     data = dot(one_hot(row == source * GROUP + place), got).astype(BF16)
     for copy in range(out_ref.shape[0]):
-        out_ref[copy] = data
+        out_ref[copy, 0:slots] = data
+        out_ref[copy, slots:] = panel_ref[...]
     source, row = iota((sources, rows), 0), iota((sources, rows), 1)
     label_ref[...] = dot(one_hot(row == source * GROUP + SLOTS), got).astype(BF16)
 
@@ -99,7 +115,8 @@
     sums_ref,
     env_ref,
 ):
-    chips, slots, _ = own_ref.shape
+    chips, rows, _ = own_ref.shape
+    slots = rows - WIDE
     cols = points_ref.shape[0]
     eqs = scale_ref.shape[1] - cols
     core = core_ref[0]
@@ -119,13 +136,13 @@
     weight = jnp.sum(diagonal, axis=1, keepdims=True)
 
     def block(points, scale):
-        z = dot(env_ref[...], points, ((1,), (1,))) * dot_scale
+        z = dot(env_ref[0:slots, :], points, ((1,), (1,))) * dot_scale
         squared = z * z
         kernel = (scale * squared * squared).astype(BF16)
         return dot(chosen, kernel, ((0,), (0,))) * weight
 
-    parts = panel_ref[WIDE:, 0:WIDE].astype(F32)
-    panel = block(panel_ref[0:WIDE, :], parts[0:1] + parts[1:2] + parts[2:3])
+    parts = panel_ref[...].astype(F32)
+    panel = block(env_ref[slots:rows, :], parts[0:1] + parts[1:2] + parts[2:3])
     matrix_ref[:, cols : cols + WIDE] = panel
     gram = dot(panel, panel, ((0,), (0,)), HIGHEST)
     high = gram.astype(BF16)
@@ -265,15 +282,21 @@
     z_groups = [[y * Z + z for z in range(Z)] for y in range(Y)]
     y_groups = [[y * Z + z for y in range(Y)] for z in range(Z)]
 
-    scale = point_scale[:WIDE]
-    high = lax.reduce_precision(scale, 8, 7)
-    middle = lax.reduce_precision(scale - high, 8, 7)
-    low = scale - high - middle
-    parts = jnp.pad(jnp.stack([high, middle, low]), ((0, 13), (0, peers * LANES - WIDE)))
-    panel = jnp.concatenate([sparse_points[:WIDE], parts.astype(BF16)], axis=0)
-
-    sent = descriptors.reshape(mine, peers, LANES).transpose(1, 0, 2)
+    length = mine + WIDE + 16
+    sent = pl.pallas_call(
+        first_kernel,
+        out_shape=jax.ShapeDtypeStruct((peers, length, LANES), BF16),
+        grid=(1,),
+        in_specs=[
+            pl.BlockSpec((mine, peers * LANES), lambda i: (0, 0)),
+            pl.BlockSpec((WIDE, peers * LANES), lambda i: (0, 0)),
+            pl.BlockSpec((1, WIDE), lambda i: (0, 0)),
+        ],
+        out_specs=pl.BlockSpec((peers, length, LANES), lambda i: (0, 0, 0)),
+        compiler_params=pltpu.CompilerParams(vmem_limit_bytes=60 * 2**20),
+    )(descriptors, sparse_points, point_scale.reshape(1, cols))
     got = lax.all_to_all(sent, "cols", split_axis=0, concat_axis=0, tiled=True)
+    panel_part, parts = got[0, mine : mine + WIDE], got[0, mine + WIDE :]
 
     packed = called(
         functools.partial(pack_kernel, owners=owners, eqs=eqs),
@@ -282,19 +305,16 @@
         (env_owner[:, 0] * eqs + env_structure).reshape(1, envs),
     )
     col = lax.axis_index("cols")
-    near = jnp.where(col == 0, panel, lax.ppermute(panel, "cols", [(0, 1)]))
-    for chip in range(1, peers // 2):
-        reached = lax.ppermute(near, "cols", [(0, 2 * chip), (1, 2 * chip + 1)])
-        panel = near + reached if chip == 1 else panel + reached
     arrived = lax.all_to_all(packed, "rows", split_axis=0, concat_axis=0, tiled=True)
     slots = owners * SLOTS
     slot_rows, labels = called(
         unpack_kernel,
         (
-            jax.ShapeDtypeStruct((peers // 2, slots, LANES), BF16),
+            jax.ShapeDtypeStruct((peers // 2, slots + WIDE, LANES), BF16),
             jax.ShapeDtypeStruct((owners, LANES), BF16),
         ),
         arrived,
+        panel_part,
     )
     own = lax.all_to_all(
         slot_rows,
@@ -317,7 +337,7 @@
         ),
         in_specs=[smem] + [vmem] * 6,
         out_specs=(vmem, vmem),
-        scratch_shapes=[pltpu.VMEM((slots, peers * LANES), BF16)],
+        scratch_shapes=[pltpu.VMEM((slots + WIDE, peers * LANES), BF16)],
         compiler_params=params,
     )(
         (col % 2).reshape(1),
@@ -326,7 +346,7 @@
         labels,
         sparse_points,
         jnp.concatenate([point_scale, row_weight]).reshape(1, cols + eqs),
-        panel,
+        parts,
     )
     def exchanged(array, groups):
         return lax.all_to_all(

time: 139 us -> 140 us (level)
  the two profiles are of different devices: /device:TPU:4 before, /device:TPU:32 now
where the time goes in v5:
time: 140 us; the launch traced here: 139 us
  blocking collectives  43.9 us (31%)
  waiting for transfers between devices  43.1 us (31%)
  starting transfers between devices  32.8 us (23%)
  Pallas kernels  16.8 us (12%)
  between operations  1.47 us (1%)
    all_to_all x2, blocking collectives, exchanged(): lax.all_to_all(array, 'rows', split_axis=0, concat_axis=0, tiled=True, ax...  33.5 us
    all_to_all x1, starting transfers between devices, body(): lax.all_to_all(packed, 'rows', split_axis=0, concat_axis=0, tiled=True)  18.4 us
    all_to_all x1, waiting for transfers between devices, body(): lax.all_to_all(packed, 'rows', split_axis=0, concat_axis=0, tiled=True)  15.7 us
    all_to_all x1, waiting for transfers between devices, exchanged(): lax.all_to_all(array, 'rows', split_axis=0, concat_axis=0, tiled=True, ax...  14.8 us
    all_to_all x1, blocking collectives, body(): lax.all_to_all(slot_rows, 'cols', split_axis=0, concat_axis=0, tiled=True...  10.5 us
    all_to_all x1, waiting for transfers between devices, body(): got = lax.all_to_all(sent, 'cols', split_axis=0, concat_axis=0, tiled=True)  8.55 us
    pallas_call x1, Pallas kernels, body(): pl.pallas_call(factor_kernel, out_shape=(square, square, square), in_spec...  5.74 us
    all_to_all x1, starting transfers between devices, exchanged(): lax.all_to_all(array, 'rows', split_axis=0, concat_axis=0, tiled=True, ax...  4.71 us
  transfers between devices with their start and end apart: 5, of which 5 were waited for; matrix products, arithmetic and copies ran while one was open for 0% of the time, Pallas kernels for 4%

profile of v5, /device:TPU:32, one launch (start us, length us, event | category | flops | bytes accessed | tf_op | source)
XLA Modules:
  0.0 139.0 jit_solution(8136049788905621798)
XLA Ops:
  0.6 0.0 copy-start.3
  0.7 1.9 %shard_map.86 = bf16[8,176,128]{2,1,0:T(8,128)(2,1)} custom-call(bf16[32,1024]{1,0:T(8,128)(2,1)} %env_ref.1, bf16[1024,1024]{1,0:T(8,128)(2,1)} %points_ref.3, f32[1,1024]{1,0:T(1,128)} %bitcast.15), custom_call_target="tpu_custom_call" | custom-call | tf_op jit(solution)/shard_map/pallas_call | solution.py:286
  2.6 4.3 %all-to-all-start = ((bf16[8,176,128]{2,1,0:T(8,128)(2,1)}), bf16[8,176,128]{2,1,0:T(8,128)(2,1)S(1)}, u32[]{:S(2)}, u32[]{:S(2)}) async-start(bf16[8,176,128]{2,1,0:T(8,128)(2,1)} %shard_map.86), calls=%async_computation | async-start | bytes 720896 | tf_op jit(solution)/shard_map/all_to_all | solution.py:298
  6.9 8.6 %all-to-all-done.env_ref = bf16[8,176,128]{2,1,0:T(8,128)(2,1)S(1)} async-done(((bf16[8,176,128]{2,1,0:T(8,128)(2,1)}), bf16[8,176,128]{2,1,0:T(8,128)(2,1)S(1)}, u32[]{:S(2)}, u32[]{:S(2)}) %all-to-all-start) | async-done | bytes 360480 | tf_op jit(solution)/shard_map/all_to_all | solution.py:298
  15.5 1.2 shard_map.87
  16.7 18.4 %all-to-all-start.1 = ((bf16[64,8,128]{2,1,0:T(8,128)(2,1)}), bf16[64,8,128]{2,1,0:T(8,128)(2,1)S(1)}, u32[]{:S(2)}, u32[]{:S(2)}) async-start(bf16[64,8,128]{2,1,0:T(8,128)(2,1)} %bitcast.5), calls=%async_computation.1 | async-start | bytes 262144 | tf_op jit(solution)/shard_map/all_to_all | solution.py:308
  35.1 15.7 %all-to-all-done.1 = bf16[64,8,128]{2,1,0:T(8,128)(2,1)S(1)} async-done(((bf16[64,8,128]{2,1,0:T(8,128)(2,1)}), bf16[64,8,128]{2,1,0:T(8,128)(2,1)S(1)}, u32[]{:S(2)}, u32[]{:S(2)}) %all-to-all-start.1) | async-done | bytes 131104 | tf_op jit(solution)/shard_map/all_to_all | solution.py:308
  50.8 0.3 shard_map.88
  51.1 10.5 %all_to_all.41.own_ref = bf16[4,512,128]{2,1,0:T(8,128)(2,1)S(1)} all-to-all(bf16[4,512,128]{2,1,0:T(8,128)(2,1)S(1)} %get-tuple-element.9), channel_id=1, replica_groups={{0,2,4,6},{1,3,5,7},{8,10,12,14},{9,11,13,15},{16,18,20,22},{17,19,21,2..., dimensions={0} | all-to-all | bytes 1048576 | tf_op jit(solution)/shard_map/all_to_all | solution.py:319
  61.6 1.9 %collective-permute-start = (bf16[4,512,128]{2,1,0:T(8,128)(2,1)S(1)}, bf16[4,512,128]{2,1,0:T(8,128)(2,1)S(1)}, u32[]{:S(2)}, u32[]{:S(2)}) collective-permute-start(bf16[4,512,128]{2,1,0:T(8,128)(2,1)S(1)} %all_to_all.41.own_ref), channel_id=1, source_target_pairs={{0,1},{1,0},{2,3},{3,2},{4,5},{5,4},{6,7},{7,6},{8,9},{9,8},{10,11... | collective-permute-start | bytes 1572872 | tf_op jit(solution)/shard_map/ppermute | solution.py:327
  63.6 1.8 %collective-permute-done.other_ref = bf16[4,512,128]{2,1,0:T(8,128)(2,1)S(1)} collective-permute-done((bf16[4,512,128]{2,1,0:T(8,128)(2,1)S(1)}, bf16[4,512,128]{2,1,0:T(8,128)(2,1)S(1)}, u32[]{:S(2)}, u32[]{:S(2)}) %collective-permute-start) | collective-permute-done | bytes 524320 | tf_op jit(solution)/shard_map/ppermute | solution.py:327
  65.4 0.0 copy-done
  65.4 4.4 %shard_map.89 = (f32[64,1152]{1,0:T(8,128)S(1)}, bf16[4,512,128]{2,1,0:T(8,128)(2,1)S(1)}) custom-call(s32[1]{0:T(128)} %bitcast.1.core_ref, bf16[4,512,128]{2,1,0:T(8,128)(2,1)S(1)} %all_to_all.41.own_ref, bf16[4,512,128]{2,1,0:T(8,128)(2,1)S(1)} %collective-permute-done.other_ref, bf16[64,128]{1,0:T(8,128)(2,1)S(1)} %get-tuple-element.10.label_ref, ...), custom_call_target="tpu_custom_call" | custom-call | tf_op jit(solution)/shard_map/pallas_call | solution.py:332
  69.8 12.9 %all_to_all.42.got_ref = bf16[4,512,128]{2,1,0:T(8,128)(2,1)S(1)} all-to-all(bf16[4,512,128]{2,1,0:T(8,128)(2,1)S(1)} %get-tuple-element.11), channel_id=1, replica_groups={{0,128,256,384},{8,136,264,392},{16,144,272,400},{24,152,280,408},{32,1..., dimensions={0} | all-to-all | bytes 1048576 | tf_op jit(solution)/shard_map/all_to_all | solution.py:352
  82.7 0.1 shard_map.90
  82.8 20.5 %all_to_all.43.got_ref = f32[16,24,128]{2,1,0:T(8,128)S(1)} all-to-all(f32[16,24,128]{2,1,0:T(8,128)S(1)} %shard_map.90), channel_id=1, replica_groups={{0,8,16,24,32,40,48,56,64,72,80,88,96,104,112,120},{128,136,144,152,160..., dimensions={0} | all-to-all | bytes 393216 | tf_op jit(solution)/shard_map/all_to_all | solution.py:352
  103.3 0.7 shard_map.91
  104.0 4.7 %all-to-all-start.5 = ((f32[16,24,128]{2,1,0:T(8,128)}), f32[16,24,128]{2,1,0:T(8,128)S(1)}, u32[]{:S(2)}, u32[]{:S(2)}) async-start(f32[16,24,128]{2,1,0:T(8,128)} %shard_map.91), calls=%async_computation.5 | async-start | bytes 393216 | tf_op jit(solution)/shard_map/all_to_all | solution.py:352
  109.4 14.8 %all-to-all-done.5.gram_ref = f32[16,24,128]{2,1,0:T(8,128)S(1)} async-done(((f32[16,24,128]{2,1,0:T(8,128)}), f32[16,24,128]{2,1,0:T(8,128)S(1)}, u32[]{:S(2)}, u32[]{:S(2)}) %all-to-all-start.5) | async-done | bytes 196640 | tf_op jit(solution)/shard_map/all_to_all | solution.py:352
  124.2 0.8 broadcast_in_dim.3
  125.0 3.5 %all-to-all-start.6 = ((f32[4,16,16,128]{3,2,1,0:T(8,128)}), f32[4,16,16,128]{3,2,1,0:T(8,128)S(1)}, u32[]{:S(2)}, u32[]{:S(2)}) async-start(f32[4,16,16,128]{3,2,1,0:T(8,128)} %broadcast_in_dim.3), calls=%async_computation.6 | async-start | bytes 1048576 | tf_op jit(solution)/shard_map/all_to_all | solution.py:51
  128.5 5.7 %shard_map.92 = (f32[128,128]{1,0:T(8,128)S(1)}, f32[128,128]{1,0:T(8,128)S(1)}, f32[128,128]{1,0:T(8,128)S(1)}) custom-call(f32[16,24,128]{2,1,0:T(8,128)S(1)} %all-to-all-done.5.gram_ref, f32[1]{0:T(128)S(6)} %copy.9.ridge_ref), custom_call_target="tpu_custom_call" | custom-call | flops 8000000000 | bytes 262144 | tf_op jit(solution)/shard_map/pallas_call | solution.py:366
  134.2 2.3 %all-to-all-done.6 = f32[4,16,16,128]{3,2,1,0:T(8,128)S(1)} async-done(((f32[4,16,16,128]{3,2,1,0:T(8,128)}), f32[4,16,16,128]{3,2,1,0:T(8,128)S(1)}, u32[]{:S(2)}, u32[]{:S(2)}) %all-to-all-start.6) | async-done | bytes 524320 | tf_op jit(solution)/shard_map/all_to_all | solution.py:51
  136.5 2.5 %shard_map.93 = (f32[128,1024]{1,0:T(8,128)}, f32[64,1024]{1,0:T(8,128)}) custom-call(s32[1]{0:T(128)} %bitcast.first_ref, f32[64,16,128]{2,1,0:T(8,128)S(1)} %bitcast.12, f32[128,128]{1,0:T(8,128)S(1)} %get-tuple-element.12.terms_ref, f32[128,128]{1,0:T(8,128)S(1)} %get-tuple-element.13.turn_ref, f32[128,128]{1,0:T(8,128)S(1)} %get-tuple-element.14.upper_ref, ...), custom_call_target="tpu_custom_call" | custom-call | tf_op jit(solution)/shard_map/pallas_call | solution.py:374
  (15 shorter events, 0.1 us)
Async XLA Ops:
  0.6 6.3 %copy-start.3 = (s32[256,1]{0,1:T(1,128)S(1)}, s32[256,1]{0,1:T(1,128)}, u32[]{:S(2)}) copy-start(s32[256,1]{0,1:T(1,128)} %param.10) | copy-start | bytes 3076
  0.6 6.3 %copy-start.2 = (s32[256]{0:T(256)S(1)}, s32[256]{0:T(256)}, u32[]{:S(2)}) copy-start(s32[256]{0:T(256)} %param.11) | copy-start | bytes 3076
  0.7 62.9 %copy-start.1 = (f32[1024]{0:T(1024)S(1)}, f32[1024]{0:T(1024)}, u32[]{:S(2)}) copy-start(f32[1024]{0:T(1024)} %param.9) | copy-start | bytes 12292
  0.7 62.9 %copy-start.4 = (f32[64]{0:T(128)S(1)}, f32[64]{0:T(128)}, u32[]{:S(2)}) copy-start(f32[64]{0:T(128)} %param.12) | copy-start | bytes 772
  0.7 64.7 %copy-start = (bf16[1024,1024]{1,0:T(8,128)(2,1)S(1)}, bf16[1024,1024]{1,0:T(8,128)(2,1)}, u32[]{:S(2)}) copy-start(bf16[1024,1024]{1,0:T(8,128)(2,1)} %points_ref.3) | copy-start | bytes 6291460
  2.6 12.9 %all-to-all-start = ((bf16[8,176,128]{2,1,0:T(8,128)(2,1)}), bf16[8,176,128]{2,1,0:T(8,128)(2,1)S(1)}, u32[]{:S(2)}, u32[]{:S(2)}) async-start(bf16[8,176,128]{2,1,0:T(8,128)(2,1)} %shard_map.86), calls=%async_computation | async-start | bytes 720896 | tf_op jit(solution)/shard_map/all_to_all | solution.py:298
  16.7 34.1 %all-to-all-start.1 = ((bf16[64,8,128]{2,1,0:T(8,128)(2,1)}), bf16[64,8,128]{2,1,0:T(8,128)(2,1)S(1)}, u32[]{:S(2)}, u32[]{:S(2)}) async-start(bf16[64,8,128]{2,1,0:T(8,128)(2,1)} %bitcast.5), calls=%async_computation.1 | async-start | bytes 262144 | tf_op jit(solution)/shard_map/all_to_all | solution.py:308
  61.6 3.8 %collective-permute-start = (bf16[4,512,128]{2,1,0:T(8,128)(2,1)S(1)}, bf16[4,512,128]{2,1,0:T(8,128)(2,1)S(1)}, u32[]{:S(2)}, u32[]{:S(2)}) collective-permute-start(bf16[4,512,128]{2,1,0:T(8,128)(2,1)S(1)} %all_to_all.41.own_ref), channel_id=1, source_target_pairs={{0,1},{1,0},{2,3},{3,2},{4,5},{5,4},{6,7},{7,6},{8,9},{9,8},{10,11... | collective-permute-start | bytes 1572872 | tf_op jit(solution)/shard_map/ppermute | solution.py:327
  104.0 20.1 %all-to-all-start.5 = ((f32[16,24,128]{2,1,0:T(8,128)}), f32[16,24,128]{2,1,0:T(8,128)S(1)}, u32[]{:S(2)}, u32[]{:S(2)}) async-start(f32[16,24,128]{2,1,0:T(8,128)} %shard_map.91), calls=%async_computation.5 | async-start | bytes 393216 | tf_op jit(solution)/shard_map/all_to_all | solution.py:352
  125.0 11.5 %all-to-all-start.6 = ((f32[4,16,16,128]{3,2,1,0:T(8,128)}), f32[4,16,16,128]{3,2,1,0:T(8,128)S(1)}, u32[]{:S(2)}, u32[]{:S(2)}) async-start(f32[4,16,16,128]{3,2,1,0:T(8,128)} %broadcast_in_dim.3), calls=%async_computation.6 | async-start | bytes 1048576 | tf_op jit(solution)/shard_map/all_to_all | solution.py:51

commit v6 on v5

--- a/solution.py
+++ b/solution.py
@@ -18,7 +18,8 @@
 SLOTS = 2 * CAP
 STEP = 4
 Y, Z = 4, 16
-F32, BF16 = jnp.float32, jnp.bfloat16
+F32, BF16, F16 = jnp.float32, jnp.bfloat16, jnp.float16
+TOP = 14
 HIGHEST = lax.Precision.HIGHEST
 VMEM_LIMIT = 20 * 2**20
 
@@ -162,20 +163,61 @@
             sums_ref[member, start : start + WIDE] = cross[:, at : at + LANES]
 
 
+def exponent(values):
+    largest = jnp.max(jnp.max(jnp.abs(values), axis=0, keepdims=True), axis=1, keepdims=True)
+    return jnp.floor(jnp.log2(jnp.maximum(largest, 1e-30)))
+
+
+def exponent_place(shape, which):
+    return (iota(shape, 0) % 8 == which) & (iota(shape, 1) == LANES - 1)
+
+
+def scaled(cross, gram):
+    of_cross, of_gram = exponent(cross), exponent(gram)
+    gram = gram * jnp.exp2(TOP - of_gram)
+    gram = jnp.where(exponent_place(gram.shape, 0), of_cross, gram)
+    gram = jnp.where(exponent_place(gram.shape, 1), of_gram, gram)
+    return cross * jnp.exp2(TOP - of_cross), gram
+
+
+def unscaled_cross(ref, at, own):
+    return ref[at, 0:own] * jnp.exp2(ref[at, own : own + 1, LANES - 1 : LANES] - TOP)
+
+
+def unscaled_gram(ref, at, own):
+    return ref[at, own:] * jnp.exp2(ref[at, own + 1 : own + 2, LANES - 1 : LANES] - TOP)
+
+
 def near_kernel(got_ref, out_ref):
     total = jnp.sum(got_ref[...].astype(F32), axis=0)
     count, length, _ = out_ref.shape
     own_rows = total.shape[0] - 2 * WIDE
     own = own_rows // count
     gram = total[own_rows : own_rows + WIDE] + total[own_rows + WIDE :]
-    out_ref[:, 0:own] = total[:own_rows].reshape(count, own, LANES)
+    cross, gram = scaled(total[:own_rows], gram)
+    out_ref[:, 0:own] = cross.reshape(count, own, LANES)
     out_ref[:, own:length] = gram.reshape(count, length - own, LANES)
 
 
 def far_kernel(got_ref, out_ref):
-    total = jnp.sum(got_ref[...], axis=0)
-    for copy in range(out_ref.shape[0]):
-        out_ref[copy] = total
+    own = out_ref.shape[0] - 8
+    cross = unscaled_cross(got_ref, 0, own)
+    gram = unscaled_gram(got_ref, 0, own)
+    for source in range(1, got_ref.shape[0]):
+        cross = cross + unscaled_cross(got_ref, source, own)
+        gram = gram + unscaled_gram(got_ref, source, own)
+    taken = exponent_place(gram.shape, 0) | exponent_place(gram.shape, 1)
+    cross, gram = scaled(cross, jnp.where(taken, 0.0, gram))
+    out_ref[0:own] = cross
+    out_ref[own:] = gram
+
+
+def spread_kernel(column_ref, out_ref):
+    own = out_ref.shape[2]
+    for at in range(column_ref.shape[0]):
+        cross = unscaled_cross(column_ref, at, own)
+        for copy in range(out_ref.shape[0]):
+            out_ref[copy, at] = cross
 
 
 def eliminated(gram, shift):
@@ -212,7 +254,10 @@
 def factor_kernel(gram_ref, ridge_ref, terms_ref, turn_ref, upper_ref):
     ridge = ridge_ref[0]
     count, length, _ = gram_ref.shape
-    gram = gram_ref[:, length - WIDE // count : length].reshape(WIDE, WIDE)
+    held = length - WIDE // count
+    gram = jnp.concatenate([unscaled_gram(gram_ref, at, held) for at in range(count)], axis=0)
+    taken = exponent_place(gram.shape, 0) | exponent_place(gram.shape, 1)
+    gram = jnp.where(taken, gram.T, gram)
     own = iota((PW, PW), 0) == iota((PW, PW), 1)
 
     def shift_of(a):
@@ -357,9 +402,11 @@
     length = own + WIDE // Z
     message = jax.ShapeDtypeStruct((Z, length, LANES), F32)
     summed = called(near_kernel, message, exchanged(sums, y_groups))
-    summed = called(far_kernel, message, exchanged(summed, z_groups))
-    column = exchanged(summed, z_groups)
-    total = to_each(column[:, :own], "rows", y_groups)
+    parts = exchanged(summed.astype(F16), z_groups).astype(F32)
+    summed = called(far_kernel, jax.ShapeDtypeStruct((length, LANES), F32), parts)
+    column = to_each(summed.astype(F16), "rows", z_groups).astype(F32)
+    copies = called(spread_kernel, jax.ShapeDtypeStruct((Y, Z, own, LANES), F32), column)
+    total = exchanged(copies, y_groups)
     total = total.reshape(owners, own, LANES)
 
     square = jax.ShapeDtypeStruct((WIDE, WIDE), F32)

time: 140 us -> 133 us (0.950)
  blocking collectives: 43.9 us -> 40.4 us
  waiting for transfers between devices: 43.1 us -> 39.7 us
    all_to_all x1, waiting for transfers between devices: 14.8 us -> 2.11 us  [exchanged(): lax.all_to_all(array, 'rows', split_axis=0, concat_axis=0, tiled=True, ax...]
    all_to_all x1, waiting for transfers between devices: 2.3 us -> 11.6 us  [to_each(): lax.all_to_all(copies, axis, split_axis=0, concat_axis=0, tiled=True, axi...]
    all_to_all x2, blocking collectives: 33.5 us -> 29.9 us  [exchanged(): lax.all_to_all(array, 'rows', split_axis=0, concat_axis=0, tiled=True, ax...]
    pallas_call x4 -> x5, Pallas kernels: 2.33 us -> 2.92 us  [called(): pl.pallas_call(kernel, out_shape=out_shape, compiler_params=pltpu.Compile...]
where the time goes in v6:
time: 133 us
  blocking collectives  40.4 us (30%)
  waiting for transfers between devices  39.7 us (30%)
  starting transfers between devices  32.6 us (25%)
  Pallas kernels  17.6 us (13%)
  between operations  1.5 us (1%)
    all_to_all x2, blocking collectives, exchanged(): lax.all_to_all(array, 'rows', split_axis=0, concat_axis=0, tiled=True, ax...  29.9 us
    all_to_all x1, starting transfers between devices, body(): lax.all_to_all(packed, 'rows', split_axis=0, concat_axis=0, tiled=True)  18.4 us
    all_to_all x1, waiting for transfers between devices, body(): lax.all_to_all(packed, 'rows', split_axis=0, concat_axis=0, tiled=True)  15.7 us
    all_to_all x1, waiting for transfers between devices, to_each(): lax.all_to_all(copies, axis, split_axis=0, concat_axis=0, tiled=True, axi...  11.6 us
    all_to_all x1, blocking collectives, body(): lax.all_to_all(slot_rows, 'cols', split_axis=0, concat_axis=0, tiled=True...  10.5 us
    all_to_all x1, waiting for transfers between devices, body(): got = lax.all_to_all(sent, 'cols', split_axis=0, concat_axis=0, tiled=True)  8.55 us
    pallas_call x1, Pallas kernels, body(): pl.pallas_call(factor_kernel, out_shape=(square, square, square), in_spec...  5.93 us
    all_to_all x1, starting transfers between devices, to_each(): lax.all_to_all(copies, axis, split_axis=0, concat_axis=0, tiled=True, axi...  4.52 us
  transfers between devices with their start and end apart: 5, of which 5 were waited for; matrix products, arithmetic and copies ran while one was open for 0% of the time, Pallas kernels for 4%

profile of v6, /device:TPU:32, one launch (start us, length us, event | category | flops | bytes accessed | tf_op | source)
XLA Modules:
  0.0 132.6 jit_solution(12510740385892403851)
XLA Ops:
  0.7 1.9 %shard_map.86 = bf16[8,176,128]{2,1,0:T(8,128)(2,1)} custom-call(bf16[32,1024]{1,0:T(8,128)(2,1)} %env_ref.1, bf16[1024,1024]{1,0:T(8,128)(2,1)} %points_ref.3, f32[1,1024]{1,0:T(1,128)} %bitcast.15), custom_call_target="tpu_custom_call" | custom-call | tf_op jit(solution)/shard_map/pallas_call | solution.py:331
  2.6 4.3 %all-to-all-start = ((bf16[8,176,128]{2,1,0:T(8,128)(2,1)}), bf16[8,176,128]{2,1,0:T(8,128)(2,1)S(1)}, u32[]{:S(2)}, u32[]{:S(2)}) async-start(bf16[8,176,128]{2,1,0:T(8,128)(2,1)} %shard_map.86), calls=%async_computation | async-start | bytes 720896 | tf_op jit(solution)/shard_map/all_to_all | solution.py:343
  6.9 8.6 %all-to-all-done.env_ref = bf16[8,176,128]{2,1,0:T(8,128)(2,1)S(1)} async-done(((bf16[8,176,128]{2,1,0:T(8,128)(2,1)}), bf16[8,176,128]{2,1,0:T(8,128)(2,1)S(1)}, u32[]{:S(2)}, u32[]{:S(2)}) %all-to-all-start) | async-done | bytes 360480 | tf_op jit(solution)/shard_map/all_to_all | solution.py:343
  15.5 1.2 shard_map.87
  16.7 18.4 %all-to-all-start.1 = ((bf16[64,8,128]{2,1,0:T(8,128)(2,1)}), bf16[64,8,128]{2,1,0:T(8,128)(2,1)S(1)}, u32[]{:S(2)}, u32[]{:S(2)}) async-start(bf16[64,8,128]{2,1,0:T(8,128)(2,1)} %bitcast.5), calls=%async_computation.1 | async-start | bytes 262144 | tf_op jit(solution)/shard_map/all_to_all | solution.py:353
  35.1 15.7 %all-to-all-done.1 = bf16[64,8,128]{2,1,0:T(8,128)(2,1)S(1)} async-done(((bf16[64,8,128]{2,1,0:T(8,128)(2,1)}), bf16[64,8,128]{2,1,0:T(8,128)(2,1)S(1)}, u32[]{:S(2)}, u32[]{:S(2)}) %all-to-all-start.1) | async-done | bytes 131104 | tf_op jit(solution)/shard_map/all_to_all | solution.py:353
  50.8 0.3 shard_map.88
  51.1 10.5 %all_to_all.41.own_ref = bf16[4,512,128]{2,1,0:T(8,128)(2,1)S(1)} all-to-all(bf16[4,512,128]{2,1,0:T(8,128)(2,1)S(1)} %get-tuple-element.9), channel_id=1, replica_groups={{0,2,4,6},{1,3,5,7},{8,10,12,14},{9,11,13,15},{16,18,20,22},{17,19,21,2..., dimensions={0} | all-to-all | bytes 1048576 | tf_op jit(solution)/shard_map/all_to_all | solution.py:364
  61.6 1.9 %collective-permute-start = (bf16[4,512,128]{2,1,0:T(8,128)(2,1)S(1)}, bf16[4,512,128]{2,1,0:T(8,128)(2,1)S(1)}, u32[]{:S(2)}, u32[]{:S(2)}) collective-permute-start(bf16[4,512,128]{2,1,0:T(8,128)(2,1)S(1)} %all_to_all.41.own_ref), channel_id=1, source_target_pairs={{0,1},{1,0},{2,3},{3,2},{4,5},{5,4},{6,7},{7,6},{8,9},{9,8},{10,11... | collective-permute-start | bytes 1572872 | tf_op jit(solution)/shard_map/ppermute | solution.py:372
  63.6 1.8 %collective-permute-done.other_ref = bf16[4,512,128]{2,1,0:T(8,128)(2,1)S(1)} collective-permute-done((bf16[4,512,128]{2,1,0:T(8,128)(2,1)S(1)}, bf16[4,512,128]{2,1,0:T(8,128)(2,1)S(1)}, u32[]{:S(2)}, u32[]{:S(2)}) %collective-permute-start) | collective-permute-done | bytes 524320 | tf_op jit(solution)/shard_map/ppermute | solution.py:372
  65.4 0.0 copy-done
  65.4 4.4 %shard_map.89 = (f32[64,1152]{1,0:T(8,128)S(1)}, bf16[4,512,128]{2,1,0:T(8,128)(2,1)S(1)}) custom-call(s32[1]{0:T(128)} %bitcast.1.core_ref, bf16[4,512,128]{2,1,0:T(8,128)(2,1)S(1)} %all_to_all.41.own_ref, bf16[4,512,128]{2,1,0:T(8,128)(2,1)S(1)} %collective-permute-done.other_ref, bf16[64,128]{1,0:T(8,128)(2,1)S(1)} %get-tuple-element.10.label_ref, ...), custom_call_target="tpu_custom_call" | custom-call | tf_op jit(solution)/shard_map/pallas_call | solution.py:377
  69.8 12.9 %all_to_all.42.got_ref = bf16[4,512,128]{2,1,0:T(8,128)(2,1)S(1)} all-to-all(bf16[4,512,128]{2,1,0:T(8,128)(2,1)S(1)} %get-tuple-element.11), channel_id=1, replica_groups={{0,128,256,384},{8,136,264,392},{16,144,272,400},{24,152,280,408},{32,1..., dimensions={0} | all-to-all | bytes 1048576 | tf_op jit(solution)/shard_map/all_to_all | solution.py:397
  82.7 0.2 shard_map.90
  82.9 17.0 %all_to_all.43 = f16[16,24,128]{2,1,0:T(8,128)(2,1)S(1)} all-to-all(f16[16,24,128]{2,1,0:T(8,128)(2,1)S(1)} %convert_element_type.12), channel_id=1, replica_groups={{0,8,16,24,32,40,48,56,64,72,80,88,96,104,112,120},{128,136,144,152,160..., dimensions={0} | all-to-all | bytes 196608 | tf_op jit(solution)/shard_map/all_to_all | solution.py:397
  99.9 0.2 shard_map.91
  100.2 0.7 broadcast_in_dim.3
  100.8 4.5 %all-to-all-start.5 = ((f16[16,24,128]{2,1,0:T(8,128)(2,1)}), f16[16,24,128]{2,1,0:T(8,128)(2,1)S(1)}, u32[]{:S(2)}, u32[]{:S(2)}) async-start(f16[16,24,128]{2,1,0:T(8,128)(2,1)} %broadcast_in_dim.3), calls=%async_computation.5 | async-start | bytes 196608 | tf_op jit(solution)/shard_map/all_to_all | solution.py:52
  106.0 11.6 %all-to-all-done.5 = f16[16,24,128]{2,1,0:T(8,128)(2,1)S(1)} async-done(((f16[16,24,128]{2,1,0:T(8,128)(2,1)}), f16[16,24,128]{2,1,0:T(8,128)(2,1)S(1)}, u32[]{:S(2)}, u32[]{:S(2)}) %all-to-all-start.5) | async-done | bytes 98336 | tf_op jit(solution)/shard_map/all_to_all | solution.py:52
  117.6 0.9 shard_map.92
  118.5 3.5 %all-to-all-start.6 = ((f32[4,16,16,128]{3,2,1,0:T(8,128)}), f32[4,16,16,128]{3,2,1,0:T(8,128)S(1)}, u32[]{:S(2)}, u32[]{:S(2)}) async-start(f32[4,16,16,128]{3,2,1,0:T(8,128)} %shard_map.92), calls=%async_computation.6 | async-start | bytes 1048576 | tf_op jit(solution)/shard_map/all_to_all | solution.py:397
  122.0 5.9 %shard_map.93 = (f32[128,128]{1,0:T(8,128)S(1)}, f32[128,128]{1,0:T(8,128)S(1)}, f32[128,128]{1,0:T(8,128)S(1)}) custom-call(f32[16,24,128]{2,1,0:T(8,128)S(1)} %convert_element_type.15.column_ref.gram_ref, f32[1]{0:T(128)S(6)} %copy.9.ridge_ref), custom_call_target="tpu_custom_call" | custom-call | flops 8000000000 | bytes 262144 | tf_op jit(solution)/shard_map/pallas_call | solution.py:413
  128.0 2.1 %all-to-all-done.6 = f32[4,16,16,128]{3,2,1,0:T(8,128)S(1)} async-done(((f32[4,16,16,128]{3,2,1,0:T(8,128)}), f32[4,16,16,128]{3,2,1,0:T(8,128)S(1)}, u32[]{:S(2)}, u32[]{:S(2)}) %all-to-all-start.6) | async-done | bytes 524320 | tf_op jit(solution)/shard_map/all_to_all | solution.py:397
  130.1 2.5 %shard_map.94 = (f32[128,1024]{1,0:T(8,128)}, f32[64,1024]{1,0:T(8,128)}) custom-call(s32[1]{0:T(128)} %bitcast.first_ref, f32[64,16,128]{2,1,0:T(8,128)S(1)} %bitcast.12, f32[128,128]{1,0:T(8,128)S(1)} %get-tuple-element.12.terms_ref, f32[128,128]{1,0:T(8,128)S(1)} %get-tuple-element.13.turn_ref, f32[128,128]{1,0:T(8,128)S(1)} %get-tuple-element.14.upper_ref, ...), custom_call_target="tpu_custom_call" | custom-call | tf_op jit(solution)/shard_map/pallas_call | solution.py:421
  (19 shorter events, 0.1 us)
Async XLA Ops:
  0.6 6.3 %copy-start.3 = (s32[256,1]{0,1:T(1,128)S(1)}, s32[256,1]{0,1:T(1,128)}, u32[]{:S(2)}) copy-start(s32[256,1]{0,1:T(1,128)} %param.10) | copy-start | bytes 3076
  0.6 6.3 %copy-start.2 = (s32[256]{0:T(256)S(1)}, s32[256]{0:T(256)}, u32[]{:S(2)}) copy-start(s32[256]{0:T(256)} %param.11) | copy-start | bytes 3076
  0.7 62.9 %copy-start.1 = (f32[1024]{0:T(1024)S(1)}, f32[1024]{0:T(1024)}, u32[]{:S(2)}) copy-start(f32[1024]{0:T(1024)} %param.9) | copy-start | bytes 12292
  0.7 62.9 %copy-start.4 = (f32[64]{0:T(128)S(1)}, f32[64]{0:T(128)}, u32[]{:S(2)}) copy-start(f32[64]{0:T(128)} %param.12) | copy-start | bytes 772
  0.7 64.7 %copy-start = (bf16[1024,1024]{1,0:T(8,128)(2,1)S(1)}, bf16[1024,1024]{1,0:T(8,128)(2,1)}, u32[]{:S(2)}) copy-start(bf16[1024,1024]{1,0:T(8,128)(2,1)} %points_ref.3) | copy-start | bytes 6291460
  2.6 12.9 %all-to-all-start = ((bf16[8,176,128]{2,1,0:T(8,128)(2,1)}), bf16[8,176,128]{2,1,0:T(8,128)(2,1)S(1)}, u32[]{:S(2)}, u32[]{:S(2)}) async-start(bf16[8,176,128]{2,1,0:T(8,128)(2,1)} %shard_map.86), calls=%async_computation | async-start | bytes 720896 | tf_op jit(solution)/shard_map/all_to_all | solution.py:343
  16.7 34.1 %all-to-all-start.1 = ((bf16[64,8,128]{2,1,0:T(8,128)(2,1)}), bf16[64,8,128]{2,1,0:T(8,128)(2,1)S(1)}, u32[]{:S(2)}, u32[]{:S(2)}) async-start(bf16[64,8,128]{2,1,0:T(8,128)(2,1)} %bitcast.5), calls=%async_computation.1 | async-start | bytes 262144 | tf_op jit(solution)/shard_map/all_to_all | solution.py:353
  61.6 3.8 %collective-permute-start = (bf16[4,512,128]{2,1,0:T(8,128)(2,1)S(1)}, bf16[4,512,128]{2,1,0:T(8,128)(2,1)S(1)}, u32[]{:S(2)}, u32[]{:S(2)}) collective-permute-start(bf16[4,512,128]{2,1,0:T(8,128)(2,1)S(1)} %all_to_all.41.own_ref), channel_id=1, source_target_pairs={{0,1},{1,0},{2,3},{3,2},{4,5},{5,4},{6,7},{7,6},{8,9},{9,8},{10,11... | collective-permute-start | bytes 1572872 | tf_op jit(solution)/shard_map/ppermute | solution.py:372
  100.8 16.8 %all-to-all-start.5 = ((f16[16,24,128]{2,1,0:T(8,128)(2,1)}), f16[16,24,128]{2,1,0:T(8,128)(2,1)S(1)}, u32[]{:S(2)}, u32[]{:S(2)}) async-start(f16[16,24,128]{2,1,0:T(8,128)(2,1)} %broadcast_in_dim.3), calls=%async_computation.5 | async-start | bytes 196608 | tf_op jit(solution)/shard_map/all_to_all | solution.py:52
  118.5 11.5 %all-to-all-start.6 = ((f32[4,16,16,128]{3,2,1,0:T(8,128)}), f32[4,16,16,128]{3,2,1,0:T(8,128)S(1)}, u32[]{:S(2)}, u32[]{:S(2)}) async-start(f32[4,16,16,128]{3,2,1,0:T(8,128)} %shard_map.92), calls=%async_computation.6 | async-start | bytes 1048576 | tf_op jit(solution)/shard_map/all_to_all | solution.py:397

commit v7 on v6

--- a/solution.py
+++ b/solution.py
@@ -28,6 +28,16 @@
     return lax.dot_general(
         a, b, (dims, ((), ())), precision=precision, preferred_element_type=F32
     )
+
+
+def halves(a):
+    high = a.astype(BF16)
+    return high, (a - high.astype(F32)).astype(BF16)
+
+
+def dot3(a, b):
+    (ah, al), (bh, bl) = a, b
+    return dot(ah, bh) + (dot(ah, bl) + dot(al, bh))
 
 
 def iota(shape, dim):
@@ -132,7 +142,7 @@
     named = dot(source, label_ref[...])
     mine = iota((slots, LANES), 1) == iota((slots, LANES), 0) % SLOTS
     label = jnp.sum(jnp.where(mine, named, 0.0), axis=1, keepdims=True)
-    chosen = one_hot(label.astype(jnp.int32) == iota((slots, eqs), 1))
+    chosen = (label.astype(jnp.int32) == iota((slots, eqs), 1)).astype(F32).T.astype(BF16)
     diagonal = jnp.where(iota((eqs, eqs), 0) == iota((eqs, eqs), 1), scale_ref[:, cols:], 0.0)
     weight = jnp.sum(diagonal, axis=1, keepdims=True)
 
@@ -140,24 +150,26 @@
         z = dot(env_ref[0:slots, :], points, ((1,), (1,))) * dot_scale
         squared = z * z
         kernel = (scale * squared * squared).astype(BF16)
-        return dot(chosen, kernel, ((0,), (0,))) * weight
+        return dot(chosen, kernel) * weight
 
     parts = panel_ref[...].astype(F32)
     panel = block(env_ref[slots:rows, :], parts[0:1] + parts[1:2] + parts[2:3])
     matrix_ref[:, cols : cols + WIDE] = panel
-    gram = dot(panel, panel, ((0,), (0,)), HIGHEST)
-    high = gram.astype(BF16)
-    low = (gram - high.astype(F32)).astype(BF16)
+    turned = panel.T
+    gram = dot(turned, panel, precision=HIGHEST)
+    high, low = halves(gram[:PW])
+    last_high, last_low = halves(gram[PW:, PW:])
+    rest = jnp.concatenate([high, low, jnp.concatenate([last_high, last_low], axis=1)], axis=0)
     members, length, _ = sums_ref.shape
-    own_rows = length - 2 * WIDE
+    own_rows = length - 3 * PW
     for member in range(members):
-        sums_ref[member, own_rows : own_rows + WIDE] = high
-        sums_ref[member, own_rows + WIDE : length] = low
+        sums_ref[member, own_rows:length] = rest
+    turned = turned.astype(BF16)
     step = 256
     for first in range(0, cols, step):
         part = block(points_ref[first : first + step, :], scale_ref[:, first : first + step])
         matrix_ref[:, first : first + step] = part
-        cross = dot(panel, part, ((0,), (0,)), HIGHEST).astype(BF16)
+        cross = dot(turned, part.astype(BF16)).astype(BF16)
         for at in range(0, step, LANES):
             member, start = divmod((first + at) // LANES * WIDE, own_rows)
             sums_ref[member, start : start + WIDE] = cross[:, at : at + LANES]
@@ -191,9 +203,13 @@
 def near_kernel(got_ref, out_ref):
     total = jnp.sum(got_ref[...].astype(F32), axis=0)
     count, length, _ = out_ref.shape
-    own_rows = total.shape[0] - 2 * WIDE
+    own_rows = total.shape[0] - 3 * PW
     own = own_rows // count
-    gram = total[own_rows : own_rows + WIDE] + total[own_rows + WIDE :]
+    upper = total[own_rows : own_rows + PW] + total[own_rows + PW : own_rows + 2 * PW]
+    last = total[own_rows + 2 * PW :]
+    last = last[:, :PW] + last[:, PW:]
+    lower = jnp.concatenate([upper.T[PW:], last], axis=1)
+    gram = jnp.concatenate([upper, lower], axis=0)
     cross, gram = scaled(total[:own_rows], gram)
     out_ref[:, 0:own] = cross.reshape(count, own, LANES)
     out_ref[:, own:length] = gram.reshape(count, length - own, LANES)
@@ -295,8 +311,9 @@
 ):
     first = first_ref[0] == 0
     cols = reduced_ref.shape[1]
-    terms = terms_ref[...]
+    terms = halves(terms_ref[...])
     q = dot(matrix_ref[:, cols : cols + WIDE], turn_ref[...], ((1,), (1,)), HIGHEST)
+    q_parts = halves(q)
     step = 256
     for k in range(cols // step):
         at = slice(k * step, (k + 1) * step)
@@ -307,9 +324,9 @@
             ],
             axis=1,
         )
-        coupled = dot(terms, cross, precision=HIGHEST)
+        coupled = dot3(terms, halves(cross))
         r_ref[:, at] = coupled * norm_scale
-        reduced_ref[:, at] = matrix_ref[:, at] - dot(q, coupled, precision=HIGHEST)
+        reduced_ref[:, at] = matrix_ref[:, at] - dot3(q_parts, halves(coupled))
 
     @pl.when(first)
     def _():
@@ -378,7 +395,7 @@
         equations_kernel,
         out_shape=(
             jax.ShapeDtypeStruct((eqs, cols + WIDE), F32),
-            jax.ShapeDtypeStruct((Y, own_rows + 2 * WIDE, LANES), BF16),
+            jax.ShapeDtypeStruct((Y, own_rows + 3 * PW, LANES), BF16),
         ),
         in_specs=[smem] + [vmem] * 6,
         out_specs=(vmem, vmem),

time: 133 us -> 132 us (level)
  transfers between devices with their start and end apart: 5 -> 5, of which waited for: 5 -> 5; matrix products, arithmetic and copies ran while one was open for 0% -> 0% of each run, Pallas kernels for 4% -> 5%
where the time goes in v7:
time: 132 us; the launch traced here: 131 us
  blocking collectives  40 us (30%)
  waiting for transfers between devices  39.7 us (30%)
  starting transfers between devices  32.3 us (24%)
  Pallas kernels  17.2 us (13%)
  between operations  1.5 us (1%)
    all_to_all x2, blocking collectives, exchanged(): lax.all_to_all(array, 'rows', split_axis=0, concat_axis=0, tiled=True, ax...  29.5 us
    all_to_all x1, starting transfers between devices, body(): lax.all_to_all(packed, 'rows', split_axis=0, concat_axis=0, tiled=True)  18.4 us
    all_to_all x1, waiting for transfers between devices, body(): lax.all_to_all(packed, 'rows', split_axis=0, concat_axis=0, tiled=True)  15.7 us
    all_to_all x1, waiting for transfers between devices, to_each(): lax.all_to_all(copies, axis, split_axis=0, concat_axis=0, tiled=True, axi...  11.6 us
    all_to_all x1, blocking collectives, body(): lax.all_to_all(slot_rows, 'cols', split_axis=0, concat_axis=0, tiled=True...  10.5 us
    all_to_all x1, waiting for transfers between devices, body(): got = lax.all_to_all(sent, 'cols', split_axis=0, concat_axis=0, tiled=True)  8.55 us
    pallas_call x1, Pallas kernels, body(): pl.pallas_call(factor_kernel, out_shape=(square, square, square), in_spec...  5.93 us
    all_to_all x1, starting transfers between devices, body(): got = lax.all_to_all(sent, 'cols', split_axis=0, concat_axis=0, tiled=True)  4.3 us
  transfers between devices with their start and end apart: 5, of which 5 were waited for; matrix products, arithmetic and copies ran while one was open for 0% of the time, Pallas kernels for 5%

profile of v7, /device:TPU:32, one launch (start us, length us, event | category | flops | bytes accessed | tf_op | source)
XLA Modules:
  0.0 131.5 jit_solution(13132274462317565040)
XLA Ops:
  0.7 1.9 %shard_map.86 = bf16[8,176,128]{2,1,0:T(8,128)(2,1)} custom-call(bf16[32,1024]{1,0:T(8,128)(2,1)} %env_ref.1, bf16[1024,1024]{1,0:T(8,128)(2,1)} %points_ref.3, f32[1,1024]{1,0:T(1,128)} %bitcast.15), custom_call_target="tpu_custom_call" | custom-call | tf_op jit(solution)/shard_map/pallas_call | solution.py:348
  2.6 4.3 %all-to-all-start = ((bf16[8,176,128]{2,1,0:T(8,128)(2,1)}), bf16[8,176,128]{2,1,0:T(8,128)(2,1)S(1)}, u32[]{:S(2)}, u32[]{:S(2)}) async-start(bf16[8,176,128]{2,1,0:T(8,128)(2,1)} %shard_map.86), calls=%async_computation | async-start | bytes 720896 | tf_op jit(solution)/shard_map/all_to_all | solution.py:360
  6.9 8.6 %all-to-all-done.env_ref = bf16[8,176,128]{2,1,0:T(8,128)(2,1)S(1)} async-done(((bf16[8,176,128]{2,1,0:T(8,128)(2,1)}), bf16[8,176,128]{2,1,0:T(8,128)(2,1)S(1)}, u32[]{:S(2)}, u32[]{:S(2)}) %all-to-all-start) | async-done | bytes 360480 | tf_op jit(solution)/shard_map/all_to_all | solution.py:360
  15.5 1.2 shard_map.87
  16.7 18.4 %all-to-all-start.1 = ((bf16[64,8,128]{2,1,0:T(8,128)(2,1)}), bf16[64,8,128]{2,1,0:T(8,128)(2,1)S(1)}, u32[]{:S(2)}, u32[]{:S(2)}) async-start(bf16[64,8,128]{2,1,0:T(8,128)(2,1)} %bitcast.5), calls=%async_computation.1 | async-start | bytes 262144 | tf_op jit(solution)/shard_map/all_to_all | solution.py:370
  35.1 15.7 %all-to-all-done.1 = bf16[64,8,128]{2,1,0:T(8,128)(2,1)S(1)} async-done(((bf16[64,8,128]{2,1,0:T(8,128)(2,1)}), bf16[64,8,128]{2,1,0:T(8,128)(2,1)S(1)}, u32[]{:S(2)}, u32[]{:S(2)}) %all-to-all-start.1) | async-done | bytes 131104 | tf_op jit(solution)/shard_map/all_to_all | solution.py:370
  50.8 0.3 shard_map.88
  51.1 10.5 %all_to_all.41.own_ref = bf16[4,512,128]{2,1,0:T(8,128)(2,1)S(1)} all-to-all(bf16[4,512,128]{2,1,0:T(8,128)(2,1)S(1)} %get-tuple-element.9), channel_id=1, replica_groups={{0,2,4,6},{1,3,5,7},{8,10,12,14},{9,11,13,15},{16,18,20,22},{17,19,21,2..., dimensions={0} | all-to-all | bytes 1048576 | tf_op jit(solution)/shard_map/all_to_all | solution.py:381
  61.6 1.9 %collective-permute-start = (bf16[4,512,128]{2,1,0:T(8,128)(2,1)S(1)}, bf16[4,512,128]{2,1,0:T(8,128)(2,1)S(1)}, u32[]{:S(2)}, u32[]{:S(2)}) collective-permute-start(bf16[4,512,128]{2,1,0:T(8,128)(2,1)S(1)} %all_to_all.41.own_ref), channel_id=1, source_target_pairs={{0,1},{1,0},{2,3},{3,2},{4,5},{5,4},{6,7},{7,6},{8,9},{9,8},{10,11... | collective-permute-start | bytes 1572872 | tf_op jit(solution)/shard_map/ppermute | solution.py:389
  63.6 1.8 %collective-permute-done.other_ref = bf16[4,512,128]{2,1,0:T(8,128)(2,1)S(1)} collective-permute-done((bf16[4,512,128]{2,1,0:T(8,128)(2,1)S(1)}, bf16[4,512,128]{2,1,0:T(8,128)(2,1)S(1)}, u32[]{:S(2)}, u32[]{:S(2)}) %collective-permute-start) | collective-permute-done | bytes 524320 | tf_op jit(solution)/shard_map/ppermute | solution.py:389
  65.4 0.0 copy-done
  65.4 4.1 %shard_map.89 = (f32[64,1152]{1,0:T(8,128)S(1)}, bf16[4,448,128]{2,1,0:T(8,128)(2,1)S(1)}) custom-call(s32[1]{0:T(128)} %bitcast.1.core_ref, bf16[4,512,128]{2,1,0:T(8,128)(2,1)S(1)} %all_to_all.41.own_ref, bf16[4,512,128]{2,1,0:T(8,128)(2,1)S(1)} %collective-permute-done.other_ref, bf16[64,128]{1,0:T(8,128)(2,1)S(1)} %get-tuple-element.10.label_ref, ...), custom_call_target="tpu_custom_call" | custom-call | tf_op jit(solution)/shard_map/pallas_call | solution.py:394
  69.5 12.2 %all_to_all.42.got_ref = bf16[4,448,128]{2,1,0:T(8,128)(2,1)S(1)} all-to-all(bf16[4,448,128]{2,1,0:T(8,128)(2,1)S(1)} %get-tuple-element.11), channel_id=1, replica_groups={{0,128,256,384},{8,136,264,392},{16,144,272,400},{24,152,280,408},{32,1..., dimensions={0} | all-to-all | bytes 917504 | tf_op jit(solution)/shard_map/all_to_all | solution.py:414
  81.7 0.3 shard_map.90
  82.1 17.3 %all_to_all.43 = f16[16,24,128]{2,1,0:T(8,128)(2,1)S(1)} all-to-all(f16[16,24,128]{2,1,0:T(8,128)(2,1)S(1)} %convert_element_type.12), channel_id=1, replica_groups={{0,8,16,24,32,40,48,56,64,72,80,88,96,104,112,120},{128,136,144,152,160..., dimensions={0} | all-to-all | bytes 196608 | tf_op jit(solution)/shard_map/all_to_all | solution.py:414
  99.4 0.2 shard_map.91
  99.7 0.7 broadcast_in_dim.3
  100.3 4.3 %all-to-all-start.5 = ((f16[16,24,128]{2,1,0:T(8,128)(2,1)}), f16[16,24,128]{2,1,0:T(8,128)(2,1)S(1)}, u32[]{:S(2)}, u32[]{:S(2)}) async-start(f16[16,24,128]{2,1,0:T(8,128)(2,1)} %broadcast_in_dim.3), calls=%async_computation.5 | async-start | bytes 196608 | tf_op jit(solution)/shard_map/all_to_all | solution.py:62
  105.2 11.6 %all-to-all-done.5 = f16[16,24,128]{2,1,0:T(8,128)(2,1)S(1)} async-done(((f16[16,24,128]{2,1,0:T(8,128)(2,1)}), f16[16,24,128]{2,1,0:T(8,128)(2,1)S(1)}, u32[]{:S(2)}, u32[]{:S(2)}) %all-to-all-start.5) | async-done | bytes 98336 | tf_op jit(solution)/shard_map/all_to_all | solution.py:62
  116.8 0.9 shard_map.92
  117.8 3.5 %all-to-all-start.6 = ((f32[4,16,16,128]{3,2,1,0:T(8,128)}), f32[4,16,16,128]{3,2,1,0:T(8,128)S(1)}, u32[]{:S(2)}, u32[]{:S(2)}) async-start(f32[4,16,16,128]{3,2,1,0:T(8,128)} %shard_map.92), calls=%async_computation.6 | async-start | bytes 1048576 | tf_op jit(solution)/shard_map/all_to_all | solution.py:414
  121.3 5.9 %shard_map.93 = (f32[128,128]{1,0:T(8,128)S(1)}, f32[128,128]{1,0:T(8,128)S(1)}, f32[128,128]{1,0:T(8,128)S(1)}) custom-call(f32[16,24,128]{2,1,0:T(8,128)S(1)} %convert_element_type.15.column_ref.gram_ref, f32[1]{0:T(128)S(6)} %copy.9.ridge_ref), custom_call_target="tpu_custom_call" | custom-call | flops 8000000000 | bytes 262144 | tf_op jit(solution)/shard_map/pallas_call | solution.py:430
  127.2 2.1 %all-to-all-done.6 = f32[4,16,16,128]{3,2,1,0:T(8,128)S(1)} async-done(((f32[4,16,16,128]{3,2,1,0:T(8,128)}), f32[4,16,16,128]{3,2,1,0:T(8,128)S(1)}, u32[]{:S(2)}, u32[]{:S(2)}) %all-to-all-start.6) | async-done | bytes 524320 | tf_op jit(solution)/shard_map/all_to_all | solution.py:414
  129.3 2.2 %shard_map.94 = (f32[128,1024]{1,0:T(8,128)}, f32[64,1024]{1,0:T(8,128)}) custom-call(s32[1]{0:T(128)} %bitcast.first_ref, f32[64,16,128]{2,1,0:T(8,128)S(1)} %bitcast.12, f32[128,128]{1,0:T(8,128)S(1)} %get-tuple-element.12.terms_ref, f32[128,128]{1,0:T(8,128)S(1)} %get-tuple-element.13.turn_ref, f32[128,128]{1,0:T(8,128)S(1)} %get-tuple-element.14.upper_ref, ...), custom_call_target="tpu_custom_call" | custom-call | tf_op jit(solution)/shard_map/pallas_call | solution.py:438
  (19 shorter events, 0.1 us)
Async XLA Ops:
  0.6 6.3 %copy-start.3 = (s32[256,1]{0,1:T(1,128)S(1)}, s32[256,1]{0,1:T(1,128)}, u32[]{:S(2)}) copy-start(s32[256,1]{0,1:T(1,128)} %param.10) | copy-start | bytes 3076
  0.6 6.3 %copy-start.2 = (s32[256]{0:T(256)S(1)}, s32[256]{0:T(256)}, u32[]{:S(2)}) copy-start(s32[256]{0:T(256)} %param.11) | copy-start | bytes 3076
  0.7 62.9 %copy-start.1 = (f32[1024]{0:T(1024)S(1)}, f32[1024]{0:T(1024)}, u32[]{:S(2)}) copy-start(f32[1024]{0:T(1024)} %param.9) | copy-start | bytes 12292
  0.7 62.9 %copy-start.4 = (f32[64]{0:T(128)S(1)}, f32[64]{0:T(128)}, u32[]{:S(2)}) copy-start(f32[64]{0:T(128)} %param.12) | copy-start | bytes 772
  0.7 64.7 %copy-start = (bf16[1024,1024]{1,0:T(8,128)(2,1)S(1)}, bf16[1024,1024]{1,0:T(8,128)(2,1)}, u32[]{:S(2)}) copy-start(bf16[1024,1024]{1,0:T(8,128)(2,1)} %points_ref.3) | copy-start | bytes 6291460
  2.6 12.9 %all-to-all-start = ((bf16[8,176,128]{2,1,0:T(8,128)(2,1)}), bf16[8,176,128]{2,1,0:T(8,128)(2,1)S(1)}, u32[]{:S(2)}, u32[]{:S(2)}) async-start(bf16[8,176,128]{2,1,0:T(8,128)(2,1)} %shard_map.86), calls=%async_computation | async-start | bytes 720896 | tf_op jit(solution)/shard_map/all_to_all | solution.py:360
  16.7 34.1 %all-to-all-start.1 = ((bf16[64,8,128]{2,1,0:T(8,128)(2,1)}), bf16[64,8,128]{2,1,0:T(8,128)(2,1)S(1)}, u32[]{:S(2)}, u32[]{:S(2)}) async-start(bf16[64,8,128]{2,1,0:T(8,128)(2,1)} %bitcast.5), calls=%async_computation.1 | async-start | bytes 262144 | tf_op jit(solution)/shard_map/all_to_all | solution.py:370
  61.6 3.8 %collective-permute-start = (bf16[4,512,128]{2,1,0:T(8,128)(2,1)S(1)}, bf16[4,512,128]{2,1,0:T(8,128)(2,1)S(1)}, u32[]{:S(2)}, u32[]{:S(2)}) collective-permute-start(bf16[4,512,128]{2,1,0:T(8,128)(2,1)S(1)} %all_to_all.41.own_ref), channel_id=1, source_target_pairs={{0,1},{1,0},{2,3},{3,2},{4,5},{5,4},{6,7},{7,6},{8,9},{9,8},{10,11... | collective-permute-start | bytes 1572872 | tf_op jit(solution)/shard_map/ppermute | solution.py:389
  100.3 16.5 %all-to-all-start.5 = ((f16[16,24,128]{2,1,0:T(8,128)(2,1)}), f16[16,24,128]{2,1,0:T(8,128)(2,1)S(1)}, u32[]{:S(2)}, u32[]{:S(2)}) async-start(f16[16,24,128]{2,1,0:T(8,128)(2,1)} %broadcast_in_dim.3), calls=%async_computation.5 | async-start | bytes 196608 | tf_op jit(solution)/shard_map/all_to_all | solution.py:62
  117.8 11.5 %all-to-all-start.6 = ((f32[4,16,16,128]{3,2,1,0:T(8,128)}), f32[4,16,16,128]{3,2,1,0:T(8,128)S(1)}, u32[]{:S(2)}, u32[]{:S(2)}) async-start(f32[4,16,16,128]{3,2,1,0:T(8,128)} %shard_map.92), calls=%async_computation.6 | async-start | bytes 1048576 | tf_op jit(solution)/shard_map/all_to_all | solution.py:414

commit v8 on v7

--- a/solution.py
+++ b/solution.py
@@ -228,14 +228,6 @@
     out_ref[own:] = gram
 
 
-def spread_kernel(column_ref, out_ref):
-    own = out_ref.shape[2]
-    for at in range(column_ref.shape[0]):
-        cross = unscaled_cross(column_ref, at, own)
-        for copy in range(out_ref.shape[0]):
-            out_ref[copy, at] = cross
-
-
 def eliminated(gram, shift):
     own = iota((PW, PW), 0) == iota((PW, PW), 1)
     eye = own.astype(F32)
@@ -311,6 +303,7 @@
 ):
     first = first_ref[0] == 0
     cols = reduced_ref.shape[1]
+    own = WIDE // 8
     terms = halves(terms_ref[...])
     q = dot(matrix_ref[:, cols : cols + WIDE], turn_ref[...], ((1,), (1,)), HIGHEST)
     q_parts = halves(q)
@@ -319,7 +312,9 @@
         at = slice(k * step, (k + 1) * step)
         cross = jnp.concatenate(
             [
-                total_ref[8 * j : 8 * j + 8].reshape(WIDE, LANES)
+                jnp.concatenate(
+                    [unscaled_cross(total_ref, at, own) for at in range(8 * j, 8 * j + 8)], axis=0
+                )
                 for j in range(k * step // LANES, (k + 1) * step // LANES)
             ],
             axis=1,
@@ -421,10 +416,8 @@
     summed = called(near_kernel, message, exchanged(sums, y_groups))
     parts = exchanged(summed.astype(F16), z_groups).astype(F32)
     summed = called(far_kernel, jax.ShapeDtypeStruct((length, LANES), F32), parts)
-    column = to_each(summed.astype(F16), "rows", z_groups).astype(F32)
-    copies = called(spread_kernel, jax.ShapeDtypeStruct((Y, Z, own, LANES), F32), column)
-    total = exchanged(copies, y_groups)
-    total = total.reshape(owners, own, LANES)
+    column = to_each(summed.astype(F16), "rows", z_groups)
+    total = to_each(column, "rows", y_groups).reshape(owners, length, LANES).astype(F32)
 
     square = jax.ShapeDtypeStruct((WIDE, WIDE), F32)
     terms, turn, upper = pl.pallas_call(
@@ -434,7 +427,7 @@
         out_specs=(vmem, vmem, vmem),
         compiler_params=params,
         cost_estimate=pl.CostEstimate(flops=8_000_000_000, bytes_accessed=262144, transcendentals=0),
-    )(column, ridge_factor)
+    )(column.astype(F32), ridge_factor)
     return pl.pallas_call(
         functools.partial(final_kernel, norm_scale=1.0 / math.sqrt(owners * eqs)),
         out_shape=(

time: 132 us -> 131 us (level)
    all_to_all x1 -> x0, starting transfers between devices: 3.47 us -> none  [exchanged(): lax.all_to_all(array, 'rows', split_axis=0, concat_axis=0, tiled=True, ax...]
    all_to_all x1 -> x2, starting transfers between devices: 4.26 us -> 7.72 us  [to_each(): lax.all_to_all(copies, axis, split_axis=0, concat_axis=0, tiled=True, axi...]
    all_to_all x1 -> x0, waiting for transfers between devices: 2.11 us -> none  [exchanged(): lax.all_to_all(array, 'rows', split_axis=0, concat_axis=0, tiled=True, ax...]
    all_to_all x1 -> x2, waiting for transfers between devices: 11.6 us -> 13 us  [to_each(): lax.all_to_all(copies, axis, split_axis=0, concat_axis=0, tiled=True, axi...]
    pallas_call x5 -> x4, Pallas kernels: 3.05 us -> 2.11 us  [called(): pl.pallas_call(kernel, out_shape=out_shape, compiler_params=pltpu.Compile...]
where the time goes in v8:
time: 131 us
  blocking collectives  40 us (31%)
  waiting for transfers between devices  39 us (30%)
  starting transfers between devices  32.3 us (25%)
  Pallas kernels  16.3 us (12%)
  between operations  1.5 us (1%)
  local copies, waits for them, and re-layouts  1.49 us (1%)
    all_to_all x2, blocking collectives, exchanged(): lax.all_to_all(array, 'rows', split_axis=0, concat_axis=0, tiled=True, ax...  29.5 us
    all_to_all x1, starting transfers between devices, body(): lax.all_to_all(packed, 'rows', split_axis=0, concat_axis=0, tiled=True)  18.4 us
    all_to_all x1, waiting for transfers between devices, body(): lax.all_to_all(packed, 'rows', split_axis=0, concat_axis=0, tiled=True)  15.7 us
    all_to_all x2, waiting for transfers between devices, to_each(): lax.all_to_all(copies, axis, split_axis=0, concat_axis=0, tiled=True, axi...  13 us
    all_to_all x1, blocking collectives, body(): lax.all_to_all(slot_rows, 'cols', split_axis=0, concat_axis=0, tiled=True...  10.5 us
    all_to_all x1, waiting for transfers between devices, body(): got = lax.all_to_all(sent, 'cols', split_axis=0, concat_axis=0, tiled=True)  8.55 us
    all_to_all x2, starting transfers between devices, to_each(): lax.all_to_all(copies, axis, split_axis=0, concat_axis=0, tiled=True, axi...  7.72 us
    pallas_call x1, Pallas kernels, body(): pl.pallas_call(factor_kernel, out_shape=(square, square, square), in_spec...  5.93 us
  transfers between devices with their start and end apart: 5, of which 5 were waited for; matrix products, arithmetic and copies ran while one was open for 0% of the time, Pallas kernels for 5%

profile of v8, /device:TPU:32, one launch (start us, length us, event | category | flops | bytes accessed | tf_op | source)
XLA Modules:
  0.0 130.7 jit_solution(10850772637379100015)
XLA Ops:
  0.7 1.9 %shard_map.86 = bf16[8,176,128]{2,1,0:T(8,128)(2,1)} custom-call(bf16[32,1024]{1,0:T(8,128)(2,1)} %env_ref.1, bf16[1024,1024]{1,0:T(8,128)(2,1)} %points_ref.3, f32[1,1024]{1,0:T(1,128)} %bitcast.16), custom_call_target="tpu_custom_call" | custom-call | tf_op jit(solution)/shard_map/pallas_call | solution.py:343
  2.6 4.3 %all-to-all-start = ((bf16[8,176,128]{2,1,0:T(8,128)(2,1)}), bf16[8,176,128]{2,1,0:T(8,128)(2,1)S(1)}, u32[]{:S(2)}, u32[]{:S(2)}) async-start(bf16[8,176,128]{2,1,0:T(8,128)(2,1)} %shard_map.86), calls=%async_computation | async-start | bytes 720896 | tf_op jit(solution)/shard_map/all_to_all | solution.py:355
  6.9 8.6 %all-to-all-done.env_ref = bf16[8,176,128]{2,1,0:T(8,128)(2,1)S(1)} async-done(((bf16[8,176,128]{2,1,0:T(8,128)(2,1)}), bf16[8,176,128]{2,1,0:T(8,128)(2,1)S(1)}, u32[]{:S(2)}, u32[]{:S(2)}) %all-to-all-start) | async-done | bytes 360480 | tf_op jit(solution)/shard_map/all_to_all | solution.py:355
  15.5 1.2 shard_map.87
  16.7 18.4 %all-to-all-start.1 = ((bf16[64,8,128]{2,1,0:T(8,128)(2,1)}), bf16[64,8,128]{2,1,0:T(8,128)(2,1)S(1)}, u32[]{:S(2)}, u32[]{:S(2)}) async-start(bf16[64,8,128]{2,1,0:T(8,128)(2,1)} %bitcast.5), calls=%async_computation.1 | async-start | bytes 262144 | tf_op jit(solution)/shard_map/all_to_all | solution.py:365
  35.1 15.7 %all-to-all-done.1 = bf16[64,8,128]{2,1,0:T(8,128)(2,1)S(1)} async-done(((bf16[64,8,128]{2,1,0:T(8,128)(2,1)}), bf16[64,8,128]{2,1,0:T(8,128)(2,1)S(1)}, u32[]{:S(2)}, u32[]{:S(2)}) %all-to-all-start.1) | async-done | bytes 131104 | tf_op jit(solution)/shard_map/all_to_all | solution.py:365
  50.8 0.3 shard_map.88
  51.1 10.5 %all_to_all.41.own_ref = bf16[4,512,128]{2,1,0:T(8,128)(2,1)S(1)} all-to-all(bf16[4,512,128]{2,1,0:T(8,128)(2,1)S(1)} %get-tuple-element.9), channel_id=1, replica_groups={{0,2,4,6},{1,3,5,7},{8,10,12,14},{9,11,13,15},{16,18,20,22},{17,19,21,2..., dimensions={0} | all-to-all | bytes 1048576 | tf_op jit(solution)/shard_map/all_to_all | solution.py:376
  61.6 1.9 %collective-permute-start = (bf16[4,512,128]{2,1,0:T(8,128)(2,1)S(1)}, bf16[4,512,128]{2,1,0:T(8,128)(2,1)S(1)}, u32[]{:S(2)}, u32[]{:S(2)}) collective-permute-start(bf16[4,512,128]{2,1,0:T(8,128)(2,1)S(1)} %all_to_all.41.own_ref), channel_id=1, source_target_pairs={{0,1},{1,0},{2,3},{3,2},{4,5},{5,4},{6,7},{7,6},{8,9},{9,8},{10,11... | collective-permute-start | bytes 1572872 | tf_op jit(solution)/shard_map/ppermute | solution.py:384
  63.6 1.8 %collective-permute-done.other_ref = bf16[4,512,128]{2,1,0:T(8,128)(2,1)S(1)} collective-permute-done((bf16[4,512,128]{2,1,0:T(8,128)(2,1)S(1)}, bf16[4,512,128]{2,1,0:T(8,128)(2,1)S(1)}, u32[]{:S(2)}, u32[]{:S(2)}) %collective-permute-start) | collective-permute-done | bytes 524320 | tf_op jit(solution)/shard_map/ppermute | solution.py:384
  65.4 4.1 %shard_map.89 = (f32[64,1152]{1,0:T(8,128)S(1)}, bf16[4,448,128]{2,1,0:T(8,128)(2,1)S(1)}) custom-call(s32[1]{0:T(128)} %bitcast.1.core_ref, bf16[4,512,128]{2,1,0:T(8,128)(2,1)S(1)} %all_to_all.41.own_ref, bf16[4,512,128]{2,1,0:T(8,128)(2,1)S(1)} %collective-permute-done.other_ref, bf16[64,128]{1,0:T(8,128)(2,1)S(1)} %get-tuple-element.10.label_ref, ...), custom_call_target="tpu_custom_call" | custom-call | tf_op jit(solution)/shard_map/pallas_call | solution.py:389
  69.5 12.2 %all_to_all.42.got_ref = bf16[4,448,128]{2,1,0:T(8,128)(2,1)S(1)} all-to-all(bf16[4,448,128]{2,1,0:T(8,128)(2,1)S(1)} %get-tuple-element.11), channel_id=1, replica_groups={{0,128,256,384},{8,136,264,392},{16,144,272,400},{24,152,280,408},{32,1..., dimensions={0} | all-to-all | bytes 917504 | tf_op jit(solution)/shard_map/all_to_all | solution.py:409
  81.7 0.3 shard_map.90
  82.1 17.3 %all_to_all.43 = f16[16,24,128]{2,1,0:T(8,128)(2,1)S(1)} all-to-all(f16[16,24,128]{2,1,0:T(8,128)(2,1)S(1)} %convert_element_type.17), channel_id=1, replica_groups={{0,8,16,24,32,40,48,56,64,72,80,88,96,104,112,120},{128,136,144,152,160..., dimensions={0} | all-to-all | bytes 196608 | tf_op jit(solution)/shard_map/all_to_all | solution.py:409
  99.4 0.2 shard_map.91
  99.7 0.7 broadcast_in_dim.6
  100.3 4.3 %all-to-all-start.5 = ((f16[16,24,128]{2,1,0:T(8,128)(2,1)}), f16[16,24,128]{2,1,0:T(8,128)(2,1)S(1)}, u32[]{:S(2)}, u32[]{:S(2)}) async-start(f16[16,24,128]{2,1,0:T(8,128)(2,1)} %broadcast_in_dim.6), calls=%async_computation.5 | async-start | bytes 196608 | tf_op jit(solution)/shard_map/all_to_all | solution.py:62
  105.2 11.6 %all-to-all-done.5 = f16[16,24,128]{2,1,0:T(8,128)(2,1)S(1)} async-done(((f16[16,24,128]{2,1,0:T(8,128)(2,1)}), f16[16,24,128]{2,1,0:T(8,128)(2,1)S(1)}, u32[]{:S(2)}, u32[]{:S(2)}) %all-to-all-start.5) | async-done | bytes 98336 | tf_op jit(solution)/shard_map/all_to_all | solution.py:62
  116.8 0.8 broadcast_in_dim.7
  117.6 3.5 %all-to-all-start.6 = ((f16[4,16,24,128]{3,2,1,0:T(8,128)(2,1)}), f16[4,16,24,128]{3,2,1,0:T(8,128)(2,1)S(1)}, u32[]{:S(2)}, u32[]{:S(2)}) async-start(f16[4,16,24,128]{3,2,1,0:T(8,128)(2,1)} %broadcast_in_dim.7), calls=%async_computation.6 | async-start | bytes 786432 | tf_op jit(solution)/shard_map/all_to_all | solution.py:62
  121.1 5.9 %shard_map.92 = (f32[128,128]{1,0:T(8,128)S(1)}, f32[128,128]{1,0:T(8,128)S(1)}, f32[128,128]{1,0:T(8,128)S(1)}) custom-call(f32[16,24,128]{2,1,0:T(8,128)S(1)} %convert_element_type.22.gram_ref, f32[1]{0:T(128)S(6)} %copy.9.ridge_ref), custom_call_target="tpu_custom_call" | custom-call | flops 8000000000 | bytes 262144 | tf_op jit(solution)/shard_map/pallas_call | solution.py:423
  127.0 1.4 %all-to-all-done.6 = f16[4,16,24,128]{3,2,1,0:T(8,128)(2,1)S(1)} async-done(((f16[4,16,24,128]{3,2,1,0:T(8,128)(2,1)}), f16[4,16,24,128]{3,2,1,0:T(8,128)(2,1)S(1)}, u32[]{:S(2)}, u32[]{:S(2)}) %all-to-all-start.6) | async-done | bytes 393248 | tf_op jit(solution)/shard_map/all_to_all | solution.py:62
  128.4 0.1 bitcast_convert_fusion.total_ref
  128.5 2.2 %shard_map.93 = (f32[128,1024]{1,0:T(8,128)}, f32[64,1024]{1,0:T(8,128)}) custom-call(s32[1]{0:T(128)} %bitcast.first_ref, f32[64,24,128]{2,1,0:T(8,128)S(1)} %bitcast_convert_fusion.total_ref, f32[128,128]{1,0:T(8,128)S(1)} %get-tuple-element.12.terms_ref, f32[128,128]{1,0:T(8,128)S(1)} %get-tuple-element.13.turn_ref, ...), custom_call_target="tpu_custom_call" | custom-call | tf_op jit(solution)/shard_map/pallas_call | solution.py:431
  (20 shorter events, 0.1 us)
Async XLA Ops:
  0.6 6.3 %copy-start.3 = (s32[256,1]{0,1:T(1,128)S(1)}, s32[256,1]{0,1:T(1,128)}, u32[]{:S(2)}) copy-start(s32[256,1]{0,1:T(1,128)} %param.10) | copy-start | bytes 3076
  0.6 6.3 %copy-start.2 = (s32[256]{0:T(256)S(1)}, s32[256]{0:T(256)}, u32[]{:S(2)}) copy-start(s32[256]{0:T(256)} %param.11) | copy-start | bytes 3076
  0.7 62.9 %copy-start.1 = (f32[1024]{0:T(1024)S(1)}, f32[1024]{0:T(1024)}, u32[]{:S(2)}) copy-start(f32[1024]{0:T(1024)} %param.9) | copy-start | bytes 12292
  0.7 62.9 %copy-start.4 = (f32[64]{0:T(128)S(1)}, f32[64]{0:T(128)}, u32[]{:S(2)}) copy-start(f32[64]{0:T(128)} %param.12) | copy-start | bytes 772
  0.7 64.7 %copy-start = (bf16[1024,1024]{1,0:T(8,128)(2,1)S(1)}, bf16[1024,1024]{1,0:T(8,128)(2,1)}, u32[]{:S(2)}) copy-start(bf16[1024,1024]{1,0:T(8,128)(2,1)} %points_ref.3) | copy-start | bytes 6291460
  2.6 12.9 %all-to-all-start = ((bf16[8,176,128]{2,1,0:T(8,128)(2,1)}), bf16[8,176,128]{2,1,0:T(8,128)(2,1)S(1)}, u32[]{:S(2)}, u32[]{:S(2)}) async-start(bf16[8,176,128]{2,1,0:T(8,128)(2,1)} %shard_map.86), calls=%async_computation | async-start | bytes 720896 | tf_op jit(solution)/shard_map/all_to_all | solution.py:355
  16.7 34.1 %all-to-all-start.1 = ((bf16[64,8,128]{2,1,0:T(8,128)(2,1)}), bf16[64,8,128]{2,1,0:T(8,128)(2,1)S(1)}, u32[]{:S(2)}, u32[]{:S(2)}) async-start(bf16[64,8,128]{2,1,0:T(8,128)(2,1)} %bitcast.5), calls=%async_computation.1 | async-start | bytes 262144 | tf_op jit(solution)/shard_map/all_to_all | solution.py:365
  61.6 3.8 %collective-permute-start = (bf16[4,512,128]{2,1,0:T(8,128)(2,1)S(1)}, bf16[4,512,128]{2,1,0:T(8,128)(2,1)S(1)}, u32[]{:S(2)}, u32[]{:S(2)}) collective-permute-start(bf16[4,512,128]{2,1,0:T(8,128)(2,1)S(1)} %all_to_all.41.own_ref), channel_id=1, source_target_pairs={{0,1},{1,0},{2,3},{3,2},{4,5},{5,4},{6,7},{7,6},{8,9},{9,8},{10,11... | collective-permute-start | bytes 1572872 | tf_op jit(solution)/shard_map/ppermute | solution.py:384
  100.3 16.5 %all-to-all-start.5 = ((f16[16,24,128]{2,1,0:T(8,128)(2,1)}), f16[16,24,128]{2,1,0:T(8,128)(2,1)S(1)}, u32[]{:S(2)}, u32[]{:S(2)}) async-start(f16[16,24,128]{2,1,0:T(8,128)(2,1)} %broadcast_in_dim.6), calls=%async_computation.5 | async-start | bytes 196608 | tf_op jit(solution)/shard_map/all_to_all | solution.py:62
  117.6 10.8 %all-to-all-start.6 = ((f16[4,16,24,128]{3,2,1,0:T(8,128)(2,1)}), f16[4,16,24,128]{3,2,1,0:T(8,128)(2,1)S(1)}, u32[]{:S(2)}, u32[]{:S(2)}) async-start(f16[4,16,24,128]{3,2,1,0:T(8,128)(2,1)} %broadcast_in_dim.7), calls=%async_computation.6 | async-start | bytes 786432 | tf_op jit(solution)/shard_map/all_to_all | solution.py:62

commit v9 on v8

--- a/solution.py
+++ b/solution.py
@@ -128,7 +128,7 @@
 ):
     chips, rows, _ = own_ref.shape
     slots = rows - WIDE
-    cols = points_ref.shape[0]
+    cols = points_ref.shape[1]
     eqs = scale_ref.shape[1] - cols
     core = core_ref[0]
     for chip in range(chips):
@@ -147,13 +147,13 @@
     weight = jnp.sum(diagonal, axis=1, keepdims=True)
 
     def block(points, scale):
-        z = dot(env_ref[0:slots, :], points, ((1,), (1,))) * dot_scale
+        z = dot(env_ref[0:slots, :], points) * dot_scale
         squared = z * z
         kernel = (scale * squared * squared).astype(BF16)
         return dot(chosen, kernel) * weight
 
     parts = panel_ref[...].astype(F32)
-    panel = block(env_ref[slots:rows, :], parts[0:1] + parts[1:2] + parts[2:3])
+    panel = block(env_ref[slots:rows, :].T, parts[0:1] + parts[1:2] + parts[2:3])
     matrix_ref[:, cols : cols + WIDE] = panel
     turned = panel.T
     gram = dot(turned, panel, precision=HIGHEST)
@@ -167,7 +167,7 @@
     turned = turned.astype(BF16)
     step = 256
     for first in range(0, cols, step):
-        part = block(points_ref[first : first + step, :], scale_ref[:, first : first + step])
+        part = block(points_ref[:, first : first + step], scale_ref[:, first : first + step])
         matrix_ref[:, first : first + step] = part
         cross = dot(turned, part.astype(BF16)).astype(BF16)
         for at in range(0, step, LANES):
@@ -362,7 +362,10 @@
         (env_owner[:, 0] * eqs + env_structure).reshape(1, envs),
     )
     col = lax.axis_index("cols")
+    packed, points = lax.optimization_barrier((packed, sparse_points))
+    points = points.T
     arrived = lax.all_to_all(packed, "rows", split_axis=0, concat_axis=0, tiled=True)
+    arrived, points = lax.optimization_barrier((arrived, points))
     slots = owners * SLOTS
     slot_rows, labels = called(
         unpack_kernel,
@@ -401,7 +404,7 @@
         own,
         other,
         labels,
-        sparse_points,
+        points,
         jnp.concatenate([point_scale, row_weight]).reshape(1, cols + eqs),
         parts,
     )

time: 131 us -> 131 us (level)
  waiting for transfers between devices: 39 us -> 36.1 us
  local copies, waits for them, and re-layouts: 1.49 us -> 4.36 us
    all_to_all x1, waiting for transfers between devices: 15.7 us -> 12.8 us  [body(): lax.all_to_all(packed, 'rows', split_axis=0, concat_axis=0, tiled=True)]
    optimization_barrier x0 -> x1, local copies, waits for them, and re-layouts: none -> 2.86 us  [body(): packed, points = lax.optimization_barrier((packed, sparse_points))]
  transfers between devices with their start and end apart: 5 -> 5, of which waited for: 5 -> 5; matrix products, arithmetic and copies ran while one was open for 0% -> 2% of each run, Pallas kernels for 5% -> 5%
where the time goes in v9:
time: 131 us; the launch traced here: 130 us
  blocking collectives  40 us (31%)
  waiting for transfers between devices  36.1 us (28%)
  starting transfers between devices  32.3 us (25%)
  Pallas kernels  16 us (12%)
  local copies, waits for them, and re-layouts  4.36 us (3%)
  between operations  1.5 us (1%)
    all_to_all x2, blocking collectives, exchanged(): lax.all_to_all(array, 'rows', split_axis=0, concat_axis=0, tiled=True, ax...  29.5 us
    all_to_all x1, starting transfers between devices, body(): lax.all_to_all(packed, 'rows', split_axis=0, concat_axis=0, tiled=True)  18.4 us
    all_to_all x2, waiting for transfers between devices, to_each(): lax.all_to_all(copies, axis, split_axis=0, concat_axis=0, tiled=True, axi...  13 us
    all_to_all x1, waiting for transfers between devices, body(): lax.all_to_all(packed, 'rows', split_axis=0, concat_axis=0, tiled=True)  12.8 us
    all_to_all x1, blocking collectives, body(): lax.all_to_all(slot_rows, 'cols', split_axis=0, concat_axis=0, tiled=True...  10.5 us
    all_to_all x1, waiting for transfers between devices, body(): got = lax.all_to_all(sent, 'cols', split_axis=0, concat_axis=0, tiled=True)  8.55 us
    all_to_all x2, starting transfers between devices, to_each(): lax.all_to_all(copies, axis, split_axis=0, concat_axis=0, tiled=True, axi...  7.72 us
    pallas_call x1, Pallas kernels, body(): pl.pallas_call(factor_kernel, out_shape=(square, square, square), in_spec...  5.93 us
  transfers between devices with their start and end apart: 5, of which 5 were waited for; matrix products, arithmetic and copies ran while one was open for 2% of the time, Pallas kernels for 5%

profile of v9, /device:TPU:32, one launch (start us, length us, event | category | flops | bytes accessed | tf_op | source)
XLA Modules:
  0.0 130.4 jit_solution(5406888585039888129)
XLA Ops:
  0.6 1.8 %shard_map.86 = bf16[8,176,128]{2,1,0:T(8,128)(2,1)} custom-call(bf16[32,1024]{1,0:T(8,128)(2,1)} %env_ref.1, bf16[1024,1024]{1,0:T(8,128)(2,1)} %points_ref.1, f32[1,1024]{1,0:T(1,128)} %bitcast.18), custom_call_target="tpu_custom_call" | custom-call | tf_op jit(solution)/shard_map/pallas_call | solution.py:343
  2.4 4.3 %all-to-all-start = ((bf16[8,176,128]{2,1,0:T(8,128)(2,1)}), bf16[8,176,128]{2,1,0:T(8,128)(2,1)S(1)}, u32[]{:S(2)}, u32[]{:S(2)}) async-start(bf16[8,176,128]{2,1,0:T(8,128)(2,1)} %shard_map.86), calls=%async_computation | async-start | bytes 720896 | tf_op jit(solution)/shard_map/all_to_all | solution.py:355
  6.7 8.6 %all-to-all-done.env_ref = bf16[8,176,128]{2,1,0:T(8,128)(2,1)S(1)} async-done(((bf16[8,176,128]{2,1,0:T(8,128)(2,1)}), bf16[8,176,128]{2,1,0:T(8,128)(2,1)S(1)}, u32[]{:S(2)}, u32[]{:S(2)}) %all-to-all-start) | async-done | bytes 360480 | tf_op jit(solution)/shard_map/all_to_all | solution.py:355
  15.3 1.2 shard_map.87
  16.5 18.4 %all-to-all-start.1 = ((bf16[64,8,128]{2,1,0:T(8,128)(2,1)}), bf16[64,8,128]{2,1,0:T(8,128)(2,1)S(1)}, u32[]{:S(2)}, u32[]{:S(2)}) async-start(bf16[64,8,128]{2,1,0:T(8,128)(2,1)} %bitcast.5), calls=%async_computation.1 | async-start | bytes 262144 | tf_op jit(solution)/shard_map/all_to_all | solution.py:367
  34.9 2.9 %copy.9 = bf16[1024,1024]{0,1:T(8,128)(2,1)S(1)} copy(bf16[1024,1024]{1,0:T(8,128)(2,1)} %points_ref.1) | data formatting | bytes 4194304 | tf_op jit(solution)/shard_map/optimization_barrier | solution.py:365
  37.8 12.8 %all-to-all-done.1 = bf16[64,8,128]{2,1,0:T(8,128)(2,1)S(1)} async-done(((bf16[64,8,128]{2,1,0:T(8,128)(2,1)}), bf16[64,8,128]{2,1,0:T(8,128)(2,1)S(1)}, u32[]{:S(2)}, u32[]{:S(2)}) %all-to-all-start.1) | async-done | bytes 131104 | tf_op jit(solution)/shard_map/all_to_all | solution.py:367
  50.6 0.3 shard_map.88
  50.9 10.5 %all_to_all.42.own_ref = bf16[4,512,128]{2,1,0:T(8,128)(2,1)S(1)} all-to-all(bf16[4,512,128]{2,1,0:T(8,128)(2,1)S(1)} %get-tuple-element.16), channel_id=1, replica_groups={{0,2,4,6},{1,3,5,7},{8,10,12,14},{9,11,13,15},{16,18,20,22},{17,19,21,2..., dimensions={0} | all-to-all | bytes 1048576 | tf_op jit(solution)/shard_map/all_to_all | solution.py:379
  61.4 1.9 %collective-permute-start = (bf16[4,512,128]{2,1,0:T(8,128)(2,1)S(1)}, bf16[4,512,128]{2,1,0:T(8,128)(2,1)S(1)}, u32[]{:S(2)}, u32[]{:S(2)}) collective-permute-start(bf16[4,512,128]{2,1,0:T(8,128)(2,1)S(1)} %all_to_all.42.own_ref), channel_id=1, source_target_pairs={{0,1},{1,0},{2,3},{3,2},{4,5},{5,4},{6,7},{7,6},{8,9},{9,8},{10,11... | collective-permute-start | bytes 1572872 | tf_op jit(solution)/shard_map/ppermute | solution.py:387
  63.4 1.8 %collective-permute-done.other_ref = bf16[4,512,128]{2,1,0:T(8,128)(2,1)S(1)} collective-permute-done((bf16[4,512,128]{2,1,0:T(8,128)(2,1)S(1)}, bf16[4,512,128]{2,1,0:T(8,128)(2,1)S(1)}, u32[]{:S(2)}, u32[]{:S(2)}) %collective-permute-start) | collective-permute-done | bytes 524320 | tf_op jit(solution)/shard_map/ppermute | solution.py:387
  65.2 4.0 %shard_map.89 = (f32[64,1152]{1,0:T(8,128)S(1)}, bf16[4,448,128]{2,1,0:T(8,128)(2,1)S(1)}) custom-call(s32[1]{0:T(128)} %bitcast.1.core_ref, bf16[4,512,128]{2,1,0:T(8,128)(2,1)S(1)} %all_to_all.42.own_ref, bf16[4,512,128]{2,1,0:T(8,128)(2,1)S(1)} %collective-permute-done.other_ref, bf16[64,128]{1,0:T(8,128)(2,1)S(1)} %get-tuple-element.17.label_ref, ...), custom_call_target="tpu_custom_call" | custom-call | tf_op jit(solution)/shard_map/pallas_call | solution.py:392
  69.2 12.2 %all_to_all.43.got_ref = bf16[4,448,128]{2,1,0:T(8,128)(2,1)S(1)} all-to-all(bf16[4,448,128]{2,1,0:T(8,128)(2,1)S(1)} %get-tuple-element.19), channel_id=1, replica_groups={{0,128,256,384},{8,136,264,392},{16,144,272,400},{24,152,280,408},{32,1..., dimensions={0} | all-to-all | bytes 917504 | tf_op jit(solution)/shard_map/all_to_all | solution.py:412
  81.4 0.3 shard_map.90
  81.8 17.3 %all_to_all.44 = f16[16,24,128]{2,1,0:T(8,128)(2,1)S(1)} all-to-all(f16[16,24,128]{2,1,0:T(8,128)(2,1)S(1)} %convert_element_type.17), channel_id=1, replica_groups={{0,8,16,24,32,40,48,56,64,72,80,88,96,104,112,120},{128,136,144,152,160..., dimensions={0} | all-to-all | bytes 196608 | tf_op jit(solution)/shard_map/all_to_all | solution.py:412
  99.1 0.2 shard_map.91
  99.3 0.7 broadcast_in_dim.6
  100.0 4.3 %all-to-all-start.5 = ((f16[16,24,128]{2,1,0:T(8,128)(2,1)}), f16[16,24,128]{2,1,0:T(8,128)(2,1)S(1)}, u32[]{:S(2)}, u32[]{:S(2)}) async-start(f16[16,24,128]{2,1,0:T(8,128)(2,1)} %broadcast_in_dim.6), calls=%async_computation.5 | async-start | bytes 196608 | tf_op jit(solution)/shard_map/all_to_all | solution.py:62
  104.9 11.6 %all-to-all-done.5 = f16[16,24,128]{2,1,0:T(8,128)(2,1)S(1)} async-done(((f16[16,24,128]{2,1,0:T(8,128)(2,1)}), f16[16,24,128]{2,1,0:T(8,128)(2,1)S(1)}, u32[]{:S(2)}, u32[]{:S(2)}) %all-to-all-start.5) | async-done | bytes 98336 | tf_op jit(solution)/shard_map/all_to_all | solution.py:62
  116.5 0.8 broadcast_in_dim.7
  117.3 3.5 %all-to-all-start.6 = ((f16[4,16,24,128]{3,2,1,0:T(8,128)(2,1)}), f16[4,16,24,128]{3,2,1,0:T(8,128)(2,1)S(1)}, u32[]{:S(2)}, u32[]{:S(2)}) async-start(f16[4,16,24,128]{3,2,1,0:T(8,128)(2,1)} %broadcast_in_dim.7), calls=%async_computation.6 | async-start | bytes 786432 | tf_op jit(solution)/shard_map/all_to_all | solution.py:62
  120.8 5.9 %shard_map.92 = (f32[128,128]{1,0:T(8,128)S(1)}, f32[128,128]{1,0:T(8,128)S(1)}, f32[128,128]{1,0:T(8,128)S(1)}) custom-call(f32[16,24,128]{2,1,0:T(8,128)S(1)} %convert_element_type.22.gram_ref, f32[1]{0:T(128)S(6)} %copy.10.ridge_ref), custom_call_target="tpu_custom_call" | custom-call | flops 8000000000 | bytes 262144 | tf_op jit(solution)/shard_map/pallas_call | solution.py:426
  126.7 1.4 %all-to-all-done.6 = f16[4,16,24,128]{3,2,1,0:T(8,128)(2,1)S(1)} async-done(((f16[4,16,24,128]{3,2,1,0:T(8,128)(2,1)}), f16[4,16,24,128]{3,2,1,0:T(8,128)(2,1)S(1)}, u32[]{:S(2)}, u32[]{:S(2)}) %all-to-all-start.6) | async-done | bytes 393248 | tf_op jit(solution)/shard_map/all_to_all | solution.py:62
  128.2 2.2 %shard_map.93 = (f32[128,1024]{1,0:T(8,128)}, f32[64,1024]{1,0:T(8,128)}) custom-call(s32[1]{0:T(128)} %bitcast.first_ref, f32[64,24,128]{2,1,0:T(8,128)S(1)} %bitcast_convert_fusion.total_ref, f32[128,128]{1,0:T(8,128)S(1)} %get-tuple-element.20.terms_ref, f32[128,128]{1,0:T(8,128)S(1)} %get-tuple-element.21.turn_ref, ...), custom_call_target="tpu_custom_call" | custom-call | tf_op jit(solution)/shard_map/pallas_call | solution.py:434
  (19 shorter events, 0.2 us)
Async XLA Ops:
  0.6 6.1 %copy-start.2 = (s32[256,1]{0,1:T(1,128)S(1)}, s32[256,1]{0,1:T(1,128)}, u32[]{:S(2)}) copy-start(s32[256,1]{0,1:T(1,128)} %param.10) | copy-start | bytes 3076
  0.6 6.1 %copy-start.1 = (s32[256]{0:T(256)S(1)}, s32[256]{0:T(256)}, u32[]{:S(2)}) copy-start(s32[256]{0:T(256)} %param.11) | copy-start | bytes 3076
  2.4 12.9 %all-to-all-start = ((bf16[8,176,128]{2,1,0:T(8,128)(2,1)}), bf16[8,176,128]{2,1,0:T(8,128)(2,1)S(1)}, u32[]{:S(2)}, u32[]{:S(2)}) async-start(bf16[8,176,128]{2,1,0:T(8,128)(2,1)} %shard_map.86), calls=%async_computation | async-start | bytes 720896 | tf_op jit(solution)/shard_map/all_to_all | solution.py:355
  16.5 34.1 %all-to-all-start.1 = ((bf16[64,8,128]{2,1,0:T(8,128)(2,1)}), bf16[64,8,128]{2,1,0:T(8,128)(2,1)S(1)}, u32[]{:S(2)}, u32[]{:S(2)}) async-start(bf16[64,8,128]{2,1,0:T(8,128)(2,1)} %bitcast.5), calls=%async_computation.1 | async-start | bytes 262144 | tf_op jit(solution)/shard_map/all_to_all | solution.py:367
  34.9 28.4 %copy-start = (f32[1024]{0:T(1024)S(1)}, f32[1024]{0:T(1024)}, u32[]{:S(2)}) copy-start(f32[1024]{0:T(1024)} %param.9) | copy-start | bytes 12292
  34.9 28.4 %copy-start.3 = (f32[64]{0:T(128)S(1)}, f32[64]{0:T(128)}, u32[]{:S(2)}) copy-start(f32[64]{0:T(128)} %param.12) | copy-start | bytes 772
  61.4 3.8 %collective-permute-start = (bf16[4,512,128]{2,1,0:T(8,128)(2,1)S(1)}, bf16[4,512,128]{2,1,0:T(8,128)(2,1)S(1)}, u32[]{:S(2)}, u32[]{:S(2)}) collective-permute-start(bf16[4,512,128]{2,1,0:T(8,128)(2,1)S(1)} %all_to_all.42.own_ref), channel_id=1, source_target_pairs={{0,1},{1,0},{2,3},{3,2},{4,5},{5,4},{6,7},{7,6},{8,9},{9,8},{10,11... | collective-permute-start | bytes 1572872 | tf_op jit(solution)/shard_map/ppermute | solution.py:387
  100.0 16.5 %all-to-all-start.5 = ((f16[16,24,128]{2,1,0:T(8,128)(2,1)}), f16[16,24,128]{2,1,0:T(8,128)(2,1)S(1)}, u32[]{:S(2)}, u32[]{:S(2)}) async-start(f16[16,24,128]{2,1,0:T(8,128)(2,1)} %broadcast_in_dim.6), calls=%async_computation.5 | async-start | bytes 196608 | tf_op jit(solution)/shard_map/all_to_all | solution.py:62
  117.3 10.8 %all-to-all-start.6 = ((f16[4,16,24,128]{3,2,1,0:T(8,128)(2,1)}), f16[4,16,24,128]{3,2,1,0:T(8,128)(2,1)S(1)}, u32[]{:S(2)}, u32[]{:S(2)}) async-start(f16[4,16,24,128]{3,2,1,0:T(8,128)(2,1)} %broadcast_in_dim.7), calls=%async_computation.6 | async-start | bytes 786432 | tf_op jit(solution)/shard_map/all_to_all | solution.py:62
